TPU v7x, 32 devices: a whole 2x2x4 slice. The times are simulated.
32 devices in a mesh: ctx: 16 (over z, x, core), shard: 2 (over y).
Axes of the slice: x: 2, y: 2, z: 4, core: 2. Of those that a mesh axis runs over, the one named last changes fastest.
Arguments:
- tokens: bfloat16 [2, 16384, 512], P('shard', 'ctx'), may hold values from -6 to 6
- expert_index: int32 [2, 16384, 8], P('shard', 'ctx'), may hold values from 0 to 23, all different within a row
- first_gain: bfloat16 [512], P('shard'), may hold values from 0.5 to 1.5
- first_shift: bfloat16 [512], P('shard'), may hold values from -0.625 to 0.625
- router_weight: bfloat16 [512, 24], P('shard'), may hold values from -0.125 to 0.125
- query_weight: bfloat16 [512, 1536], P('shard'), may hold values from -0.5 to 0.5
- key_weight: bfloat16 [512, 64], P('shard'), may hold values from -0.25 to 0.25
- value_weight: bfloat16 [512, 64], P('shard'), may hold values from -0.25 to 0.25
- output_weight: bfloat16 [1536, 512], P('shard'), may hold values from -24 to 24
- second_gain: bfloat16 [512], P('shard'), may hold values from 0.5 to 1.5
- second_shift: bfloat16 [512], P('shard'), may hold values from -0.625 to 0.625
- up_weight: bfloat16 [512, 2048], P('shard'), may hold values from -0.25 to 0.25
- up_bias: bfloat16 [2048], P('shard'), may hold values from -0.625 to 0.625
- down_weight: bfloat16 [2048, 512], P('shard'), may hold values from -0.1875 to 0.1875
- down_bias: bfloat16 [512], P('shard'), may hold values from -1.75 to 1.75
- out_grad: bfloat16 [2, 16384, 512], P('shard', 'ctx'), may hold values from -6 to 6
Outputs:
- layer_out: bfloat16 [2, 16384, 512], P('shard', 'ctx')
- tokens_grad: bfloat16 [2, 16384, 512], P('shard', 'ctx')
- first_gain_grad: float32 [512], P('shard')
- first_shift_grad: float32 [512], P('shard')
- router_weight_grad: float32 [512, 24], P('shard')
- query_weight_grad: float32 [512, 1536], P('shard')
- key_weight_grad: float32 [512, 64], P('shard')
- value_weight_grad: float32 [512, 64], P('shard')
- output_weight_grad: float32 [1536, 512], P('shard')
- second_gain_grad: float32 [512], P('shard')
- second_shift_grad: float32 [512], P('shard')
- up_weight_grad: float32 [512, 2048], P('shard')
- up_bias_grad: float32 [2048], P('shard')
- down_weight_grad: float32 [2048, 512], P('shard')
- down_bias_grad: float32 [512], P('shard')
Inputs may be any that keep to these rules, and one draw needn't show every extreme that they name: `expert_index`: each token names 8 different experts.
All inputs are finite; a program needn't handle non-finite values.
Results may differ from a plain program's by a relative error of at most 0.017.
Values may be sent and summed in bfloat16 or wider, within the bound.
No kernel may reach another device: no remote copies, remote signals or barrier semaphores. Data moves between devices by JAX's collectives and lax.ppermute only.
A program may use at most 256 MiB of HBM per device.

v0:
```python
import math

import jax
import jax.numpy as jnp
from jax import lax
from jax.sharding import PartitionSpec as P

PROMPT = 8192
CLEN = 1024


norm_eps = 1e-05
mask_fill = -1e30


def layer_norm(values, gain, shift):
    center = jnp.mean(values, axis=-1, keepdims=True)
    centred = values - center
    spread = jnp.mean(centred * centred, axis=-1, keepdims=True)
    inverse = lax.rsqrt(spread + norm_eps)
    normed = centred * inverse
    return (normed * gain + shift, normed, inverse)


def norm_back(grad, normed, inverse, gain):
    scaled = grad * gain
    inner = (
        scaled
        - jnp.mean(scaled, axis=-1, keepdims=True)
        - normed * jnp.mean(scaled * normed, axis=-1, keepdims=True)
    )
    return (inner * inverse, jnp.sum(grad * normed, axis=0), jnp.sum(grad, axis=0))


def smooth_gate(values):
    return jax.nn.gelu(values, approximate=True)


def segment_of(position):
    return jnp.where(position < PROMPT, 0, 1 + (position - PROMPT) // CLEN)


def visible(query_pos, key_pos):
    query_seg = segment_of(query_pos)[:, None]
    key_seg = segment_of(key_pos)[None, :]
    return (key_pos[None, :] <= query_pos[:, None]) & ((key_seg == 0) | (key_seg == query_seg))


def key_rows(rows):
    return math.gcd(rows, 1024)


def forward_fold(query_grid, query_pos, scale):
    width = query_grid.shape[-1]

    def update(state, block, key_start):
        size = block.shape[1]
        key_pos = key_start + jnp.arange(size, dtype=jnp.int32)
        allowed = visible(query_pos, key_pos)

        def update_compute(current):
            run_max, run_sum, accum = current
            keys = block[:, :, :width]
            values = block[:, :, width:]
            wide = allowed[None, :, None, :]
            scores = (
                jnp.einsum("gbhd,gkd->gbhk", query_grid, keys, preferred_element_type=jnp.float32)
                * scale
            )
            scores = jnp.where(wide, scores, mask_fill)
            new_max = jnp.maximum(run_max, jnp.max(scores, axis=-1))
            factor = jnp.exp(run_max - new_max)
            weights = jnp.where(wide, jnp.exp(scores - new_max[..., None]), 0.0)
            new_sum = run_sum * factor + jnp.sum(weights, axis=-1)
            weights_low = weights.astype(jnp.bfloat16)
            new_acc = accum * factor[..., None] + jnp.einsum(
                "gbhk,gkd->gbhd", weights_low, values, preferred_element_type=jnp.float32
            )
            return (new_max, new_sum, new_acc)

        def unchanged(current):
            return current

        return lax.cond(jnp.any(allowed), update_compute, unchanged, state)

    def fold(carry, piece, start):
        rows = piece.shape[1]
        size = key_rows(rows)

        def fold_step(index, state):
            block = lax.dynamic_slice_in_dim(piece, index * size, size, 1)
            return update(state, block, index * size)

        return lax.fori_loop(0, rows // size, fold_step, carry)

    return fold


def block_grads(block, key_pos, context):
    query_grid, query_pos, grad_low, log_total, delta, scale = context
    width = query_grid.shape[-1]
    allowed = visible(query_pos, key_pos)

    def block_compute(unused):
        keys = block[:, :, :width]
        values = block[:, :, width:]
        wide = allowed[None, :, None, :]
        scores = (
            jnp.einsum("gbhd,gkd->gbhk", query_grid, keys, preferred_element_type=jnp.float32)
            * scale
        )
        probs = jnp.where(wide, jnp.exp(scores - log_total[..., None]), 0.0)
        probs_low = probs.astype(jnp.bfloat16)
        value_grad = jnp.einsum(
            "gbhk,gbhd->gkd", probs_low, grad_low, preferred_element_type=jnp.float32
        )
        prob_grad = jnp.einsum(
            "gbhd,gkd->gbhk", grad_low, values, preferred_element_type=jnp.float32
        )
        score_grad = (probs * (prob_grad - delta[..., None])).astype(jnp.bfloat16)
        query_add = (
            jnp.einsum("gbhk,gkd->gbhd", score_grad, keys, preferred_element_type=jnp.float32)
            * scale
        )
        key_add = (
            jnp.einsum("gbhk,gbhd->gkd", score_grad, query_grid, preferred_element_type=jnp.float32)
            * scale
        )
        return (query_add, jnp.concatenate([key_add, value_grad], axis=-1))

    def skipped(unused):
        return (jnp.zeros(query_grid.shape, jnp.float32), jnp.zeros(block.shape, jnp.float32))

    return lax.cond(jnp.any(allowed), block_compute, skipped, 0)


def sweep(piece, context):
    query_grid = context[0]
    rows = piece.shape[1]
    size = key_rows(rows)

    def sweep_step(query_acc, index):
        offset = index * size
        block = lax.dynamic_slice_in_dim(piece, offset, size, 1)
        key_pos = offset + jnp.arange(size, dtype=jnp.int32)
        query_add, block_grad = block_grads(block, key_pos, context)
        return (query_acc + query_add, block_grad)

    query_acc, parts = lax.scan(
        sweep_step,
        jnp.zeros(query_grid.shape, jnp.float32),
        jnp.arange(rows // size, dtype=jnp.int32),
    )
    piece_grad = jnp.moveaxis(parts, 0, 1).reshape(piece.shape[0], rows, piece.shape[2])
    return (query_acc, piece_grad)


def per_device(
    tokens,
    expert_index,
    first_gain,
    first_shift,
    router_weight,
    query_weight,
    key_weight,
    value_weight,
    output_weight,
    second_gain,
    second_shift,
    up_weight,
    up_bias,
    down_weight,
    down_bias,
    out_grad,
):
    (
        first_gain,
        first_shift,
        router_weight,
        query_weight,
        key_weight,
        value_weight,
        output_weight,
        second_gain,
        second_shift,
        up_weight,
        up_bias,
        down_weight,
        down_bias,
    ) = (
        lax.all_gather(first_gain, "shard", axis=0, tiled=True),
        lax.all_gather(first_shift, "shard", axis=0, tiled=True),
        lax.all_gather(router_weight, "shard", axis=0, tiled=True),
        lax.all_gather(query_weight, "shard", axis=0, tiled=True),
        lax.all_gather(key_weight, "shard", axis=0, tiled=True),
        lax.all_gather(value_weight, "shard", axis=0, tiled=True),
        lax.all_gather(output_weight, "shard", axis=0, tiled=True),
        lax.all_gather(second_gain, "shard", axis=0, tiled=True),
        lax.all_gather(second_shift, "shard", axis=0, tiled=True),
        lax.all_gather(up_weight, "shard", axis=0, tiled=True),
        lax.all_gather(up_bias, "shard", axis=0, tiled=True),
        lax.all_gather(down_weight, "shard", axis=0, tiled=True),
        lax.all_gather(down_bias, "shard", axis=0, tiled=True),
    )
    groups, block, width = tokens.shape
    topk = expert_index.shape[-1]
    experts = router_weight.shape[1]
    head = key_weight.shape[1]
    count = groups * block
    flat = tokens.reshape(count, width).astype(jnp.float32)
    chosen = expert_index.reshape(count, topk)
    gain_one = first_gain.astype(jnp.float32)
    gain_two = second_gain.astype(jnp.float32)
    normed_one, unit_one, inverse_one = layer_norm(flat, gain_one, first_shift.astype(jnp.float32))
    first_low = normed_one.astype(jnp.bfloat16)
    logits = jnp.dot(first_low, router_weight, preferred_element_type=jnp.float32)
    gate = jax.nn.softmax(jnp.take_along_axis(logits, chosen, axis=1), axis=-1)
    projected = jnp.dot(first_low, query_weight, preferred_element_type=jnp.float32).reshape(
        count, experts, head
    )
    queries = jnp.take_along_axis(projected, chosen[:, :, None], axis=1).astype(jnp.bfloat16)
    key_value_weight = jnp.concatenate([key_weight, value_weight], axis=1)
    key_value = (
        jnp.dot(first_low, key_value_weight, preferred_element_type=jnp.float32)
        .astype(jnp.bfloat16)
        .reshape(groups, block, 2 * head)
    )
    query_grid = queries.reshape(groups, block, topk, head)
    query_pos = lax.axis_index("ctx") * block + jnp.arange(block, dtype=jnp.int32)
    scale = head ** (-0.5)
    start_state = (
        jnp.full((groups, block, topk), mask_fill, jnp.float32),
        jnp.zeros((groups, block, topk), jnp.float32),
        jnp.zeros((groups, block, topk, head), jnp.float32),
    )
    run_max, run_sum, accum = forward_fold(query_grid, query_pos, scale)(
        start_state, lax.all_gather(key_value, "ctx", axis=1, tiled=True), jnp.int32(0)
    )
    attended = accum / run_sum[..., None]
    log_total = run_max + jnp.log(run_sum)
    attended_flat = attended.reshape(count, topk, head)
    weighted = (gate[:, :, None] * attended_flat).astype(jnp.bfloat16)
    onehot = chosen[:, :, None] == jnp.arange(experts, dtype=jnp.int32)[None, None, :]
    onehot_low = onehot.astype(jnp.bfloat16)
    spread_out = (
        jnp.einsum("tje,tjd->ted", onehot_low, weighted, preferred_element_type=jnp.float32)
        .astype(jnp.bfloat16)
        .reshape(count, experts * head)
    )
    middle = flat + jnp.dot(spread_out, output_weight, preferred_element_type=jnp.float32)
    normed_two, unit_two, inverse_two = layer_norm(
        middle, gain_two, second_shift.astype(jnp.float32)
    )
    second_low = normed_two.astype(jnp.bfloat16)
    pre = jnp.dot(second_low, up_weight, preferred_element_type=jnp.float32) + up_bias.astype(
        jnp.float32
    )
    activated, gate_pull = jax.vjp(smooth_gate, pre)
    hidden = activated.astype(jnp.bfloat16)
    result = (
        middle
        + jnp.dot(hidden, down_weight, preferred_element_type=jnp.float32)
        + down_bias.astype(jnp.float32)
    )
    layer_out = result.astype(jnp.bfloat16).reshape(groups, block, width)
    grad_low = out_grad.reshape(count, width)
    grad_result = grad_low.astype(jnp.float32)
    down_weight_grad = jnp.einsum("tf,td->fd", hidden, grad_low, preferred_element_type=jnp.float32)
    down_bias_grad = jnp.sum(grad_result, axis=0)
    hidden_grad = jnp.einsum("td,fd->tf", grad_low, down_weight, preferred_element_type=jnp.float32)
    pre_grad = gate_pull(hidden_grad)[0].astype(jnp.bfloat16)
    up_weight_grad = jnp.einsum(
        "td,tf->df", second_low, pre_grad, preferred_element_type=jnp.float32
    )
    up_bias_grad = jnp.sum(pre_grad.astype(jnp.float32), axis=0)
    second_grad = jnp.einsum("tf,df->td", pre_grad, up_weight, preferred_element_type=jnp.float32)
    middle_norm_grad, second_gain_grad, second_shift_grad = norm_back(
        second_grad, unit_two, inverse_two, gain_two
    )
    middle_grad = grad_result + middle_norm_grad
    middle_low = middle_grad.astype(jnp.bfloat16)
    output_weight_grad = jnp.einsum(
        "te,td->ed", spread_out, middle_low, preferred_element_type=jnp.float32
    )
    spread_grad = jnp.einsum(
        "td,ed->te", middle_low, output_weight, preferred_element_type=jnp.float32
    ).reshape(count, experts, head)
    chosen_grad = jnp.take_along_axis(spread_grad, chosen[:, :, None], axis=1)
    gate_grad = jnp.sum(chosen_grad * attended_flat, axis=-1)
    attended_grad = (gate[:, :, None] * chosen_grad).astype(jnp.bfloat16)
    pick_grad = gate * (gate_grad - jnp.sum(gate * gate_grad, axis=-1, keepdims=True))
    logit_grad = jnp.sum(onehot.astype(jnp.float32) * pick_grad[:, :, None], axis=1).astype(
        jnp.bfloat16
    )
    router_weight_grad = jnp.einsum(
        "td,te->de", first_low, logit_grad, preferred_element_type=jnp.float32
    )
    grad_grid = attended_grad.reshape(groups, block, topk, head)
    delta = jnp.sum(grad_grid.astype(jnp.float32) * attended, axis=-1)
    context = (query_grid, query_pos, grad_grid, log_total, delta, scale)
    query_add, piece_grad = sweep(lax.all_gather(key_value, "ctx", axis=1, tiled=True), context)
    key_value_grad = lax.psum_scatter(piece_grad, "ctx", scatter_dimension=1, tiled=True)
    query_grad_low = query_add.reshape(count, topk, head).astype(jnp.bfloat16)
    placed_grad = (
        jnp.einsum("tje,tjd->ted", onehot_low, query_grad_low, preferred_element_type=jnp.float32)
        .astype(jnp.bfloat16)
        .reshape(count, experts * head)
    )
    query_weight_grad = jnp.einsum(
        "td,te->de", first_low, placed_grad, preferred_element_type=jnp.float32
    )
    key_value_low = key_value_grad.reshape(count, 2 * head).astype(jnp.bfloat16)
    key_value_weight_grad = jnp.einsum(
        "td,tk->dk", first_low, key_value_low, preferred_element_type=jnp.float32
    )
    first_grad = jnp.einsum(
        "te,de->td", placed_grad, query_weight, preferred_element_type=jnp.float32
    )
    first_grad = first_grad + jnp.einsum(
        "tk,dk->td", key_value_low, key_value_weight, preferred_element_type=jnp.float32
    )
    first_grad = first_grad + jnp.einsum(
        "te,de->td", logit_grad, router_weight, preferred_element_type=jnp.float32
    )
    first_norm_grad, first_gain_grad, first_shift_grad = norm_back(
        first_grad, unit_one, inverse_one, gain_one
    )
    tokens_grad = (middle_grad + first_norm_grad).astype(jnp.bfloat16).reshape(groups, block, width)
    key_weight_grad = key_value_weight_grad[:, :head]
    value_weight_grad = key_value_weight_grad[:, head:]
    (
        first_gain_grad,
        first_shift_grad,
        router_weight_grad,
        query_weight_grad,
        key_weight_grad,
        value_weight_grad,
        output_weight_grad,
        second_gain_grad,
        second_shift_grad,
        up_weight_grad,
        up_bias_grad,
        down_weight_grad,
        down_bias_grad,
    ) = lax.psum(
        (
            first_gain_grad,
            first_shift_grad,
            router_weight_grad,
            query_weight_grad,
            key_weight_grad,
            value_weight_grad,
            output_weight_grad,
            second_gain_grad,
            second_shift_grad,
            up_weight_grad,
            up_bias_grad,
            down_weight_grad,
            down_bias_grad,
        ),
        "ctx",
    )
    (
        first_gain_grad,
        first_shift_grad,
        router_weight_grad,
        query_weight_grad,
        key_weight_grad,
        value_weight_grad,
        output_weight_grad,
        second_gain_grad,
        second_shift_grad,
        up_weight_grad,
        up_bias_grad,
        down_weight_grad,
        down_bias_grad,
    ) = (
        lax.psum_scatter(
            first_gain_grad.astype(jnp.bfloat16), "shard", scatter_dimension=0, tiled=True
        ).astype(jnp.float32),
        lax.psum_scatter(
            first_shift_grad.astype(jnp.bfloat16), "shard", scatter_dimension=0, tiled=True
        ).astype(jnp.float32),
        lax.psum_scatter(
            router_weight_grad.astype(jnp.bfloat16), "shard", scatter_dimension=0, tiled=True
        ).astype(jnp.float32),
        lax.psum_scatter(
            query_weight_grad.astype(jnp.bfloat16), "shard", scatter_dimension=0, tiled=True
        ).astype(jnp.float32),
        lax.psum_scatter(
            key_weight_grad.astype(jnp.bfloat16), "shard", scatter_dimension=0, tiled=True
        ).astype(jnp.float32),
        lax.psum_scatter(
            value_weight_grad.astype(jnp.bfloat16), "shard", scatter_dimension=0, tiled=True
        ).astype(jnp.float32),
        lax.psum_scatter(
            output_weight_grad.astype(jnp.bfloat16), "shard", scatter_dimension=0, tiled=True
        ).astype(jnp.float32),
        lax.psum_scatter(
            second_gain_grad.astype(jnp.bfloat16), "shard", scatter_dimension=0, tiled=True
        ).astype(jnp.float32),
        lax.psum_scatter(
            second_shift_grad.astype(jnp.bfloat16), "shard", scatter_dimension=0, tiled=True
        ).astype(jnp.float32),
        lax.psum_scatter(
            up_weight_grad.astype(jnp.bfloat16), "shard", scatter_dimension=0, tiled=True
        ).astype(jnp.float32),
        lax.psum_scatter(
            up_bias_grad.astype(jnp.bfloat16), "shard", scatter_dimension=0, tiled=True
        ).astype(jnp.float32),
        lax.psum_scatter(
            down_weight_grad.astype(jnp.bfloat16), "shard", scatter_dimension=0, tiled=True
        ).astype(jnp.float32),
        lax.psum_scatter(
            down_bias_grad.astype(jnp.bfloat16), "shard", scatter_dimension=0, tiled=True
        ).astype(jnp.float32),
    )
    return (
        layer_out,
        tokens_grad,
        first_gain_grad,
        first_shift_grad,
        router_weight_grad,
        query_weight_grad,
        key_weight_grad,
        value_weight_grad,
        output_weight_grad,
        second_gain_grad,
        second_shift_grad,
        up_weight_grad,
        up_bias_grad,
        down_weight_grad,
        down_bias_grad,
    )


def solution(mesh):
    in_specs = (
        P("shard", "ctx", None),
        P("shard", "ctx", None),
        P("shard"),
        P("shard"),
        P("shard", None),
        P("shard", None),
        P("shard", None),
        P("shard", None),
        P("shard", None),
        P("shard"),
        P("shard"),
        P("shard", None),
        P("shard"),
        P("shard", None),
        P("shard"),
        P("shard", "ctx", None),
    )
    out_specs = (
        P("shard", "ctx", None),
        P("shard", "ctx", None),
        P("shard"),
        P("shard"),
        P("shard", None),
        P("shard", None),
        P("shard", None),
        P("shard", None),
        P("shard", None),
        P("shard"),
        P("shard"),
        P("shard", None),
        P("shard"),
        P("shard", None),
        P("shard"),
    )
    return jax.shard_map(
        per_device, mesh=mesh, in_specs=in_specs, out_specs=out_specs, check_vma=False
    )
```

profile of v0, /device:TPU:0, one launch (start us, length us, event | category | flops | bytes accessed | tf_op | source)
XLA Modules:
  0.0 2158.2 jit_solution(3663871249257719316)
XLA Ops:
  8.0 5.8 all_gather.46
  13.8 4.8 all_gather.47
  19.2 4.2 all-gather.1
  24.1 4.2 all-gather.2
  35.2 4.2 all-gather.3
  40.0 4.2 all-gather.4
  44.8 4.3 all_gather.54
  49.8 4.4 all_gather.45
  55.9 65.5 %gather_fusion = f32[8192]{0:T(1024)S(1)} fusion(f32[1024,24]{0,1:T(8,128)S(1)} %fusion.131, s32[8192]{0:T(1024)S(1)} %reshape.560), kind=kCustom, calls=%fused_computation.2 | custom fusion | bytes 131072 | tf_op jit(solution)/shard_map/jit(take_along_axis)/gather | solution.py:217
  125.8 3.7 fusion.99
  129.5 7.9 copy.100
  137.4 98.5 %gather_fusion.1 = bf16[8192,64]{1,0:T(8,128)(2,1)S(1)} fusion(bf16[1024,24,64]{2,1,0:T(8,128)(2,1)} %copy.100, s32[8192]{0:T(1024)S(1)} %reshape.560), kind=kCustom, calls=%fused_computation.clone | custom fusion | bytes 2162688 | tf_op jit(solution)/shard_map/jit(take_along_axis)/gather | solution.py:221
  237.6 6.5 copy.102
  245.7 93.4 %while.37 = (s32[]{:T(128)}, f32[1,1024,8]{1,2,0:T(8,128)S(1)}, f32[1,1024,8]{1,2,0:T(8,128)S(1)}, f32[1,1024,8,64]{1,3,2,0:T(8,128)}, bf16[1,16384,128]{1,2,0:T...) while((s32[]{:T(128)}, f32[1,1024,8]{1,2,0:T(8,128)S(1)}, ...), condition=%wide.region_10.12_spmd.clone, body=%wide.region_4.11_spmd.clone.sunk | while | flops 2262914048 | bytes 127699296 | solution.py:94
  249.1 45.4 %conditional.6 = ((f32[1,1024,8]{1,2,0:T(8,128)S(1)}, f32[1,1024,8]{1,2,0:T(8,128)S(1)}, f32[1,1024,8,64]{1,3,2,0:T(8,128)})) conditional(s32[]{:T(128)} %convert_element_type.405, (f32[1,1024,8]{1,2,0:T(8,128)S(1)}, f32[1,1024,8]{1,2,0:T(8,128)S(1)}, f32[1,1024,8,64]{1,3,2,0:T(8,128)}) %tuple.150, (pred[1024,1024]{0,1:T(8,128)(4,1)S(1)}, s32[]{:T(128)}, ...), branch_computations={%region_6.7_spmd, %region_7.10_spmd} | conditional | flops 2257608704 | bytes 126615704 | solution.py:84
  249.1 14.5 fusion.4
  263.7 15.3 bitcast_add_fusion
  279.0 15.5 fusion.6
  344.6 9.1 fusion.65
  353.8 7.9 copy.104
  361.7 4.2 fusion.129
  367.6 8.1 fusion.121
  375.8 10.7 convert_reduce_fusion
  386.5 4.3 fusion.130
  398.4 4.5 fusion.107
  402.9 9.7 copy.110
  412.6 119.1 %gather_fusion.2 = f32[8192,64]{1,0:T(8,128)} fusion(f32[1024,24,64]{2,1,0:T(8,128)} %copy.110, s32[8192]{0:T(1024)S(1)} %copy-done.1), kind=kCustom, calls=%fused_computation.1.clone | custom fusion | bytes 4259840 | tf_op jit(solution)/shard_map/jit(take_along_axis)/gather | solution.py:288
  531.7 4.0 copy.111
  538.8 234.1 %while.38 = (s32[]{:T(128)}, f32[1,1024,8,64]{1,3,2,0:T(8,128)}, f32[16,1,1024,128]{3,2,0,1:T(8,128)}, s32[16]{0:T(128)S(1)}, bf16[1,16384,128]{1,2,0:T(8,128)(2...) while((s32[]{:T(128)}, f32[1,1024,8,64]{1,3,2,0:T(8,128)}, ...), condition=%wide.region_20.22_spmd.clone, body=%wide.region_16.21_spmd.clone.sunk | while | flops 5459670016 | bytes 179308912 | solution.py:149
  544.1 53.5 %conditional.7 = (f32[1,1024,8,64]{1,3,2,0:T(8,128)S(1)}, f32[1,1,1024,128]{2,3,1,0:T(8,128)}) conditional(s32[]{:T(128)} %convert_element_type.406, () %tuple.156, (pred[1024,1024]{0,1:T(8,128)(4,1)}, s32[]{:T(128)}, bf16[1,16384,128]{1,2,0:T(8,128)(2,1)}, bf16[1,1024,8,64]{1,3,2,0:T(8,128)(2,1)S(1)}, f32[1,1024,8]{1,2,0:T(8,128)S(1)}, ...), branch_computations={%region_18.19_spmd, %region_19.20_spmd} | conditional | flops 5453316096 | bytes 169836672 | solution.py:134
  544.1 14.3 fusion.33
  558.5 13.9 fusion.25
  572.4 15.1 fusion.20
  587.5 4.0 multiply_bitcast_fusion
  591.5 5.2 fusion.29
  607.4 3.4 select_add_fusion.2
  618.9 3.4 select_add_fusion.2
  630.3 3.4 select_add_fusion.2
  641.8 3.4 select_add_fusion.2
  653.2 3.4 select_add_fusion.2
  664.6 3.4 select_add_fusion.2
  676.0 3.4 select_add_fusion.2
  687.4 3.4 select_add_fusion.2
  710.3 3.4 select_add_fusion.2
  721.7 3.4 select_add_fusion.2
  744.5 3.4 select_add_fusion.2
  756.0 3.4 select_add_fusion.2
  767.4 3.4 select_add_fusion.2
  774.3 9.8 fusion.96
  784.1 4.5 fusion.120
  788.7 3.6 fusion.105
  794.1 7.1 select_reduce_fusion
  806.0 8.2 fusion.66
  814.2 7.7 copy.114
  822.0 5.6 fusion.101
  829.4 832.2 %reduce-scatter.9.cloned.1.call-done = f32[1,1024,128]{2,1,0:T(8,128)} async-done(((f32[1,16384,128]{2,1,0:T(8,128)}), f32[1,1024,128]{2,1,0:T(8,128)}) %reduce-scatter.9.cloned.1.call-update) | async-done | bytes 524304 | tf_op jit(solution)/shard_map/reduce_scatter | solution.py:302
  1667.6 316.7 %all-reduce.9 = (bf16[512]{0:T(512)(128)(2,1)S(1)}, bf16[512]{0:T(512)(128)(2,1)S(1)}, bf16[512,24]{0,1:T(8,128)(2,1)}, bf16[512,1536]{1,0:T(8,128)(2,1)}, bf16[...) all-reduce(f32[512]{0:T(512)} %get-tuple-element.680, ...), channel_id=1, replica_groups=mesh['ctx'=16,'shard'=2] {'ctx'}, use_global_device_ids=true, to_apply=%region_28.30 | all-reduce | flops 3752448 | bytes 22514688 | tf_op jit(solution)/shard_map/psum | solution.py:345
  1990.5 4.5 all-gather.5
  1995.0 8.7 fusion.92
  2011.6 5.0 all-reduce.7
  2024.5 26.9 %reduce-scatter.19.cloned.1.call-done = bf16[768,512]{1,0:T(8,128)(2,1)} async-done(((bf16[1536,512]{1,0:T(8,128)(2,1)}), bf16[768,512]{1,0:T(8,128)(2,1)}) %reduce-scatter.19.cloned.1.call-update) | async-done | bytes 786448 | tf_op jit(solution)/shard_map/reduce_scatter | solution.py:396
  2054.0 26.5 %reduce-scatter.13.cloned.1.call-done = bf16[256,1536]{1,0:T(8,128)(2,1)} async-done(((bf16[512,1536]{1,0:T(8,128)(2,1)}), bf16[256,1536]{1,0:T(8,128)(2,1)}) %reduce-scatter.13.cloned.1.call-update) | async-done | bytes 786448 | tf_op jit(solution)/shard_map/reduce_scatter | solution.py:387
  2083.0 31.5 %reduce-scatter.23.cloned.1.call-done = bf16[1024,512]{1,0:T(8,128)(2,1)} async-done(((bf16[2048,512]{1,0:T(8,128)(2,1)}), bf16[1024,512]{1,0:T(8,128)(2,1)}) %reduce-scatter.23.cloned.1.call-update) | async-done | bytes 1048592 | tf_op jit(solution)/shard_map/reduce_scatter | solution.py:411
  2117.3 31.3 %reduce-scatter.21.cloned.1.call-done = bf16[256,2048]{1,0:T(8,128)(2,1)} async-done(((bf16[512,2048]{1,0:T(8,128)(2,1)}), bf16[256,2048]{1,0:T(8,128)(2,1)}) %reduce-scatter.21.cloned.1.call-update) | async-done | bytes 1048592 | tf_op jit(solution)/shard_map/reduce_scatter | solution.py:405
  (522 shorter events, 253.0 us)
Async XLA Ops:
  7.2 116.8 %all-gather.12.cloned.1.call-start = ((), (), s32[]{:S(2)}) async-start(), calls=%async_computation.8 | async-start | bytes 2359296 | tf_op jit(solution)/shard_map/all_gather | solution.py:194
  7.9 229.7 %all-gather.20.cloned.1.call-start = ((), (), s32[]{:S(2)}) async-start(), calls=%async_computation.20 | async-start | bytes 4456448 | tf_op jit(solution)/shard_map/all_gather | solution.py:237
  23.5 7.8 copy-start.58
  30.8 4.3 copy-start.75
  30.8 9.2 copy-start.76
  30.8 14.0 copy-start.71
  30.8 18.9 copy-start.64
  31.3 24.3 %copy-start.21 = (bf16[1024,512]{0,1:T(8,128)(2,1)}, bf16[1024,512]{0,1:T(8,128)(2,1)S(1)}, u32[]{:S(2)}) copy-start(bf16[1024,512]{0,1:T(8,128)(2,1)S(1)} %fusion.76) | copy-start | bytes 3145732
  32.5 329.1 %all-gather.14.cloned.1.call-start = ((), (), s32[]{:S(2)}) async-start(), calls=%async_computation.9 | async-start | bytes 2359296 | tf_op jit(solution)/shard_map/all_gather | solution.py:197
  33.3 334.3 %all-gather.16.cloned.1.call-start = ((), (), s32[]{:S(2)}) async-start(), calls=%async_computation.10 | async-start | bytes 3145728 | tf_op jit(solution)/shard_map/all_gather | solution.py:200
  33.9 341.9 %all-gather.18.cloned.1.call-start = ((), (), s32[]{:S(2)}) async-start(), calls=%async_computation.11 | async-start | bytes 3145728 | tf_op jit(solution)/shard_map/all_gather | solution.py:202
  34.5 1627.2 %reduce-scatter.9.cloned.1.call-start = ((), (), s32[]{:S(2)}) async-start(), calls=%async_computation.12 | async-start | bytes 8912896 | tf_op jit(solution)/shard_map/reduce_scatter | solution.py:302
  54.2 67.3 %copy-start.43 = (bf16[512,24]{0,1:T(8,128)(2,1)}, bf16[512,24]{0,1:T(8,128)(2,1)S(1)}, u32[]{:S(2)}) copy-start(bf16[512,24]{0,1:T(8,128)(2,1)S(1)} %all_gather.45) | copy-start | bytes 73732
  54.6 82.7 %copy-start = (s32[8192]{0:T(1024)}, s32[8192]{0:T(1024)S(1)}, u32[]{:S(2)}) copy-start(s32[8192]{0:T(1024)S(1)} %reshape.560) | copy-start | bytes 98308
  55.9 66.1 %copy-start.32 = (s32[1,1024,8]{1,2,0:T(8,128)S(1)}, s32[1,1024,8]{1,2,0:T(8,128)}, u32[]{:S(2)}) copy-start(s32[1,1024,8]{1,2,0:T(8,128)} %param.27) | copy-start | bytes 98308
  55.9 66.8 %copy-start.33 = (bf16[1,1024,512]{2,1,0:T(8,128)(2,1)S(1)}, bf16[1,1024,512]{2,1,0:T(8,128)(2,1)}, u32[]{:S(2)}) copy-start(bf16[1,1024,512]{2,1,0:T(8,128)(2,1)} %param.41) | copy-start | bytes 3145732
  245.7 93.4 %copy-start.37 = (f32[1024,8]{0,1:T(8,128)S(1)}, f32[1024,8]{0,1:T(8,128)}, u32[]{:S(2)}) copy-start(f32[1024,8]{0,1:T(8,128)} %fusion.117) | copy-start | bytes 98308
  249.1 14.6 copy-start.7
  279.0 15.5 copy-start.8
  339.1 196.6 %copy-start.25 = (f32[1,1024,8]{1,2,0:T(8,128)}, f32[1,1024,8]{1,2,0:T(8,128)S(1)}, u32[]{:S(2)}) copy-start(f32[1,1024,8]{1,2,0:T(8,128)S(1)} %get-tuple-element.520) | copy-start | bytes 98308
  353.8 7.9 copy-start.5
  361.7 5.9 copy-start.61
  361.7 5.9 copy-start.72
  365.9 30.9 %copy-start.51 = (f32[1024]{0:T(1024)}, f32[1024]{0:T(1024)S(1)}, u32[]{:S(2)}) copy-start(f32[1024]{0:T(1024)S(1)} %broadcast_multiply_fusion.4) | copy-start | bytes 12292
  367.5 29.3 %copy-start.56 = (f32[1024]{0:T(1024)}, f32[1024]{0:T(1024)S(1)}, u32[]{:S(2)}) copy-start(f32[1024]{0:T(1024)S(1)} %add_rsqrt_fusion) | copy-start | bytes 12292
  367.6 8.2 copy-start.34
  367.6 8.1 copy-start.65
  375.8 10.7 copy-start.74
  386.5 4.3 copy-start.79
  398.4 4.5 copy-start.18
  402.9 9.7 copy-start.1
  531.7 4.0 copy-start.9
  531.7 4.0 copy-start.46
  544.1 14.4 copy-start.11
  544.1 14.4 copy-start.36
  773.0 1247.4 %reduce-scatter.11.cloned.1.call-start = ((), (), s32[]{:S(2)}) async-start(), calls=%async_computation.13 | async-start | bytes 36864 | tf_op jit(solution)/shard_map/reduce_scatter | solution.py:384
  774.2 9.9 copy-start.14
  774.2 9.9 copy-start.52
  774.2 9.9 copy-start.57
  774.2 9.9 copy-start.62
  774.3 9.9 copy-start.73
  774.3 9.9 copy-start.80
  784.1 4.5 copy-start.19
  784.1 4.5 copy-start.27
  792.3 8.9 copy-start.22
  792.3 9.9 copy-start.2
  814.2 7.7 copy-start.6
  814.2 7.7 copy-start.50
  814.2 7.7 copy-start.55
  814.2 7.7 copy-start.60
  814.2 7.7 copy-start.70
  822.0 5.6 copy-start.28
  822.0 5.6 copy-start.30
  829.4 834.7 %copy-start.40 = (bf16[512,128]{0,1:T(8,128)(2,1)S(1)}, bf16[512,128]{0,1:T(8,128)(2,1)}, u32[]{:S(2)}) copy-start(bf16[512,128]{0,1:T(8,128)(2,1)} %copy-done.39) | copy-start | bytes 393220
  1984.4 37.4 %reduce-scatter.17.cloned.1.call-start = ((), (), s32[]{:S(2)}) async-start(), calls=%async_computation.16 | async-start | bytes 98304 | tf_op jit(solution)/shard_map/reduce_scatter | solution.py:393
  1985.1 38.0 %reduce-scatter.15.cloned.1.call-start = ((), (), s32[]{:S(2)}) async-start(), calls=%async_computation.15 | async-start | bytes 98304 | tf_op jit(solution)/shard_map/reduce_scatter | solution.py:390
  1985.9 65.6 %reduce-scatter.19.cloned.1.call-start = ((), (), s32[]{:S(2)}) async-start(), calls=%async_computation.17 | async-start | bytes 2359296 | tf_op jit(solution)/shard_map/reduce_scatter | solution.py:396
  1986.5 4.0 copy-start.77
  1986.5 8.5 copy-start.15
  1986.5 8.5 copy-start.67
  1986.5 94.0 %reduce-scatter.13.cloned.1.call-start = ((), (), s32[]{:S(2)}) async-start(), calls=%async_computation.14 | async-start | bytes 2359296 | tf_op jit(solution)/shard_map/reduce_scatter | solution.py:387
  1987.2 127.2 %reduce-scatter.23.cloned.1.call-start = ((), (), s32[]{:S(2)}) async-start(), calls=%async_computation.19 | async-start | bytes 3145728 | tf_op jit(solution)/shard_map/reduce_scatter | solution.py:411
  1987.8 160.8 %reduce-scatter.21.cloned.1.call-start = ((), (), s32[]{:S(2)}) async-start(), calls=%async_computation.18 | async-start | bytes 3145728 | tf_op jit(solution)/shard_map/reduce_scatter | solution.py:405
  1994.9 11.2 copy-start.63
  (30 other events, 80.8 us)
Sparse Core Ops, SparseCore 0:
  9.6 29.9 all-gather.11
  42.3 50.7 all-gather.19
  94.6 25.7 all-gather.13
  121.7 33.1 all-gather.15
  156.3 33.1 all-gather.17
  773.2 888.4 reduce-scatter.8
  1984.5 12.7 reduce-scatter.10
  2000.1 9.8 reduce-scatter.16
  2012.8 9.9 reduce-scatter.14
  2025.4 26.0 reduce-scatter.18
  2054.4 26.0 reduce-scatter.12
  2082.6 31.8 reduce-scatter.22
  2116.8 31.8 reduce-scatter.20
where the time goes:
time: 2170 us; the launch traced here: 2160 us
  waiting for transfers between devices  955 us (44%)
  local copies, waits for them, and re-layouts  415 us (19%)
  blocking collectives  362 us (17%)
  other arithmetic  198 us (9%)
  matrix products  177 us (8%)
  loops' own time  34.1 us (2%)
    reduce_scatter x1, waiting for transfers between devices, per_device(): lax.psum_scatter(piece_grad, 'ctx', scatter_dimension=1, tiled=True)  832 us
    psum x1, blocking collectives, per_device(): lax.psum((first_gain_grad, first_shift_grad, router_weight_grad, query_we...  317 us
    gather x2, local copies, waits for them, and re-layouts, per_device(): chosen_grad = jnp.take_along_axis(spread_grad, chosen[:, :, None], axis=1)  123 us
    gather x2, local copies, waits for them, and re-layouts, per_device(): jnp.take_along_axis(projected, chosen[:, :, None], axis=1)  99.9 us
    gather x5, local copies, waits for them, and re-layouts, per_device(): gate = jax.nn.softmax(jnp.take_along_axis(logits, chosen, axis=1), axis=-1)  66.4 us
    add x16, other arithmetic, sweep_step(): return (query_acc + query_add, block_grad)  52.5 us
    reduce_or x16, other arithmetic, block_grads(): return lax.cond(jnp.any(allowed), block_compute, skipped, 0)  46.3 us
  transfers between devices with their start and end apart: 13, of which 5 were waited for; matrix products, arithmetic and copies ran while one was open for 19% of the time, Pallas kernels for 0%

commit v1 on v0

v1 whole, which is shorter than its diff:
```python
import functools
import math

import jax
import jax.numpy as jnp
from jax import lax
from jax.experimental import pallas as pl
from jax.experimental.pallas import tpu as pltpu
from jax.sharding import PartitionSpec as P

PROMPT = 8192
CLEN = 1024
ROWS = 128
TILE = 256
FULL = 1024
PART = 256
VMEM = 60 << 20

norm_eps = 1e-05
mask_fill = -1e30
LOG2E = math.log2(math.e)
bf16 = jnp.bfloat16
f32 = jnp.float32


def dot(a, b):
    return lax.dot_general(a, b, (((1,), (0,)), ((), ())), preferred_element_type=f32)


def dot_tn(a, b):
    return lax.dot_general(a, b, (((0,), (0,)), ((), ())), preferred_element_type=f32)


def dot_nt(a, b):
    return lax.dot_general(a, b, (((1,), (1,)), ((), ())), preferred_element_type=f32)


def params(**kw):
    return pltpu.CompilerParams(vmem_limit_bytes=VMEM, **kw)


def whole(shape):
    return pl.BlockSpec(shape, lambda i: tuple(0 for _ in shape))


def column_norm(values):
    center = jnp.mean(values, axis=0, keepdims=True)
    centred = values - center
    spread = jnp.mean(centred * centred, axis=0, keepdims=True)
    inverse = lax.rsqrt(spread + norm_eps)
    return centred * inverse, inverse


def column_norm_back(grad, unit, inverse, gain):
    scaled = grad * gain
    inner = (
        scaled
        - jnp.mean(scaled, axis=0, keepdims=True)
        - unit * jnp.mean(scaled * unit, axis=0, keepdims=True)
    )
    return inner * inverse


def fold_lanes(values):
    width = values.shape[1]
    total = values[:, :128]
    for start in range(128, width, 128):
        total = total + values[:, start : start + 128]
    return total


def first_kernel(tokens_ref, gain_ref, shift_ref, kv_weight_ref, first_ref, kv_ref):
    unit, _ = column_norm(tokens_ref[...].astype(f32).T)
    first = (unit * gain_ref[...] + shift_ref[...]).astype(bf16)
    first_ref[...] = first
    kv_ref[...] = dot_tn(kv_weight_ref[...], first).T.astype(bf16)


def first_call(tokens, gain, shift, kv_weight):
    count, width = tokens.shape
    pair = kv_weight.shape[1]
    return pl.pallas_call(
        first_kernel,
        grid=(count // TILE,),
        in_specs=[
            pl.BlockSpec((TILE, width), lambda i: (i, 0)),
            whole((width, 1)),
            whole((width, 1)),
            whole((width, pair)),
        ],
        out_specs=[
            pl.BlockSpec((width, TILE), lambda i: (0, i)),
            pl.BlockSpec((TILE, pair), lambda i: (i, 0)),
        ],
        out_shape=[
            jax.ShapeDtypeStruct((width, count), bf16),
            jax.ShapeDtypeStruct((count, pair), bf16),
        ],
        compiler_params=params(),
        name="first_norm",
    )(tokens, gain, shift, kv_weight)


def query_kernel(first_ref, query_weight_ref, router_ref, index_ref, qt_ref, q_ref, gate_ref):
    topk = index_ref.shape[0]
    head = qt_ref.shape[1]
    experts = query_weight_ref.shape[1] // head
    first = first_ref[...]
    projected = dot_tn(query_weight_ref[...], first)
    logits = dot_tn(router_ref[...], first)
    index = index_ref[...]
    picked = jnp.zeros(index.shape, f32)
    for expert in range(experts):
        picked = jnp.where(index == expert, logits[expert : expert + 1, :], picked)
    picked = jnp.exp(picked - jnp.max(picked, axis=0, keepdims=True))
    gate_ref[...] = picked / jnp.sum(picked, axis=0, keepdims=True)
    for part in range(TILE // ROWS):
        lanes = slice(part * ROWS, (part + 1) * ROWS)
        for j in range(topk):
            row = index[j : j + 1, lanes]
            chosen = jnp.zeros((head, ROWS), f32)
            for expert in range(experts):
                chosen = jnp.where(
                    row == expert, projected[expert * head : (expert + 1) * head, lanes], chosen
                )
            qt_ref[part, :, j * ROWS : (j + 1) * ROWS] = chosen.astype(bf16)
            q_ref[part, j * ROWS : (j + 1) * ROWS, :] = chosen.T.astype(bf16)


def query_call(first, query_weight, router, index, head):
    width, count = first.shape
    topk = index.shape[0]
    tiles = count // ROWS
    per = TILE // ROWS
    return pl.pallas_call(
        query_kernel,
        grid=(count // TILE,),
        in_specs=[
            pl.BlockSpec((width, TILE), lambda i: (0, i)),
            whole(query_weight.shape),
            whole(router.shape),
            pl.BlockSpec((topk, TILE), lambda i: (0, i)),
        ],
        out_specs=[
            pl.BlockSpec((per, head, topk * ROWS), lambda i: (i, 0, 0)),
            pl.BlockSpec((per, topk * ROWS, head), lambda i: (i, 0, 0)),
            pl.BlockSpec((topk, TILE), lambda i: (0, i)),
        ],
        out_shape=[
            jax.ShapeDtypeStruct((tiles, head, topk * ROWS), bf16),
            jax.ShapeDtypeStruct((tiles, topk * ROWS, head), bf16),
            jax.ShapeDtypeStruct((topk, count), f32),
        ],
        compiler_params=params(),
        name="queries",
    )(first, query_weight, router, index)


def tile_ranges(base):
    prompt = base < PROMPT
    steps = jnp.where(prompt, base // FULL, PROMPT // FULL)
    begin = steps * FULL
    position = jnp.where(prompt, begin, PROMPT + (base - PROMPT) // CLEN * CLEN)
    parts = (base + ROWS - position + PART - 1) // PART
    return steps, begin, position, parts


def allowed_mask(position, base, width):
    key_pos = position + lax.broadcasted_iota(jnp.int32, (PART, width), 0)
    query_pos = base + lax.rem(lax.broadcasted_iota(jnp.int32, (PART, width), 1), ROWS)
    return key_pos <= query_pos


def attend_kernel(base_ref, kv_ref, qt_ref, out_ref, lse_ref, vt_ref, knorm_ref, acc_ref, max_ref):
    tile = pl.program_id(0)
    head, width = qt_ref.shape[1:]
    total_keys = kv_ref.shape[0]
    factor = LOG2E * head ** (-0.5)

    @pl.when(tile == 0)
    def _():
        knorm_ref[0] = 0.0

        def turn(i, carry):
            span = pl.ds(pl.multiple_of(i * FULL, FULL), FULL)
            both = kv_ref[span, :].T
            vt_ref[:head, span] = both[head:, :]
            vt_ref[head:, span] = jnp.ones((vt_ref.shape[0] - head, FULL), bf16)
            keys = both[:head, :].astype(f32)
            most = jnp.max(jnp.sum(keys * keys, axis=0, keepdims=True))
            knorm_ref[0] = jnp.maximum(knorm_ref[0], most)
            return carry

        lax.fori_loop(0, total_keys // FULL, turn, 0)

    base = base_ref[tile]
    steps, begin, position, parts = tile_ranges(base)
    query = qt_ref[0].astype(f32)
    qnorm = jnp.max(jnp.sum(query * query, axis=0, keepdims=True))
    narrow = qnorm * knorm_ref[0] * (factor * factor) < 100.0 * 100.0
    acc_ref[...] = jnp.zeros(acc_ref.shape, f32)
    max_ref[...] = jnp.zeros(max_ref.shape, f32)

    def plain(offset, size, mask):
        span = pl.ds(pl.multiple_of(offset, size), size)
        scores = dot(kv_ref[span, :head], qt_ref[0]) * factor
        if mask is not None:
            scores = jnp.where(mask, scores, mask_fill)
        probs = jnp.exp2(scores).astype(bf16)
        acc_ref[...] += dot(vt_ref[:, span], probs)

    @pl.when(narrow)
    def _():
        def step(i, carry):
            plain(i * FULL, FULL, None)
            return carry

        def part(i, carry):
            plain(begin + i * PART, PART, allowed_mask(position + i * PART, base, width))
            return carry

        lax.fori_loop(0, steps, step, 0)
        lax.fori_loop(0, parts, part, 0)

    @pl.when(jnp.logical_not(narrow))
    def _():
        max_ref[...] = jnp.full(max_ref.shape, mask_fill, f32)

        def part(i, carry):
            before = i < steps * (FULL // PART)
            offset = i * PART
            span = pl.ds(pl.multiple_of(offset, PART), PART)
            shifted = jnp.where(before, -(1 << 24), position + offset - begin)
            mask = allowed_mask(shifted, base, width)
            scores = dot(kv_ref[span, :head], qt_ref[0]) * factor
            scores = jnp.where(mask, scores, mask_fill)
            old = max_ref[...]
            new = jnp.maximum(old, jnp.max(scores, axis=0, keepdims=True))
            probs = jnp.where(mask, jnp.exp2(scores - new), 0.0).astype(bf16)
            acc_ref[...] = acc_ref[...] * jnp.exp2(old - new) + dot(vt_ref[:, span], probs)
            max_ref[...] = new
            return carry

        lax.fori_loop(0, steps * (FULL // PART) + parts, part, 0)

    total = acc_ref[head : head + 1, :]
    out_ref[0] = acc_ref[:head, :] / total
    lse_ref[0] = max_ref[...] + jnp.log2(total)


def attend_call(bases, kv, qt):
    tiles, head, width = qt.shape
    total_keys, pair = kv.shape
    return pl.pallas_call(
        attend_kernel,
        grid_spec=pltpu.PrefetchScalarGridSpec(
            num_scalar_prefetch=1,
            grid=(tiles,),
            in_specs=[
                pl.BlockSpec((total_keys, pair), lambda i, b: (0, 0)),
                pl.BlockSpec((1, head, width), lambda i, b: (i, 0, 0)),
            ],
            out_specs=[
                pl.BlockSpec((1, head, width), lambda i, b: (i, 0, 0)),
                pl.BlockSpec((1, 1, width), lambda i, b: (i, 0, 0)),
            ],
            scratch_shapes=[
                pltpu.VMEM((head + 16, total_keys), bf16),
                pltpu.SMEM((1,), f32),
                pltpu.VMEM((head + 16, width), f32),
                pltpu.VMEM((1, width), f32),
            ],
        ),
        out_shape=[
            jax.ShapeDtypeStruct((tiles, head, width), f32),
            jax.ShapeDtypeStruct((tiles, 1, width), f32),
        ],
        compiler_params=params(),
        name="attend",
    )(bases, kv, qt)


def attend_back_kernel(
    base_ref, kv_ref, qt_ref, q_ref, dot_ref, do_ref, lse_ref, delta_ref, dq_ref, dkv_ref, kt_ref
):
    tile = pl.program_id(0)
    head, width = qt_ref.shape[1:]
    total_keys = kv_ref.shape[0]
    scale = head ** (-0.5)

    @pl.when(tile == 0)
    def _():
        def turn(i, carry):
            span = pl.ds(pl.multiple_of(i * FULL, FULL), FULL)
            kt_ref[:, span] = kv_ref[span, :].T[:head, :]
            dkv_ref[span, :] = jnp.zeros((FULL, 2 * head), f32)
            return carry

        lax.fori_loop(0, total_keys // FULL, turn, 0)

    base = base_ref[tile]
    steps, begin, position, parts = tile_ranges(base)
    dq_ref[...] = jnp.zeros(dq_ref.shape, f32)

    def block(offset, size, mask):
        span = pl.ds(pl.multiple_of(offset, size), size)
        scores = dot(kv_ref[span, :head], qt_ref[0]) * (LOG2E * scale) - lse_ref[0]
        probs = jnp.exp2(scores)
        if mask is not None:
            probs = jnp.where(mask, probs, 0.0)
        prob_grad = dot(kv_ref[span, head:], dot_ref[0])
        score_grad = (probs * (prob_grad - delta_ref[0])).astype(bf16)
        dq_ref[0] += dot(kt_ref[:, span], score_grad)
        dkv_ref[span, :head] += dot(score_grad, q_ref[0])
        dkv_ref[span, head:] += dot(probs.astype(bf16), do_ref[0])

    def step(i, carry):
        block(i * FULL, FULL, None)
        return carry

    def part(i, carry):
        block(begin + i * PART, PART, allowed_mask(position + i * PART, base, width))
        return carry

    lax.fori_loop(0, steps, step, 0)
    lax.fori_loop(0, parts, part, 0)
    dq_ref[...] = dq_ref[...] * scale

    @pl.when(tile == pl.num_programs(0) - 1)
    def _():
        def finish(i, carry):
            span = pl.ds(pl.multiple_of(i * FULL, FULL), FULL)
            dkv_ref[span, :head] = dkv_ref[span, :head] * scale
            return carry

        lax.fori_loop(0, total_keys // FULL, finish, 0)


def attend_back_call(bases, kv, qt, q, grad_t, grad, lse, delta):
    tiles, head, width = qt.shape
    total_keys, pair = kv.shape
    one = lambda shape: pl.BlockSpec((1,) + shape, lambda i, b: (i, 0, 0))
    return pl.pallas_call(
        attend_back_kernel,
        grid_spec=pltpu.PrefetchScalarGridSpec(
            num_scalar_prefetch=1,
            grid=(tiles,),
            in_specs=[
                pl.BlockSpec((total_keys, pair), lambda i, b: (0, 0)),
                one((head, width)),
                one((width, head)),
                one((head, width)),
                one((width, head)),
                one((1, width)),
                one((1, width)),
            ],
            out_specs=[
                one((head, width)),
                pl.BlockSpec((total_keys, pair), lambda i, b: (0, 0)),
            ],
            scratch_shapes=[pltpu.VMEM((head, total_keys), bf16)],
        ),
        out_shape=[
            jax.ShapeDtypeStruct((tiles, head, width), f32),
            jax.ShapeDtypeStruct((total_keys, pair), f32),
        ],
        compiler_params=params(),
        name="attend_back",
    )(bases, kv, qt, q, grad_t, grad, lse, delta)


def place(index, pieces, expert):
    total = jnp.zeros(pieces[0].shape, f32)
    for j, piece in enumerate(pieces):
        total = jnp.where(index[j : j + 1, :] == expert, piece, total)
    return total


def middle_kernel(
    tokens_ref,
    grad_ref,
    index_ref,
    gate_ref,
    attended_ref,
    output_weight_ref,
    up_weight_ref,
    down_weight_ref,
    gain_ref,
    shift_ref,
    up_bias_ref,
    down_bias_ref,
    layer_out_ref,
    middle_grad_ref,
    grad_t_ref,
    grad_rows_ref,
    delta_ref,
    logit_grad_ref,
    output_weight_grad_ref,
    up_weight_grad_ref,
    down_weight_grad_ref,
    gain_grad_ref,
    shift_grad_ref,
    up_bias_grad_ref,
    down_bias_grad_ref,
    spread_ref,
    chosen_ref,
    dwo_ref,
    dup_ref,
    ddown_ref,
):
    step = pl.program_id(0)
    topk = index_ref.shape[0]
    head = attended_ref.shape[1]
    experts = output_weight_ref.shape[0] // head
    per = TILE // ROWS

    @pl.when(step == 0)
    def _():
        for ref in (
            dwo_ref,
            dup_ref,
            ddown_ref,
            gain_grad_ref,
            shift_grad_ref,
            up_bias_grad_ref,
            down_bias_grad_ref,
        ):
            ref[...] = jnp.zeros(ref.shape, ref.dtype)

    index = index_ref[...]
    gate = gate_ref[...]
    for part in range(per):
        lanes = slice(part * ROWS, (part + 1) * ROWS)
        pieces = [
            attended_ref[part, :, j * ROWS : (j + 1) * ROWS] * gate[j : j + 1, lanes]
            for j in range(topk)
        ]
        for expert in range(experts):
            spread_ref[expert * head : (expert + 1) * head, lanes] = place(
                index[:, lanes], pieces, expert
            ).astype(bf16)

    middle = tokens_ref[...].astype(f32).T + dot_tn(output_weight_ref[...], spread_ref[...])
    unit, inverse = column_norm(middle)
    second = (unit * gain_ref[...] + shift_ref[...]).astype(bf16)
    pre = dot_tn(up_weight_ref[...], second) + up_bias_ref[...]
    coeff = math.sqrt(2.0 / math.pi)
    square = pre * pre
    wave = jnp.tanh(coeff * pre * (1.0 + 0.044715 * square))
    half = 0.5 * (1.0 + wave)
    hidden = (pre * half).astype(bf16)
    slope = half + 0.5 * pre * (1.0 - wave * wave) * (coeff * (1.0 + 3 * 0.044715 * square))
    result = middle + dot_tn(down_weight_ref[...], hidden) + down_bias_ref[...]
    layer_out_ref[...] = result.T.astype(bf16)

    grad_rows = grad_ref[...]
    grad_wide = grad_rows.astype(f32)
    grad_t = grad_wide.T
    ddown_ref[...] += dot(hidden, grad_rows)
    down_bias_grad_ref[...] += jnp.sum(grad_wide, axis=0, keepdims=True)
    pre_grad = (dot(down_weight_ref[...], grad_t.astype(bf16)) * slope).astype(bf16)
    dup_ref[...] += dot_nt(second, pre_grad)
    up_bias_grad_ref[...] += fold_lanes(pre_grad.astype(f32))
    second_grad = dot(up_weight_ref[...], pre_grad)
    gain_grad_ref[...] += fold_lanes(second_grad * unit)
    shift_grad_ref[...] += fold_lanes(second_grad)
    middle_grad = grad_t + column_norm_back(second_grad, unit, inverse, gain_ref[...])
    middle_grad_ref[...] = middle_grad
    middle_low = middle_grad.astype(bf16)
    dwo_ref[...] += dot_nt(spread_ref[...], middle_low)
    chosen_ref[...] = dot(output_weight_ref[...], middle_low)

    for part in range(per):
        lanes = slice(part * ROWS, (part + 1) * ROWS)
        picks = []
        for j in range(topk):
            span = slice(j * ROWS, (j + 1) * ROWS)
            row = index[j : j + 1, lanes]
            chosen = jnp.zeros((head, ROWS), f32)
            for expert in range(experts):
                chosen = jnp.where(
                    row == expert, chosen_ref[expert * head : (expert + 1) * head, lanes], chosen
                )
            attended = attended_ref[part, :, span]
            picks.append(jnp.sum(chosen * attended, axis=0, keepdims=True))
            back = (chosen * gate[j : j + 1, lanes]).astype(bf16)
            grad_t_ref[part, :, span] = back
            back = back.astype(f32)
            grad_rows_ref[part, span, :] = back.T.astype(bf16)
            delta_ref[part, :, span] = jnp.sum(back * attended, axis=0, keepdims=True)
        gates = [gate[j : j + 1, lanes] for j in range(topk)]
        mean = sum(g * p for g, p in zip(gates, picks))
        rows = [g * (p - mean) for g, p in zip(gates, picks)]
        spare = logit_grad_ref.shape[0] - experts
        logit = [place(index[:, lanes], rows, expert) for expert in range(experts)]
        logit.append(jnp.zeros((spare, ROWS), f32))
        logit_grad_ref[:, lanes] = jnp.concatenate(logit, axis=0).astype(bf16)

    @pl.when(step == pl.num_programs(0) - 1)
    def _():
        output_weight_grad_ref[...] = dwo_ref[...].astype(bf16)
        up_weight_grad_ref[...] = dup_ref[...].astype(bf16)
        down_weight_grad_ref[...] = ddown_ref[...].astype(bf16)


def middle_call(
    tokens, grad, index, gate, attended, output_weight, up_weight, down_weight,
    gain, shift, up_bias, down_bias, padded,
):
    count, width = tokens.shape
    topk = index.shape[0]
    tiles, head, wide = attended.shape
    per = TILE // ROWS
    hidden = up_weight.shape[1]
    spread = output_weight.shape[0]
    rows = pl.BlockSpec((TILE, width), lambda i: (i, 0))
    columns = lambda n: pl.BlockSpec((n, TILE), lambda i: (0, i))
    tile = lambda shape: pl.BlockSpec((per,) + shape, lambda i: (i, 0, 0))
    shape = jax.ShapeDtypeStruct
    return pl.pallas_call(
        middle_kernel,
        grid=(count // TILE,),
        in_specs=[
            rows,
            rows,
            columns(topk),
            columns(topk),
            tile((head, wide)),
            whole(output_weight.shape),
            whole(up_weight.shape),
            whole(down_weight.shape),
            whole((width, 1)),
            whole((width, 1)),
            whole((hidden, 1)),
            whole((width, 1)),
        ],
        out_specs=[
            rows,
            columns(width),
            tile((head, wide)),
            tile((wide, head)),
            tile((1, wide)),
            columns(padded),
            whole(output_weight.shape),
            whole(up_weight.shape),
            whole(down_weight.shape),
            whole((width, 128)),
            whole((width, 128)),
            whole((hidden, 128)),
            whole((1, width)),
        ],
        out_shape=[
            shape((count, width), bf16),
            shape((width, count), f32),
            shape((tiles, head, wide), bf16),
            shape((tiles, wide, head), bf16),
            shape((tiles, 1, wide), f32),
            shape((padded, count), bf16),
            shape(output_weight.shape, bf16),
            shape(up_weight.shape, bf16),
            shape(down_weight.shape, bf16),
            shape((width, 128), f32),
            shape((width, 128), f32),
            shape((hidden, 128), f32),
            shape((1, width), f32),
        ],
        scratch_shapes=[
            pltpu.VMEM((spread, TILE), bf16),
            pltpu.VMEM((spread, TILE), f32),
            pltpu.VMEM(output_weight.shape, f32),
            pltpu.VMEM(up_weight.shape, f32),
            pltpu.VMEM(down_weight.shape, f32),
        ],
        compiler_params=params(),
        name="middle",
    )(tokens, grad, index, gate, attended, output_weight, up_weight, down_weight,
      gain, shift, up_bias, down_bias)


def query_back_kernel(
    first_ref,
    index_ref,
    dq_ref,
    query_weight_ref,
    logit_grad_ref,
    router_ref,
    partial_ref,
    query_weight_grad_ref,
    router_grad_ref,
    placed_ref,
    dwq_ref,
    dr_ref,
):
    step = pl.program_id(0)
    topk = index_ref.shape[0]
    head = dq_ref.shape[1]
    experts = query_weight_ref.shape[1] // head

    @pl.when(step == 0)
    def _():
        dwq_ref[...] = jnp.zeros(dwq_ref.shape, f32)
        dr_ref[...] = jnp.zeros(dr_ref.shape, f32)

    index = index_ref[...]
    for part in range(TILE // ROWS):
        lanes = slice(part * ROWS, (part + 1) * ROWS)
        pieces = [dq_ref[part, :, j * ROWS : (j + 1) * ROWS] for j in range(topk)]
        for expert in range(experts):
            placed_ref[expert * head : (expert + 1) * head, lanes] = place(
                index[:, lanes], pieces, expert
            ).astype(bf16)
    first = first_ref[...]
    dwq_ref[...] += dot_nt(first, placed_ref[...])
    dr_ref[...] += dot_nt(first, logit_grad_ref[...])
    partial_ref[...] = dot(query_weight_ref[...], placed_ref[...]) + dot(
        router_ref[...], logit_grad_ref[...]
    )

    @pl.when(step == pl.num_programs(0) - 1)
    def _():
        query_weight_grad_ref[...] = dwq_ref[...].astype(bf16)
        router_grad_ref[...] = dr_ref[...]


def query_back_call(first, index, dq, query_weight, logit_grad, router):
    width, count = first.shape
    topk = index.shape[0]
    tiles, head, wide = dq.shape
    padded = router.shape[1]
    columns = lambda n: pl.BlockSpec((n, TILE), lambda i: (0, i))
    shape = jax.ShapeDtypeStruct
    return pl.pallas_call(
        query_back_kernel,
        grid=(count // TILE,),
        in_specs=[
            columns(width),
            columns(topk),
            pl.BlockSpec((TILE // ROWS, head, wide), lambda i: (i, 0, 0)),
            whole(query_weight.shape),
            columns(padded),
            whole(router.shape),
        ],
        out_specs=[columns(width), whole(query_weight.shape), whole(router.shape)],
        out_shape=[
            shape((width, count), f32),
            shape(query_weight.shape, bf16),
            shape(router.shape, f32),
        ],
        scratch_shapes=[
            pltpu.VMEM((query_weight.shape[1], TILE), bf16),
            pltpu.VMEM(query_weight.shape, f32),
            pltpu.VMEM(router.shape, f32),
        ],
        compiler_params=params(),
        name="query_back",
    )(first, index, dq, query_weight, logit_grad, router)


def first_back_kernel(
    tokens_ref,
    first_ref,
    partial_ref,
    middle_grad_ref,
    dkv_ref,
    kv_weight_ref,
    gain_ref,
    tokens_grad_ref,
    kv_weight_grad_ref,
    gain_grad_ref,
    shift_grad_ref,
):
    step = pl.program_id(0)

    @pl.when(step == 0)
    def _():
        for ref in (kv_weight_grad_ref, gain_grad_ref, shift_grad_ref):
            ref[...] = jnp.zeros(ref.shape, ref.dtype)

    unit, inverse = column_norm(tokens_ref[...].astype(f32).T)
    dkv = dkv_ref[...]
    kv_weight_grad_ref[...] += dot(first_ref[...], dkv)
    first_grad = partial_ref[...] + dot_nt(kv_weight_ref[...], dkv)
    gain_grad_ref[...] += fold_lanes(first_grad * unit)
    shift_grad_ref[...] += fold_lanes(first_grad)
    total = middle_grad_ref[...] + column_norm_back(first_grad, unit, inverse, gain_ref[...])
    tokens_grad_ref[...] = total.T.astype(bf16)


def first_back_call(tokens, first, partial, middle_grad, dkv, kv_weight, gain):
    count, width = tokens.shape
    pair = kv_weight.shape[1]
    columns = lambda n: pl.BlockSpec((n, TILE), lambda i: (0, i))
    rows = lambda n: pl.BlockSpec((TILE, n), lambda i: (i, 0))
    shape = jax.ShapeDtypeStruct
    return pl.pallas_call(
        first_back_kernel,
        grid=(count // TILE,),
        in_specs=[
            rows(width),
            columns(width),
            columns(width),
            columns(width),
            rows(pair),
            whole(kv_weight.shape),
            whole((width, 1)),
        ],
        out_specs=[rows(width), whole(kv_weight.shape), whole((width, 128)), whole((width, 128))],
        out_shape=[
            shape((count, width), bf16),
            shape(kv_weight.shape, f32),
            shape((width, 128), f32),
            shape((width, 128), f32),
        ],
        compiler_params=params(),
        name="first_back",
    )(tokens, first, partial, middle_grad, dkv, kv_weight, gain)


def join(value):
    count = lax.axis_size("shard")
    if count != 2:
        return lax.all_gather(value, "shard", axis=0, tiled=True)
    other = lax.ppermute(value, "shard", [(0, 1), (1, 0)])
    low = lax.axis_index("shard") == 0
    return jnp.concatenate([jnp.where(low, value, other), jnp.where(low, other, value)], axis=0)


def reduce_parameter(grad):
    part = lax.psum_scatter(grad.astype(bf16), "shard", scatter_dimension=0, tiled=True)
    return lax.psum(part, "ctx").astype(f32)


def per_device(
    tokens,
    expert_index,
    first_gain,
    first_shift,
    router_weight,
    query_weight,
    key_weight,
    value_weight,
    output_weight,
    second_gain,
    second_shift,
    up_weight,
    up_bias,
    down_weight,
    down_bias,
    out_grad,
):
    groups, block, width = tokens.shape
    assert groups == 1
    topk = expert_index.shape[-1]
    experts = router_weight.shape[1]
    head = key_weight.shape[1]
    padded = 32
    spare = jnp.zeros((key_weight.shape[0], padded - experts), bf16)
    vectors = [first_gain, first_shift, second_gain, second_shift, down_bias]
    small = jnp.concatenate(
        [key_weight, value_weight, router_weight, spare] + [v[:, None] for v in vectors], axis=1
    )
    small = join(small)
    kv_weight = small[:, : 2 * head]
    router = small[:, 2 * head : 2 * head + padded]
    columns = [
        small[:, 2 * head + padded + i : 2 * head + padded + i + 1].astype(f32)
        for i in range(len(vectors))
    ]
    gain_one, shift_one, gain_two, shift_two, down_bias_all = columns
    query_all = join(query_weight)
    output_all = join(output_weight)
    up_all = join(up_weight)
    down_all = join(down_weight)
    up_bias_all = join(up_bias).astype(f32)[:, None]

    flat = tokens[0]
    grad = out_grad[0]
    index = expert_index[0].T
    first, kv = first_call(flat, gain_one, shift_one, kv_weight)
    gathered = lax.all_gather(kv, "ctx", axis=0, tiled=True)
    qt, q, gate = query_call(first, query_all, router, index, head)
    base = lax.axis_index("ctx") * block
    bases = base + jnp.arange(block // ROWS, dtype=jnp.int32) * ROWS
    segment = jnp.maximum(base, PROMPT) // CLEN * CLEN
    keys = jnp.concatenate(
        [gathered[:PROMPT], lax.dynamic_slice_in_dim(gathered, segment, CLEN, 0)], axis=0
    )
    attended, lse = attend_call(bases, keys, qt)
    (
        layer_out, middle_grad, grad_t, grad_rows, delta, logit_grad,
        output_weight_grad, up_weight_grad, down_weight_grad,
        second_gain_grad, second_shift_grad, up_bias_grad, down_bias_grad,
    ) = middle_call(
        flat, grad, index, gate, attended, output_all, up_all, down_all,
        gain_two, shift_two, up_bias_all, down_bias_all, padded,
    )
    output_weight_grad = reduce_parameter(output_weight_grad)
    up_weight_grad = reduce_parameter(up_weight_grad)
    down_weight_grad = reduce_parameter(down_weight_grad)
    dq, dkeys = attend_back_call(bases, keys, qt, q, grad_t, grad_rows, lse, delta)
    dall = jnp.concatenate(
        [dkeys[:PROMPT], jnp.zeros((gathered.shape[0] - PROMPT, 2 * head), f32)], axis=0
    )
    dall = lax.dynamic_update_slice_in_dim(
        dall, jnp.where(base >= PROMPT, dkeys[PROMPT:], 0.0), segment, 0
    )
    dkv = lax.psum_scatter(dall.astype(bf16), "ctx", scatter_dimension=0, tiled=True)
    partial, query_weight_grad, router_grad = query_back_call(
        first, index, dq, query_all, logit_grad, router
    )
    query_weight_grad = reduce_parameter(query_weight_grad)
    tokens_grad, kv_weight_grad, first_gain_grad, first_shift_grad = first_back_call(
        flat, first, partial, middle_grad, dkv, kv_weight, gain_one
    )
    vector_grads = [
        jnp.sum(first_gain_grad, axis=1),
        jnp.sum(first_shift_grad, axis=1),
        jnp.sum(second_gain_grad, axis=1),
        jnp.sum(second_shift_grad, axis=1),
        down_bias_grad[0],
    ]
    small_grad = jnp.concatenate(
        [kv_weight_grad, router_grad] + [v[:, None] for v in vector_grads], axis=1
    )
    small_grad = reduce_parameter(small_grad)
    up_bias_grad = reduce_parameter(jnp.sum(up_bias_grad, axis=1))
    at = 2 * head + padded
    return (
        layer_out[None],
        tokens_grad[None],
        small_grad[:, at],
        small_grad[:, at + 1],
        small_grad[:, 2 * head : 2 * head + experts],
        query_weight_grad,
        small_grad[:, :head],
        small_grad[:, head : 2 * head],
        output_weight_grad,
        small_grad[:, at + 2],
        small_grad[:, at + 3],
        up_weight_grad,
        up_bias_grad,
        down_weight_grad,
        small_grad[:, at + 4],
    )


def solution(mesh):
    split = P("shard", "ctx", None)
    vector = P("shard")
    matrix = P("shard", None)
    in_specs = (
        split, split, vector, vector, matrix, matrix, matrix, matrix, matrix,
        vector, vector, matrix, vector, matrix, vector, split,
    )
    out_specs = (
        split, split, vector, vector, matrix, matrix, matrix, matrix, matrix,
        vector, vector, matrix, vector, matrix, vector,
    )
    return jax.shard_map(
        per_device, mesh=mesh, in_specs=in_specs, out_specs=out_specs, check_vma=False
    )
```

time: 2170 us -> 837 us (0.39)
  local copies, waits for them, and re-layouts: 415 us -> 29.5 us
  waiting for transfers between devices: 955 us -> 593 us
  blocking collectives: 362 us -> 37.8 us
  matrix products: 177 us -> 0 us
  other arithmetic: 198 us -> 33.6 us
  Pallas kernels: 0 us -> 118 us
  loops' own time: 34.1 us -> 0 us
    reduce_scatter x8 -> x6, waiting for transfers between devices: 949 us -> 440 us  [the longest x1 312 us: per_device(): lax.psum_scatter(dall.astype(bf16), 'ctx', scatter_dimension=0, tiled=True)]
    gather x9 -> x0, local copies, waits for them, and re-layouts: 289 us -> none  [the longest x2 123 us: per_device(): chosen_grad = jnp.take_along_axis(spread_grad, chosen[:, :, None], axis=1)]
    psum x1, blocking collectives: 317 us -> 32.8 us  [reduce_parameter(): return lax.psum(part, 'ctx').astype(f32)]
    dot_general x27 -> x0, matrix products: 177 us -> none  [the longest x1 15.3 us: update_compute(): jnp.einsum('gbhk,gkd->gbhd', weights_low, values, preferred_element_type=...]
    pallas_call x0 -> x7, Pallas kernels: none -> 118 us  [the longest x1 44.5 us: middle_call(): pl.pallas_call(middle_kernel, grid=(count // TILE,), in_specs=[rows, rows...]
    reduce_or x32 -> x0, other arithmetic: 81.8 us -> none  [the longest x16 46.3 us: block_grads(): return lax.cond(jnp.any(allowed), block_compute, skipped, 0)]
    ppermute x0 -> x6, waiting for transfers between devices: none -> 78.1 us  [join(): other = lax.ppermute(value, 'shard', [(0, 1), (1, 0)])]
    psum x0 -> x1, waiting for transfers between devices: none -> 73.9 us  [reduce_parameter(): return lax.psum(part, 'ctx').astype(f32)]
  transfers between devices with their start and end apart: 13 -> 14, of which waited for: 5 -> 9; matrix products, arithmetic and copies ran while one was open for 19% -> 2% of each run, Pallas kernels for 0% -> 3%
where the time goes in v1:
time: 837 us; the launch traced here: 836 us
  waiting for transfers between devices  593 us (71%)
  Pallas kernels  118 us (14%)
  blocking collectives  37.8 us (5%)
  other arithmetic  33.6 us (4%)
  local copies, waits for them, and re-layouts  29.5 us (4%)
  between operations  15.1 us (2%)
  starting transfers between devices  9.21 us (1%)
    reduce_scatter x1, waiting for transfers between devices, per_device(): lax.psum_scatter(dall.astype(bf16), 'ctx', scatter_dimension=0, tiled=True)  312 us
    reduce_scatter x5, waiting for transfers between devices, reduce_parameter(): lax.psum_scatter(grad.astype(bf16), 'shard', scatter_dimension=0, tiled=T...  128 us
    ppermute x6, waiting for transfers between devices, join(): other = lax.ppermute(value, 'shard', [(0, 1), (1, 0)])  78.1 us
    psum x1, waiting for transfers between devices, reduce_parameter(): return lax.psum(part, 'ctx').astype(f32)  73.9 us
    pallas_call x1, Pallas kernels, middle_call(): pl.pallas_call(middle_kernel, grid=(count // TILE,), in_specs=[rows, rows...  44.5 us
    psum x1, blocking collectives, reduce_parameter(): return lax.psum(part, 'ctx').astype(f32)  32.8 us
    pallas_call x1, Pallas kernels, attend_back_call(): pl.pallas_call(attend_back_kernel, grid_spec=pltpu.PrefetchScalarGridSpec...  26.6 us
  transfers between devices with their start and end apart: 14, of which 9 were waited for; matrix products, arithmetic and copies ran while one was open for 2% of the time, Pallas kernels for 3%

profile of v1, /device:TPU:0, one launch (start us, length us, event | category | flops | bytes accessed | tf_op | source)
XLA Modules:
  0.0 836.3 jit_solution(4122400341575969587)
XLA Ops:
  7.2 0.8 broadcast_in_dim.59
  8.0 0.8 broadcast_in_dim.60
  8.7 0.8 broadcast_in_dim.61
  9.5 0.8 broadcast_in_dim.62
  10.3 0.8 broadcast_in_dim.63
  11.0 0.9 copy.72
  11.9 0.9 copy.73
  12.8 0.8 copy.74
  13.9 3.0 collective-permute-start
  16.9 3.5 collective-permute-done
  20.5 1.3 fusion.10
  21.7 0.7 fusion.6.kv_weight_ref
  22.4 4.7 first_norm.1
  27.2 1.8 collective-permute-start.1
  29.3 1.7 collective-permute-start.4
  31.3 1.7 collective-permute-start.5
  33.6 74.5 %collective-permute-done.5 = bf16[1024]{0:T(1024)(128)(2,1)S(1)} collective-permute-done((bf16[1024]{0:T(1024)(128)(2,1)S(1)}, bf16[1024]{0:T(1024)(128)(2,1)S(1)}, u32[]{:S(2)}, u32[]{:S(2)}) %collective-permute-start.5) | collective-permute-done | bytes 2080 | tf_op jit(solution)/shard_map/ppermute | solution.py:723
  108.2 1.4 copy.80.up_bias_ref
  109.5 0.7 fusion.7.router_ref
  110.2 1.5 broadcast_select_fusion.7
  111.7 1.2 pad_maximum_fusion.3.query_weight_ref
  112.9 9.6 %queries.1 = (bf16[8,64,1024]{2,1,0:T(8,128)(2,1)}, bf16[8,1024,64]{2,1,0:T(8,128)(2,1)}, f32[8,1024]{1,0:T(8,128)}) custom-call(bf16[512,1024]{1,0:T(8,128)(2,1)} %get-tuple-element.44.first_ref, bf16[512,1536]{1,0:T(8,128)(2,1)} %pad_maximum_fusion.3.query_weight_ref, bf16[512,32]{1,0:T(8,128)(2,1)} %fusion.7.router_ref, s32[8,1024]{1,0:T(8,128)} %bitcast.14), custom_call_target="tpu_custom_call" | custom-call | tf_op jit(solution)/shard_map/queries/pallas_call | solution.py:135
  122.6 1.5 broadcast_select_fusion.5
  124.1 1.2 pad_maximum_fusion.4.output_weight_ref
  125.3 1.4 broadcast_select_fusion.3
  126.7 1.6 pad_maximum_fusion.1.up_weight_ref
  128.4 1.5 pad_maximum_fusion.2.down_weight_ref
  129.9 1.7 slice.80
  131.6 1.0 constant_dynamic-slice_fusion
  132.6 6.2 pad_maximum_fusion.kv_ref
  138.8 16.3 %attend.1 = (f32[8,64,1024]{2,1,0:T(8,128)}, f32[8,1,1024]{2,1,0:T(1,128)}) custom-call(s32[8]{0:T(128)} %multiply_add_fusion.base_ref, bf16[9216,128]{1,0:T(8,128)(2,1)} %pad_maximum_fusion.kv_ref, bf16[8,64,1024]{2,1,0:T(8,128)(2,1)} %get-tuple-element.47.qt_ref), custom_call_target="tpu_custom_call" | custom-call | tf_op jit(solution)/shard_map/attend/pallas_call | solution.py:254
  155.0 44.5 %middle.1 = (bf16[1024,512]{1,0:T(8,128)(2,1)}, f32[512,1024]{1,0:T(8,128)}, bf16[8,64,1024]{2,1,0:T(8,128)(2,1)}, bf16[8,1024,64]{2,1,0:T(8,128)(2,1)}, f32[8,1...) custom-call(bf16[1024,512]{1,0:T(8,128)(2,1)} %bitcast.11, ...), custom_call_target="tpu_custom_call" | custom-call | tf_op jit(solution)/shard_map/middle/pallas_call | solution.py:520
  199.6 26.6 %attend_back.1 = (f32[8,64,1024]{2,1,0:T(8,128)}, f32[9216,128]{1,0:T(8,128)}) custom-call(s32[8]{0:T(128)} %multiply_add_fusion.base_ref, bf16[9216,128]{1,0:T(8,128)(2,1)} %pad_maximum_fusion.kv_ref, bf16[8,64,1024]{2,1,0:T(8,128)(2,1)} %get-tuple-element.47.qt_ref, bf16[8,1024,64]{2,1,0:T(8,128)(2,1)} %get-tuple-element.50.q_ref, ...), custom_call_target="tpu_custom_call" | custom-call | tf_op jit(solution)/shard_map/attend_back/pallas_call | solution.py:343
  226.2 2.4 slice.62
  228.6 9.0 %concatenate.52 = bf16[16384,128]{1,0:T(8,128)(2,1)} pad(bf16[8192,128]{1,0:T(8,128)(2,1)S(1)} %slice.62, f32[]{:T(128)} %constant.38.clone.1), padding=0_8192x0_0 | pad | bytes 6291460 | tf_op jit(solution)/shard_map/concatenate | solution.py:801
  237.6 1.8 select_dynamic-update-slice_fusion
  239.5 9.5 %query_back.1 = (f32[512,1024]{1,0:T(8,128)}, bf16[512,1536]{1,0:T(8,128)(2,1)}, f32[512,32]{1,0:T(8,128)}) custom-call(bf16[512,1024]{1,0:T(8,128)(2,1)} %get-tuple-element.44.first_ref, s32[8,1024]{1,0:T(8,128)} %bitcast.16, f32[8,64,1024]{2,1,0:T(8,128)} %get-tuple-element.55.dq_ref, bf16[512,1536]{1,0:T(8,128)(2,1)} %pad_maximum_fusion.3.query_weight_ref, ...), custom_call_target="tpu_custom_call" | custom-call | tf_op jit(solution)/shard_map/query_back/pallas_call | solution.py:632
  251.6 312.1 %reduce-scatter.7.cloned.1.call-done.dkv_ref = bf16[1024,128]{1,0:T(8,128)(2,1)} async-done(((bf16[16384,128]{1,0:T(8,128)(2,1)}), bf16[1024,128]{1,0:T(8,128)(2,1)}) %reduce-scatter.7.cloned.1.call-update) | async-done | bytes 262160 | tf_op jit(solution)/shard_map/reduce_scatter | solution.py:807
  563.7 6.5 first_back.1
  570.2 1.1 reduce_sum.45
  571.5 1.1 reduce_sum.46
  572.8 1.0 convert.26
  573.7 1.1 concatenate.53
  574.9 16.8 %reduce-scatter.11.cloned.1.call-done = bf16[256,1536]{1,0:T(8,128)(2,1)} async-done(((bf16[512,1536]{1,0:T(8,128)(2,1)}), bf16[256,1536]{1,0:T(8,128)(2,1)}) %reduce-scatter.11.cloned.1.call-update) | async-done | bytes 786448 | tf_op jit(solution)/shard_map/reduce_scatter | solution.py:729
  591.7 28.2 %reduce-scatter.13.cloned.1.call-done = bf16[768,512]{1,0:T(8,128)(2,1)} async-done(((bf16[1536,512]{1,0:T(8,128)(2,1)}), bf16[768,512]{1,0:T(8,128)(2,1)}) %reduce-scatter.13.cloned.1.call-update) | async-done | bytes 786448 | tf_op jit(solution)/shard_map/reduce_scatter | solution.py:729
  619.9 34.1 %reduce-scatter.15.cloned.1.call-done = bf16[256,2048]{1,0:T(8,128)(2,1)} async-done(((bf16[512,2048]{1,0:T(8,128)(2,1)}), bf16[256,2048]{1,0:T(8,128)(2,1)}) %reduce-scatter.15.cloned.1.call-update) | async-done | bytes 1048592 | tf_op jit(solution)/shard_map/reduce_scatter | solution.py:729
  654.0 34.0 %reduce-scatter.17.cloned.1.call-done = bf16[1024,512]{1,0:T(8,128)(2,1)} async-done(((bf16[2048,512]{1,0:T(8,128)(2,1)}), bf16[1024,512]{1,0:T(8,128)(2,1)}) %reduce-scatter.17.cloned.1.call-update) | async-done | bytes 1048592 | tf_op jit(solution)/shard_map/reduce_scatter | solution.py:729
  688.0 14.6 %reduce-scatter.9.cloned.1.call-done = bf16[256,165]{1,0:T(8,128)(2,1)} async-done(((bf16[512,165]{1,0:T(8,128)(2,1)}), bf16[256,165]{1,0:T(8,128)(2,1)}) %reduce-scatter.9.cloned.1.call-update) | async-done | bytes 84496 | tf_op jit(solution)/shard_map/reduce_scatter | solution.py:729
  702.6 0.6 dynamic-slice
  704.2 4.9 all-reduce.1
  709.1 32.8 %psum.46 = bf16[1024]{0:T(1024)(128)(2,1)S(1)} all-reduce(bf16[1024]{0:T(1024)(128)(2,1)S(1)} %dynamic-slice.1), channel_id=1, replica_groups=mesh['ctx'=16,'shard'=2] {'ctx'}, use_global_device_ids=true, to_apply=%region_15.16 | all-reduce | flops 1024 | bytes 4096 | tf_op jit(solution)/shard_map/psum | solution.py:730
  742.0 0.6 convert_element_type.62
  742.6 73.9 %all-reduce.5.cloned.1.call-done = (bf16[256,165]{1,0:T(8,128)(2,1)}, bf16[256,1536]{1,0:T(8,128)(2,1)}, bf16[768,512]{1,0:T(8,128)(2,1)}, bf16[256,2048]{1,0:T(8,128)(2,1)}, bf16[1024,512]{1,0:T(8,128)(2,1)}) async-done(((bf16[256,165]{1,0:T(8,128)(2,1)}, bf16[256,1536]{1,0:T(8,128)(2,1)}, bf16[768,512]{1,0:T(8,128)(2,1)}, bf16[256,2048]{1,0:T(8,128)(2,1)}, bf16[1024,512]{1,0:T(8,128)(2,1)}), ...) | async-done | bytes 3754512 | tf_op jit(solution)/shard_map/psum | solution.py:730
  816.4 1.0 fusion.11
  817.5 0.9 convert_element_type.57
  818.4 0.9 slice.87
  819.3 2.8 convert_element_type.60
  822.1 1.6 convert_element_type.63
  823.7 1.3 convert_element_type.58
  825.0 1.4 convert_element_type.59
  826.4 0.7 copy.87
  827.1 0.7 copy.88
  827.8 1.0 slice_reduce_fusion
  828.8 0.7 copy.86
  (67 shorter events, 4.9 us)
Async XLA Ops:
  7.2 122.7 %all-gather.2.cloned.1.call-start = ((), (), s32[]{:S(2)}) async-start(), calls=%async_computation.6 | async-start | bytes 4456448 | tf_op jit(solution)/shard_map/all_gather | solution.py:780
  13.9 6.5 collective-permute-start
  20.4 8.6 %copy-start = (bf16[256,2048]{1,0:T(8,128)(2,1)S(1)}, bf16[256,2048]{1,0:T(8,128)(2,1)}, u32[]{:S(2)}) copy-start(bf16[256,2048]{1,0:T(8,128)(2,1)} %param.27) | copy-start | bytes 3145732
  20.4 8.9 %copy-start.1 = (bf16[1024,512]{1,0:T(8,128)(2,1)S(1)}, bf16[1024,512]{1,0:T(8,128)(2,1)}, u32[]{:S(2)}) copy-start(bf16[1024,512]{1,0:T(8,128)(2,1)} %param.29) | copy-start | bytes 3145732
  20.4 10.9 %copy-start.9 = (bf16[1024]{0:T(1024)(128)(2,1)S(1)}, bf16[1024]{0:T(1024)(128)(2,1)}, u32[]{:S(2)}) copy-start(bf16[1024]{0:T(1024)(128)(2,1)} %param.28) | copy-start | bytes 6148
  27.1 536.6 %reduce-scatter.7.cloned.1.call-start = ((), (), s32[]{:S(2)}) async-start(), calls=%async_computation.7 | async-start | bytes 4456448 | tf_op jit(solution)/shard_map/reduce_scatter | solution.py:807
  27.2 83.0 %collective-permute-start.1 = (bf16[256,1536]{1,0:T(8,128)(2,1)}, bf16[256,1536]{1,0:T(8,128)(2,1)}, u32[]{:S(2)}, u32[]{:S(2)}) collective-permute-start(bf16[256,1536]{1,0:T(8,128)(2,1)} %param.21), channel_id=1, source_target_pairs={{0,1},{1,0},{2,3},{3,2},{4,5},{5,4},{6,7},{7,6},{8,9},{9,8},{10,11... | collective-permute-start | bytes 2359304 | tf_op jit(solution)/shard_map/ppermute | solution.py:723
  29.0 96.3 %collective-permute-start.3 = (bf16[256,2048]{1,0:T(8,128)(2,1)S(1)}, bf16[256,2048]{1,0:T(8,128)(2,1)}, u32[]{:S(2)}, u32[]{:S(2)}) collective-permute-start(bf16[256,2048]{1,0:T(8,128)(2,1)S(1)} %copy-done), channel_id=1, source_target_pairs={{0,1},{1,0},{2,3},{3,2},{4,5},{5,4},{6,7},{7,6},{8,9},{9,8},{10,11... | collective-permute-start | bytes 3145736 | tf_op jit(solution)/shard_map/ppermute | solution.py:723
  29.3 98.9 %collective-permute-start.4 = (bf16[1024,512]{1,0:T(8,128)(2,1)S(1)}, bf16[1024,512]{1,0:T(8,128)(2,1)S(1)}, u32[]{:S(2)}, u32[]{:S(2)}) collective-permute-start(bf16[1024,512]{1,0:T(8,128)(2,1)S(1)} %copy-done.1), channel_id=1, source_target_pairs={{0,1},{1,0},{2,3},{3,2},{4,5},{5,4},{6,7},{7,6},{8,9},{9,8},{10,11... | collective-permute-start | bytes 3145736 | tf_op jit(solution)/shard_map/ppermute | solution.py:723
  31.0 91.5 %collective-permute-start.2 = (bf16[768,512]{1,0:T(8,128)(2,1)}, bf16[768,512]{1,0:T(8,128)(2,1)}, u32[]{:S(2)}, u32[]{:S(2)}) collective-permute-start(bf16[768,512]{1,0:T(8,128)(2,1)} %param.24), channel_id=1, source_target_pairs={{0,1},{1,0},{2,3},{3,2},{4,5},{5,4},{6,7},{7,6},{8,9},{9,8},{10,11... | collective-permute-start | bytes 2359304 | tf_op jit(solution)/shard_map/ppermute | solution.py:723
  31.3 76.8 %collective-permute-start.5 = (bf16[1024]{0:T(1024)(128)(2,1)S(1)}, bf16[1024]{0:T(1024)(128)(2,1)S(1)}, u32[]{:S(2)}, u32[]{:S(2)}) collective-permute-start(bf16[1024]{0:T(1024)(128)(2,1)S(1)} %copy-done.9), channel_id=1, source_target_pairs={{0,1},{1,0},{2,3},{3,2},{4,5},{5,4},{6,7},{7,6},{8,9},{9,8},{10,11... | collective-permute-start | bytes 6152 | tf_op jit(solution)/shard_map/ppermute | solution.py:723
  239.4 352.3 %reduce-scatter.11.cloned.1.call-start = ((), (), s32[]{:S(2)}) async-start(), calls=%async_computation.9 | async-start | bytes 2359296 | tf_op jit(solution)/shard_map/reduce_scatter | solution.py:729
  249.0 370.9 %reduce-scatter.13.cloned.1.call-start = ((), (), s32[]{:S(2)}) async-start(), calls=%async_computation.10 | async-start | bytes 2359296 | tf_op jit(solution)/shard_map/reduce_scatter | solution.py:729
  249.6 404.4 %reduce-scatter.15.cloned.1.call-start = ((), (), s32[]{:S(2)}) async-start(), calls=%async_computation.11 | async-start | bytes 3145728 | tf_op jit(solution)/shard_map/reduce_scatter | solution.py:729
  249.6 1.2 copy-start.6
  249.6 1.2 copy-start.10
  249.7 1.4 copy-start.8
  249.7 1.7 copy-start.7
  250.2 437.8 %reduce-scatter.17.cloned.1.call-start = ((), (), s32[]{:S(2)}) async-start(), calls=%async_computation.12 | async-start | bytes 3145728 | tf_op jit(solution)/shard_map/reduce_scatter | solution.py:729
  250.8 451.8 %reduce-scatter.9.cloned.1.call-start = ((), (), s32[]{:S(2)}) async-start(), calls=%async_computation.8 | async-start | bytes 393216 | tf_op jit(solution)/shard_map/reduce_scatter | solution.py:729
  574.8 127.7 %copy-start.11 = (u32[32]{0:T(128)S(1)}, u32[32]{0:T(128)}, u32[]{:S(2)}) copy-start(u32[32]{0:T(128)} %constant.46) | copy-start | bytes 388
  574.8 129.0 %copy-start.3 = (f32[2048,128]{1,0:T(8,128)S(1)}, f32[2048,128]{1,0:T(8,128)}, u32[]{:S(2)}) copy-start(f32[2048,128]{1,0:T(8,128)} %get-tuple-element.71) | copy-start | bytes 3145732
  574.9 241.6 %all-reduce.5.cloned.1.call-start = ((), (), s32[]{:S(2)}) async-start(), calls=%async_computation.13 | async-start | bytes 7602176 | tf_op jit(solution)/shard_map/psum | solution.py:730
  816.4 5.6 copy-start.2
  822.0 1.6 copy-start.5
  822.0 2.9 copy-start.4
Sparse Core Ops, SparseCore 0:
  27.3 52.0 all-gather.1
  239.5 324.1 reduce-scatter.6
  566.6 25.0 reduce-scatter.10
  593.8 26.0 reduce-scatter.12
  622.1 31.8 reduce-scatter.14
  656.1 31.8 reduce-scatter.16
  690.8 11.6 reduce-scatter.8
  706.9 109.4 all-reduce.4

commit v2 on v1

--- a/solution.py
+++ b/solution.py
@@ -14,6 +14,7 @@
 TILE = 256
 FULL = 1024
 PART = 256
+HALF = PROMPT // 2
 VMEM = 60 << 20
 
 norm_eps = 1e-05
@@ -37,6 +38,10 @@
 
 def params(**kw):
     return pltpu.CompilerParams(vmem_limit_bytes=VMEM, **kw)
+
+
+def cost(us):
+    return pl.CostEstimate(flops=int(us * 1.15e9), transcendentals=0, bytes_accessed=0)
 
 
 def whole(shape):
@@ -97,12 +102,27 @@
             jax.ShapeDtypeStruct((count, pair), bf16),
         ],
         compiler_params=params(),
+        cost_estimate=cost(5),
         name="first_norm",
     )(tokens, gain, shift, kv_weight)
 
 
-def query_kernel(first_ref, query_weight_ref, router_ref, index_ref, qt_ref, q_ref, gate_ref):
+def join_rows(shard, own_ref, other_ref, all_ref):
+    half = own_ref.shape[0]
+    all_ref[pl.ds(pl.multiple_of(shard * half, half), half), :] = own_ref[...]
+    all_ref[pl.ds(pl.multiple_of((1 - shard) * half, half), half), :] = other_ref[...]
+
+
+def query_kernel(
+    shard_ref, first_ref, own_ref, other_ref, router_ref, index_ref,
+    qt_ref, q_ref, gate_ref, query_weight_ref,
+):
     topk = index_ref.shape[0]
+
+    @pl.when(pl.program_id(0) == 0)
+    def _():
+        join_rows(shard_ref[0], own_ref, other_ref, query_weight_ref)
+
     head = qt_ref.shape[1]
     experts = query_weight_ref.shape[1] // head
     first = first_ref[...]
@@ -127,42 +147,52 @@
             q_ref[part, j * ROWS : (j + 1) * ROWS, :] = chosen.T.astype(bf16)
 
 
-def query_call(first, query_weight, router, index, head):
+def query_call(shard, first, own, other, router, index, head):
     width, count = first.shape
     topk = index.shape[0]
     tiles = count // ROWS
     per = TILE // ROWS
+    keep = lambda shape: pl.BlockSpec(shape, lambda i, s: (0, 0))
     return pl.pallas_call(
         query_kernel,
-        grid=(count // TILE,),
-        in_specs=[
-            pl.BlockSpec((width, TILE), lambda i: (0, i)),
-            whole(query_weight.shape),
-            whole(router.shape),
-            pl.BlockSpec((topk, TILE), lambda i: (0, i)),
-        ],
-        out_specs=[
-            pl.BlockSpec((per, head, topk * ROWS), lambda i: (i, 0, 0)),
-            pl.BlockSpec((per, topk * ROWS, head), lambda i: (i, 0, 0)),
-            pl.BlockSpec((topk, TILE), lambda i: (0, i)),
-        ],
+        grid_spec=pltpu.PrefetchScalarGridSpec(
+            num_scalar_prefetch=1,
+            grid=(count // TILE,),
+            in_specs=[
+                pl.BlockSpec((width, TILE), lambda i, s: (0, i)),
+                keep(own.shape),
+                keep(other.shape),
+                keep(router.shape),
+                pl.BlockSpec((topk, TILE), lambda i, s: (0, i)),
+            ],
+            out_specs=[
+                pl.BlockSpec((per, head, topk * ROWS), lambda i, s: (i, 0, 0)),
+                pl.BlockSpec((per, topk * ROWS, head), lambda i, s: (i, 0, 0)),
+                pl.BlockSpec((topk, TILE), lambda i, s: (0, i)),
+            ],
+            scratch_shapes=[pltpu.VMEM((width, own.shape[1]), bf16)],
+        ),
         out_shape=[
             jax.ShapeDtypeStruct((tiles, head, topk * ROWS), bf16),
             jax.ShapeDtypeStruct((tiles, topk * ROWS, head), bf16),
             jax.ShapeDtypeStruct((topk, count), f32),
         ],
         compiler_params=params(),
+        cost_estimate=cost(10),
         name="queries",
-    )(first, query_weight, router, index)
-
-
-def tile_ranges(base):
+    )(shard, first, own, other, router, index)
+
+
+def tile_ranges(base, origin, segment):
     prompt = base < PROMPT
-    steps = jnp.where(prompt, base // FULL, PROMPT // FULL)
-    begin = steps * FULL
-    position = jnp.where(prompt, begin, PROMPT + (base - PROMPT) // CLEN * CLEN)
-    parts = (base + ROWS - position + PART - 1) // PART
-    return steps, begin, position, parts
+    seen = jnp.clip(base // FULL * FULL - origin, 0, HALF)
+    begin = jnp.where(prompt, seen, HALF)
+    position = jnp.where(prompt, origin + seen, PROMPT + (base - PROMPT) // CLEN * CLEN)
+    inside = prompt & (base >= origin) & (base < origin + HALF)
+    if segment:
+        inside = inside | jnp.logical_not(prompt)
+    parts = jnp.where(inside, (base + ROWS - position + PART - 1) // PART, 0)
+    return begin // FULL, begin, position, parts
 
 
 def allowed_mask(position, base, width):
@@ -171,35 +201,55 @@
     return key_pos <= query_pos
 
 
-def attend_kernel(base_ref, kv_ref, qt_ref, out_ref, lse_ref, vt_ref, knorm_ref, acc_ref, max_ref):
+def for_slots(refs, table_ref, visit):
+    slot = 0
+    for ref in refs:
+        for row in range(0, ref.shape[0], PART):
+            place_of = pl.multiple_of(table_ref[slot] * PART, PART)
+            visit(ref, row, pl.ds(place_of, PART))
+            slot += 1
+
+
+def attend_kernel(origin, buffers, first, last, base_ref, table_ref, *refs):
+    sources = refs[:buffers]
+    qt_ref = refs[buffers]
+    refs = refs[buffers + 1 :]
+    if not first:
+        acc_in_ref, max_in_ref = refs[:2]
+        refs = refs[2:]
+    out_ref, lse_ref, kv_ref, vt_ref, knorm_ref, acc_ref, max_ref = refs
     tile = pl.program_id(0)
     head, width = qt_ref.shape[1:]
-    total_keys = kv_ref.shape[0]
     factor = LOG2E * head ** (-0.5)
 
     @pl.when(tile == 0)
     def _():
         knorm_ref[0] = 0.0
 
-        def turn(i, carry):
-            span = pl.ds(pl.multiple_of(i * FULL, FULL), FULL)
-            both = kv_ref[span, :].T
+        def turn(ref, row, span):
+            rows = ref[row : row + PART, :]
+            kv_ref[span, :] = rows
+            both = rows.T
             vt_ref[:head, span] = both[head:, :]
-            vt_ref[head:, span] = jnp.ones((vt_ref.shape[0] - head, FULL), bf16)
+            vt_ref[head:, span] = jnp.ones((vt_ref.shape[0] - head, PART), bf16)
             keys = both[:head, :].astype(f32)
             most = jnp.max(jnp.sum(keys * keys, axis=0, keepdims=True))
             knorm_ref[0] = jnp.maximum(knorm_ref[0], most)
-            return carry
-
-        lax.fori_loop(0, total_keys // FULL, turn, 0)
+
+        for_slots(sources, table_ref, turn)
 
     base = base_ref[tile]
-    steps, begin, position, parts = tile_ranges(base)
+    steps, begin, position, parts = tile_ranges(base, origin, buffers > 2)
     query = qt_ref[0].astype(f32)
     qnorm = jnp.max(jnp.sum(query * query, axis=0, keepdims=True))
     narrow = qnorm * knorm_ref[0] * (factor * factor) < 100.0 * 100.0
-    acc_ref[...] = jnp.zeros(acc_ref.shape, f32)
-    max_ref[...] = jnp.zeros(max_ref.shape, f32)
+    if first:
+        acc_ref[...] = jnp.zeros(acc_ref.shape, f32)
+        max_ref[...] = jnp.full(max_ref.shape, jnp.where(narrow, 0.0, mask_fill), f32)
+    else:
+        acc_ref[...] = acc_in_ref[0]
+        max_ref[...] = max_in_ref[0]
+        narrow = narrow & (jnp.max(jnp.abs(max_in_ref[0])) == 0.0)
 
     def plain(offset, size, mask):
         span = pl.ds(pl.multiple_of(offset, size), size)
@@ -224,8 +274,6 @@
 
     @pl.when(jnp.logical_not(narrow))
     def _():
-        max_ref[...] = jnp.full(max_ref.shape, mask_fill, f32)
-
         def part(i, carry):
             before = i < steps * (FULL // PART)
             offset = i * PART
@@ -243,28 +291,35 @@
 
         lax.fori_loop(0, steps * (FULL // PART) + parts, part, 0)
 
-    total = acc_ref[head : head + 1, :]
-    out_ref[0] = acc_ref[:head, :] / total
-    lse_ref[0] = max_ref[...] + jnp.log2(total)
-
-
-def attend_call(bases, kv, qt):
+    if last:
+        total = acc_ref[head : head + 1, :]
+        out_ref[0] = acc_ref[:head, :] / total
+        lse_ref[0] = max_ref[...] + jnp.log2(total)
+    else:
+        out_ref[0] = acc_ref[...]
+        lse_ref[0] = max_ref[...]
+
+
+def attend_call(origin, sources, table, bases, qt, state=None, last=False):
     tiles, head, width = qt.shape
-    total_keys, pair = kv.shape
+    total_keys = sum(x.shape[0] for x in sources)
+    pair = sources[0].shape[1]
+    rows = head if last else head + 16
+    one = lambda shape: pl.BlockSpec((1,) + shape, lambda i, b, t: (i, 0, 0))
+    keep = lambda x: pl.BlockSpec(x.shape, lambda i, b, t: (0, 0))
+    state = () if state is None else tuple(state)
+    body = functools.partial(attend_kernel, origin, len(sources), not state, last)
     return pl.pallas_call(
-        attend_kernel,
+        body,
         grid_spec=pltpu.PrefetchScalarGridSpec(
-            num_scalar_prefetch=1,
+            num_scalar_prefetch=2,
             grid=(tiles,),
-            in_specs=[
-                pl.BlockSpec((total_keys, pair), lambda i, b: (0, 0)),
-                pl.BlockSpec((1, head, width), lambda i, b: (i, 0, 0)),
-            ],
-            out_specs=[
-                pl.BlockSpec((1, head, width), lambda i, b: (i, 0, 0)),
-                pl.BlockSpec((1, 1, width), lambda i, b: (i, 0, 0)),
-            ],
+            in_specs=[keep(x) for x in sources]
+            + [one((head, width))]
+            + ([one((head + 16, width)), one((1, width))] if state else []),
+            out_specs=[one((rows, width)), one((1, width))],
             scratch_shapes=[
+                pltpu.VMEM((total_keys, pair), bf16),
                 pltpu.VMEM((head + 16, total_keys), bf16),
                 pltpu.SMEM((1,), f32),
                 pltpu.VMEM((head + 16, width), f32),
@@ -272,35 +327,42 @@
             ],
         ),
         out_shape=[
-            jax.ShapeDtypeStruct((tiles, head, width), f32),
+            jax.ShapeDtypeStruct((tiles, rows, width), f32),
             jax.ShapeDtypeStruct((tiles, 1, width), f32),
         ],
         compiler_params=params(),
+        cost_estimate=cost(33),
         name="attend",
-    )(bases, kv, qt)
-
-
-def attend_back_kernel(
-    base_ref, kv_ref, qt_ref, q_ref, dot_ref, do_ref, lse_ref, delta_ref, dq_ref, dkv_ref, kt_ref
-):
+    )(bases, table, *sources, qt, *state)
+
+
+def attend_back_kernel(origin, buffers, first, base_ref, table_ref, *refs):
+    sources = refs[:buffers]
+    qt_ref, q_ref, dot_ref, do_ref, lse_ref, delta_ref = refs[buffers : buffers + 6]
+    refs = refs[buffers + 6 :]
+    if not first:
+        dq_in_ref = refs[0]
+        refs = refs[1:]
+    dq_ref = refs[0]
+    outs = refs[1 : 1 + buffers]
+    kv_ref, kt_ref, dkv_ref = refs[1 + buffers :]
     tile = pl.program_id(0)
     head, width = qt_ref.shape[1:]
-    total_keys = kv_ref.shape[0]
     scale = head ** (-0.5)
 
     @pl.when(tile == 0)
     def _():
-        def turn(i, carry):
-            span = pl.ds(pl.multiple_of(i * FULL, FULL), FULL)
-            kt_ref[:, span] = kv_ref[span, :].T[:head, :]
-            dkv_ref[span, :] = jnp.zeros((FULL, 2 * head), f32)
-            return carry
-
-        lax.fori_loop(0, total_keys // FULL, turn, 0)
+        def turn(ref, row, span):
+            rows = ref[row : row + PART, :]
+            kv_ref[span, :] = rows
+            kt_ref[:, span] = rows.T[:head, :]
+            dkv_ref[span, :] = jnp.zeros((PART, 2 * head), f32)
+
+        for_slots(sources, table_ref, turn)
 
     base = base_ref[tile]
-    steps, begin, position, parts = tile_ranges(base)
-    dq_ref[...] = jnp.zeros(dq_ref.shape, f32)
+    steps, begin, position, parts = tile_ranges(base, origin, buffers > 2)
+    dq_ref[...] = jnp.zeros(dq_ref.shape, f32) if first else dq_in_ref[...]
 
     def block(offset, size, mask):
         span = pl.ds(pl.multiple_of(offset, size), size)
@@ -310,7 +372,7 @@
             probs = jnp.where(mask, probs, 0.0)
         prob_grad = dot(kv_ref[span, head:], dot_ref[0])
         score_grad = (probs * (prob_grad - delta_ref[0])).astype(bf16)
-        dq_ref[0] += dot(kt_ref[:, span], score_grad)
+        dq_ref[0] += dot(kt_ref[:, span], score_grad) * scale
         dkv_ref[span, :head] += dot(score_grad, q_ref[0])
         dkv_ref[span, head:] += dot(probs.astype(bf16), do_ref[0])
 
@@ -324,49 +386,53 @@
 
     lax.fori_loop(0, steps, step, 0)
     lax.fori_loop(0, parts, part, 0)
-    dq_ref[...] = dq_ref[...] * scale
 
     @pl.when(tile == pl.num_programs(0) - 1)
     def _():
-        def finish(i, carry):
-            span = pl.ds(pl.multiple_of(i * FULL, FULL), FULL)
-            dkv_ref[span, :head] = dkv_ref[span, :head] * scale
-            return carry
-
-        lax.fori_loop(0, total_keys // FULL, finish, 0)
-
-
-def attend_back_call(bases, kv, qt, q, grad_t, grad, lse, delta):
+        lane = lax.broadcasted_iota(jnp.int32, (PART, 2 * head), 1)
+        both = jnp.where(lane < head, scale, 1.0)
+
+        def finish(ref, row, span):
+            ref[row : row + PART, :] = (dkv_ref[span, :] * both).astype(ref.dtype)
+
+        for_slots(outs, table_ref, finish)
+
+
+def attend_back_call(origin, sources, kinds, table, bases, qt, q, grad_t, grad, lse, delta, dq=None):
     tiles, head, width = qt.shape
-    total_keys, pair = kv.shape
-    one = lambda shape: pl.BlockSpec((1,) + shape, lambda i, b: (i, 0, 0))
+    total_keys = sum(x.shape[0] for x in sources)
+    pair = sources[0].shape[1]
+    one = lambda shape: pl.BlockSpec((1,) + shape, lambda i, b, t: (i, 0, 0))
+    keep = lambda x: pl.BlockSpec(x.shape, lambda i, b, t: (0, 0))
+    extra = () if dq is None else (dq,)
     return pl.pallas_call(
-        attend_back_kernel,
+        functools.partial(attend_back_kernel, origin, len(sources), dq is None),
         grid_spec=pltpu.PrefetchScalarGridSpec(
-            num_scalar_prefetch=1,
+            num_scalar_prefetch=2,
             grid=(tiles,),
-            in_specs=[
-                pl.BlockSpec((total_keys, pair), lambda i, b: (0, 0)),
+            in_specs=[keep(x) for x in sources]
+            + [
                 one((head, width)),
                 one((width, head)),
                 one((head, width)),
                 one((width, head)),
                 one((1, width)),
                 one((1, width)),
+            ]
+            + [one((head, width)) for _ in extra],
+            out_specs=[one((head, width))] + [keep(x) for x in sources],
+            scratch_shapes=[
+                pltpu.VMEM((total_keys, pair), bf16),
+                pltpu.VMEM((head, total_keys), bf16),
+                pltpu.VMEM((total_keys, pair), f32),
             ],
-            out_specs=[
-                one((head, width)),
-                pl.BlockSpec((total_keys, pair), lambda i, b: (0, 0)),
-            ],
-            scratch_shapes=[pltpu.VMEM((head, total_keys), bf16)],
         ),
-        out_shape=[
-            jax.ShapeDtypeStruct((tiles, head, width), f32),
-            jax.ShapeDtypeStruct((total_keys, pair), f32),
-        ],
+        out_shape=[jax.ShapeDtypeStruct((tiles, head, width), f32)]
+        + [jax.ShapeDtypeStruct(x.shape, kind) for x, kind in zip(sources, kinds)],
         compiler_params=params(),
+        cost_estimate=cost(80),
         name="attend_back",
-    )(bases, kv, qt, q, grad_t, grad, lse, delta)
+    )(bases, table, *sources, qt, q, grad_t, grad, lse, delta, *extra)
 
 
 def place(index, pieces, expert):
@@ -377,14 +443,18 @@
 
 
 def middle_kernel(
+    shard_ref,
     tokens_ref,
     grad_ref,
     index_ref,
     gate_ref,
     attended_ref,
-    output_weight_ref,
-    up_weight_ref,
-    down_weight_ref,
+    output_own_ref,
+    output_other_ref,
+    up_own_ref,
+    up_other_ref,
+    down_own_ref,
+    down_other_ref,
     gain_ref,
     shift_ref,
     up_bias_ref,
@@ -395,13 +465,15 @@
     grad_rows_ref,
     delta_ref,
     logit_grad_ref,
-    output_weight_grad_ref,
-    up_weight_grad_ref,
-    down_weight_grad_ref,
+    keep_ref,
+    send_ref,
     gain_grad_ref,
     shift_grad_ref,
     up_bias_grad_ref,
     down_bias_grad_ref,
+    output_weight_ref,
+    up_weight_ref,
+    down_weight_ref,
     spread_ref,
     chosen_ref,
     dwo_ref,
@@ -416,6 +488,10 @@
 
     @pl.when(step == 0)
     def _():
+        shard = shard_ref[0]
+        join_rows(shard, output_own_ref, output_other_ref, output_weight_ref)
+        join_rows(shard, up_own_ref, up_other_ref, up_weight_ref)
+        join_rows(shard, down_own_ref, down_other_ref, down_weight_ref)
         for ref in (
             dwo_ref,
             dup_ref,
@@ -498,57 +574,65 @@
 
     @pl.when(step == pl.num_programs(0) - 1)
     def _():
-        output_weight_grad_ref[...] = dwo_ref[...].astype(bf16)
-        up_weight_grad_ref[...] = dup_ref[...].astype(bf16)
-        down_weight_grad_ref[...] = ddown_ref[...].astype(bf16)
+        for target, part in ((keep_ref, shard_ref[0]), (send_ref, 1 - shard_ref[0])):
+            place_of = 0
+            for ref in (dwo_ref, ddown_ref, dup_ref):
+                half = ref.shape[0] // 2
+                rows = pl.ds(pl.multiple_of(part * half, half), half)
+                for column in range(0, ref.shape[1], target.shape[1]):
+                    span = slice(column, column + target.shape[1])
+                    target[place_of : place_of + half, :] = ref[rows, span].astype(bf16)
+                    place_of += half
 
 
 def middle_call(
-    tokens, grad, index, gate, attended, output_weight, up_weight, down_weight,
-    gain, shift, up_bias, down_bias, padded,
+    shard, tokens, grad, index, gate, attended, weights, gain, shift, up_bias, down_bias, padded
 ):
     count, width = tokens.shape
     topk = index.shape[0]
     tiles, head, wide = attended.shape
     per = TILE // ROWS
-    hidden = up_weight.shape[1]
-    spread = output_weight.shape[0]
-    rows = pl.BlockSpec((TILE, width), lambda i: (i, 0))
-    columns = lambda n: pl.BlockSpec((n, TILE), lambda i: (0, i))
-    tile = lambda shape: pl.BlockSpec((per,) + shape, lambda i: (i, 0, 0))
+    spread = 2 * weights[0].shape[0]
+    hidden = weights[2].shape[1]
+    sent = spread // 2 + hidden
+    keep = lambda shape: pl.BlockSpec(shape, lambda i, s: tuple(0 for _ in shape))
+    rows = pl.BlockSpec((TILE, width), lambda i, s: (i, 0))
+    columns = lambda n: pl.BlockSpec((n, TILE), lambda i, s: (0, i))
+    tile = lambda shape: pl.BlockSpec((per,) + shape, lambda i, s: (i, 0, 0))
     shape = jax.ShapeDtypeStruct
     return pl.pallas_call(
         middle_kernel,
-        grid=(count // TILE,),
-        in_specs=[
-            rows,
-            rows,
-            columns(topk),
-            columns(topk),
-            tile((head, wide)),
-            whole(output_weight.shape),
-            whole(up_weight.shape),
-            whole(down_weight.shape),
-            whole((width, 1)),
-            whole((width, 1)),
-            whole((hidden, 1)),
-            whole((width, 1)),
-        ],
-        out_specs=[
-            rows,
-            columns(width),
-            tile((head, wide)),
-            tile((wide, head)),
-            tile((1, wide)),
-            columns(padded),
-            whole(output_weight.shape),
-            whole(up_weight.shape),
-            whole(down_weight.shape),
-            whole((width, 128)),
-            whole((width, 128)),
-            whole((hidden, 128)),
-            whole((1, width)),
-        ],
+        grid_spec=pltpu.PrefetchScalarGridSpec(
+            num_scalar_prefetch=1,
+            grid=(count // TILE,),
+            in_specs=[rows, rows, columns(topk), columns(topk), tile((head, wide))]
+            + [keep(w.shape) for w in weights]
+            + [keep((width, 1)), keep((width, 1)), keep((hidden, 1)), keep((width, 1))],
+            out_specs=[
+                rows,
+                columns(width),
+                tile((head, wide)),
+                tile((wide, head)),
+                tile((1, wide)),
+                columns(padded),
+                keep((sent, width)),
+                keep((sent, width)),
+                keep((width, 128)),
+                keep((width, 128)),
+                keep((hidden, 128)),
+                keep((1, width)),
+            ],
+            scratch_shapes=[
+                pltpu.VMEM((spread, width), bf16),
+                pltpu.VMEM((width, hidden), bf16),
+                pltpu.VMEM((hidden, width), bf16),
+                pltpu.VMEM((spread, TILE), bf16),
+                pltpu.VMEM((spread, TILE), f32),
+                pltpu.VMEM((spread, width), f32),
+                pltpu.VMEM((width, hidden), f32),
+                pltpu.VMEM((hidden, width), f32),
+            ],
+        ),
         out_shape=[
             shape((count, width), bf16),
             shape((width, count), f32),
@@ -556,37 +640,33 @@
             shape((tiles, wide, head), bf16),
             shape((tiles, 1, wide), f32),
             shape((padded, count), bf16),
-            shape(output_weight.shape, bf16),
-            shape(up_weight.shape, bf16),
-            shape(down_weight.shape, bf16),
+            shape((sent, width), bf16),
+            shape((sent, width), bf16),
             shape((width, 128), f32),
             shape((width, 128), f32),
             shape((hidden, 128), f32),
             shape((1, width), f32),
         ],
-        scratch_shapes=[
-            pltpu.VMEM((spread, TILE), bf16),
-            pltpu.VMEM((spread, TILE), f32),
-            pltpu.VMEM(output_weight.shape, f32),
-            pltpu.VMEM(up_weight.shape, f32),
-            pltpu.VMEM(down_weight.shape, f32),
-        ],
         compiler_params=params(),
+        cost_estimate=cost(44),
         name="middle",
-    )(tokens, grad, index, gate, attended, output_weight, up_weight, down_weight,
-      gain, shift, up_bias, down_bias)
+    )(shard, tokens, grad, index, gate, attended, *weights, gain, shift, up_bias, down_bias)
 
 
 def query_back_kernel(
+    place_ref,
     first_ref,
     index_ref,
     dq_ref,
-    query_weight_ref,
+    own_ref,
+    other_ref,
     logit_grad_ref,
     router_ref,
     partial_ref,
-    query_weight_grad_ref,
+    keep_ref,
+    send_ref,
     router_grad_ref,
+    query_weight_ref,
     placed_ref,
     dwq_ref,
     dr_ref,
@@ -598,6 +678,7 @@
 
     @pl.when(step == 0)
     def _():
+        join_rows(place_ref[0], own_ref, other_ref, query_weight_ref)
         dwq_ref[...] = jnp.zeros(dwq_ref.shape, f32)
         dr_ref[...] = jnp.zeros(dr_ref.shape, f32)
 
@@ -618,42 +699,56 @@
 
     @pl.when(step == pl.num_programs(0) - 1)
     def _():
-        query_weight_grad_ref[...] = dwq_ref[...].astype(bf16)
         router_grad_ref[...] = dr_ref[...]
-
-
-def query_back_call(first, index, dq, query_weight, logit_grad, router):
+        size = keep_ref.shape[1]
+        for target, core in ((keep_ref, place_ref[1]), (send_ref, 1 - place_ref[1])):
+            for half in range(2):
+                rows = pl.ds(pl.multiple_of((2 * half + core) * size, size), size)
+                target[half] = dwq_ref[rows, :].astype(bf16)
+
+
+def query_back_call(place_of, first, index, dq, own, other, logit_grad, router):
     width, count = first.shape
     topk = index.shape[0]
     tiles, head, wide = dq.shape
     padded = router.shape[1]
-    columns = lambda n: pl.BlockSpec((n, TILE), lambda i: (0, i))
+    spread = own.shape[1]
+    keep = lambda shape: pl.BlockSpec(shape, lambda i, s: tuple(0 for _ in shape))
+    columns = lambda n: pl.BlockSpec((n, TILE), lambda i, s: (0, i))
     shape = jax.ShapeDtypeStruct
+    quarters = (2, width // 4, spread)
     return pl.pallas_call(
         query_back_kernel,
-        grid=(count // TILE,),
-        in_specs=[
-            columns(width),
-            columns(topk),
-            pl.BlockSpec((TILE // ROWS, head, wide), lambda i: (i, 0, 0)),
-            whole(query_weight.shape),
-            columns(padded),
-            whole(router.shape),
-        ],
-        out_specs=[columns(width), whole(query_weight.shape), whole(router.shape)],
+        grid_spec=pltpu.PrefetchScalarGridSpec(
+            num_scalar_prefetch=1,
+            grid=(count // TILE,),
+            in_specs=[
+                columns(width),
+                columns(topk),
+                pl.BlockSpec((TILE // ROWS, head, wide), lambda i, s: (i, 0, 0)),
+                keep(own.shape),
+                keep(other.shape),
+                columns(padded),
+                keep(router.shape),
+            ],
+            out_specs=[columns(width), keep(quarters), keep(quarters), keep(router.shape)],
+            scratch_shapes=[
+                pltpu.VMEM((width, spread), bf16),
+                pltpu.VMEM((spread, TILE), bf16),
+                pltpu.VMEM((width, spread), f32),
+                pltpu.VMEM(router.shape, f32),
+            ],
+        ),
         out_shape=[
             shape((width, count), f32),
-            shape(query_weight.shape, bf16),
+            shape(quarters, bf16),
+            shape(quarters, bf16),
             shape(router.shape, f32),
         ],
-        scratch_shapes=[
-            pltpu.VMEM((query_weight.shape[1], TILE), bf16),
-            pltpu.VMEM(query_weight.shape, f32),
-            pltpu.VMEM(router.shape, f32),
-        ],
         compiler_params=params(),
+        cost_estimate=cost(10),
         name="query_back",
-    )(first, index, dq, query_weight, logit_grad, router)
+    )(place_of, first, index, dq, own, other, logit_grad, router)
 
 
 def first_back_kernel(
@@ -712,22 +807,142 @@
             shape((width, 128), f32),
         ],
         compiler_params=params(),
+        cost_estimate=cost(7),
         name="first_back",
     )(tokens, first, partial, middle_grad, dkv, kv_weight, gain)
 
 
-def join(value):
-    count = lax.axis_size("shard")
-    if count != 2:
-        return lax.all_gather(value, "shard", axis=0, tiled=True)
-    other = lax.ppermute(value, "shard", [(0, 1), (1, 0)])
+def after(value, *others):
+    return lax.optimization_barrier((value,) + others)[0]
+
+
+def other_half(value):
+    return lax.ppermute(value, "shard", [(0, 1), (1, 0)])
+
+
+def join(value, other):
     low = lax.axis_index("shard") == 0
     return jnp.concatenate([jnp.where(low, value, other), jnp.where(low, other, value)], axis=0)
 
 
-def reduce_parameter(grad):
-    part = lax.psum_scatter(grad.astype(bf16), "shard", scatter_dimension=0, tiled=True)
-    return lax.psum(part, "ctx").astype(f32)
+def swap(value, mask):
+    count = lax.axis_size("ctx")
+    return lax.ppermute(value, "ctx", [(i, i ^ mask) for i in range(count)])
+
+
+def bit_masks():
+    count = lax.axis_size("ctx")
+    return [1 << k for k in reversed(range(count.bit_length() - 1))]
+
+
+def gather_keys(mine):
+    masks = bit_masks()
+    held = mine
+    for mask in masks[:-1]:
+        held = jnp.concatenate([held, swap(held, mask)], axis=1)
+    return held, swap(held, masks[-1])
+
+
+def scatter_keys(total):
+    for mask in reversed(bit_masks()[:-1]):
+        half = total.shape[1] // 2
+        total = total[:, :half] + swap(total[:, half:].astype(bf16), mask).astype(f32)
+    return total
+
+
+def add_low(a, b):
+    return (a.astype(f32) + b.astype(f32)).astype(bf16)
+
+
+def halves(value, bit):
+    half = value.shape[0] // 2
+    keep = lax.dynamic_slice_in_dim(value, bit * half, half, 0)
+    send = lax.dynamic_slice_in_dim(value, (1 - bit) * half, half, 0)
+    return keep, send
+
+
+def reduce_quarters(keep, send, halvings):
+    me = lax.axis_index("ctx")
+    bit = lambda mask: (me // mask) % 2
+    _, rows, width = keep.shape
+    total = add_low(keep, swap(send, 1)).reshape(2 * rows, width)
+    keep, send = halves(total, lax.axis_index("shard"))
+    total = add_low(keep, other_half(send))
+    masks = bit_masks()[:-1][::-1]
+    for mask in masks[:halvings]:
+        keep, send = halves(total, bit(mask))
+        total = add_low(keep, swap(send, mask))
+    for mask in masks[halvings:]:
+        total = add_low(total, swap(total, mask))
+    for mask in masks[:halvings][::-1] + [1]:
+        other = swap(total, mask)
+        low = bit(mask) == 0
+        total = jnp.concatenate(
+            [jnp.where(low, total, other), jnp.where(low, other, total)], axis=0
+        )
+    return total.astype(f32)
+
+
+def home_plan(count, block):
+    half = count // 2
+    if block != 4 * PART or block * half != PROMPT or block != CLEN or half % 2:
+        return None
+    sends = [None] * count
+    hops = [[], [], []]
+    for a in range(half // 2):
+        b = half - 1 - a
+        p, q = a + half, b + half
+        sends[a], sends[b] = (0, 1, 2, 3), (2, 3, 0, 1)
+        sends[p] = sends[q] = (0, 3, 1, 2)
+        hops[0] += [(a, b), (b, a)]
+        hops[1] += [(a, p), (p, a), (b, q), (q, b)]
+        hops[2] += [(a, q), (b, p), (p, a), (q, b)]
+    places = [[(i, sends[i][0]), (i, sends[i][1]), None, None] for i in range(count)]
+    for k, hop in enumerate(hops):
+        for source, target in hop:
+            places[target][k + 1] = (source, sends[source][k + 1])
+    return sends, hops, places
+
+
+def exchange(value, plan, extra=None):
+    sends, hops, _ = plan
+    me = lax.axis_index("ctx")
+    rows, width = value.shape
+    size = rows // 4
+    starts = jnp.array(sends, jnp.int32)[me] * size
+    pieces = [lax.dynamic_slice_in_dim(value, starts[k], size, 0) for k in range(4)]
+    if extra is not None:
+        count = extra.shape[0]
+        tail = count * size // width
+        blank = jnp.zeros((-tail % 16, width), value.dtype)
+        for k in range(4):
+            part = lax.dynamic_slice_in_dim(extra, starts[k], size, 1).reshape(tail, width)
+            pieces[k] = jnp.concatenate([pieces[k], part, blank], axis=0)
+    got = [lax.ppermute(pieces[k + 1], "ctx", hops[k]) for k in range(3)]
+    got[0] = jnp.where(me < lax.axis_size("ctx") // 2, got[0], pieces[1])
+    got = [pieces[0]] + got
+    main = jnp.concatenate([x[:size] for x in got], axis=0)
+    if extra is None:
+        return main
+    parts = [x[size : size + tail].reshape(count, size) for x in got]
+    return main, jnp.concatenate(parts, axis=1)
+
+
+def exchange_back(value, plan):
+    sends, hops, _ = plan
+    me = lax.axis_index("ctx")
+    size = value.shape[0] // 4
+    pieces = [value[k * size : (k + 1) * size] for k in range(4)]
+    got = [
+        lax.ppermute(pieces[k + 1], "ctx", [(t, s) for s, t in hops[k]]) for k in range(3)
+    ]
+    got[0] = jnp.where(me < lax.axis_size("ctx") // 2, got[0], pieces[1])
+    held = jnp.concatenate([pieces[0]] + got, axis=0)
+    order = [[send.index(k) for k in range(4)] for send in sends]
+    starts = jnp.array(order, jnp.int32)[me] * size
+    return jnp.concatenate(
+        [lax.dynamic_slice_in_dim(held, starts[k], size, 0) for k in range(4)], axis=0
+    )
 
 
 def per_device(
@@ -749,66 +964,146 @@
     out_grad,
 ):
     groups, block, width = tokens.shape
-    assert groups == 1
-    topk = expert_index.shape[-1]
+    assert groups == 1 and lax.axis_size("shard") == 2
+    count = lax.axis_size("ctx")
+    me = lax.axis_index("ctx")
+    shard = lax.axis_index("shard").astype(jnp.int32)[None]
     experts = router_weight.shape[1]
     head = key_weight.shape[1]
+    pair = 2 * head
     padded = 32
+    plan = home_plan(count, block)
+    flat = tokens[0]
+    index = expert_index[0].T
+    if plan:
+        flat, index = exchange(flat, plan, index.astype(bf16))
+        index = index.astype(jnp.int32)
+
     spare = jnp.zeros((key_weight.shape[0], padded - experts), bf16)
     vectors = [first_gain, first_shift, second_gain, second_shift, down_bias]
+    half_width = width // 2
     small = jnp.concatenate(
-        [key_weight, value_weight, router_weight, spare] + [v[:, None] for v in vectors], axis=1
-    )
-    small = join(small)
-    kv_weight = small[:, : 2 * head]
-    router = small[:, 2 * head : 2 * head + padded]
-    columns = [
-        small[:, 2 * head + padded + i : 2 * head + padded + i + 1].astype(f32)
-        for i in range(len(vectors))
-    ]
+        [key_weight, value_weight, router_weight, spare]
+        + [v[:, None] for v in vectors]
+        + [up_bias.reshape(half_width, -1)],
+        axis=1,
+    )
+    small = join(small, other_half(small))
+    query_other = other_half(after(query_weight, small))
+    kv_weight = small[:, :pair]
+    router = small[:, pair : pair + padded]
+    at = pair + padded
+    columns = [small[:, at + i : at + i + 1].astype(f32) for i in range(len(vectors))]
     gain_one, shift_one, gain_two, shift_two, down_bias_all = columns
-    query_all = join(query_weight)
-    output_all = join(output_weight)
-    up_all = join(up_weight)
-    down_all = join(down_weight)
-    up_bias_all = join(up_bias).astype(f32)[:, None]
-
-    flat = tokens[0]
+    end = at + len(vectors)
+    up_bias_all = small[:, end:].reshape(-1, 1).astype(f32)
+    first, kv = first_call(flat, gain_one, shift_one, kv_weight)
+
+    if plan:
+        _, _, places = plan
+        where = [[source * 4 + quarter for source, quarter in row] for row in places]
+        low_slot = [next(k for k in range(4) if row[k] < HALF // PART) for row in where]
+        high_slot = [
+            next(k for k in range(4) if HALF // PART <= row[k] < PROMPT // PART) for row in where
+        ]
+        own_slot = [2 if i < count // 2 else 0 for i in range(count)]
+        low_at = [row[k] for row, k in zip(where, low_slot)]
+        high_at = [row[k] - HALF // PART for row, k in zip(where, high_slot)]
+        own_at = [[row[k] % 4, row[k + 1] % 4] for row, k in zip(where, own_slot)]
+        masks = bit_masks()
+        slots = [sum(m for k, m in enumerate(masks) if j >> k & 1) for j in range(count)]
+        low_table = [[low_at[i ^ m] for m in slots] for i in range(count)]
+        high_table = [
+            [high_at[i ^ m] for m in slots]
+            + [HALF // PART + x for x in own_at[i] + own_at[i ^ (count // 2)]]
+            for i in range(count)
+        ]
+        pick = lambda table: jnp.array(table, jnp.int32)[me]
+        bases = pick([[x * PART + r for x in row for r in range(0, PART, ROWS)] for row in where])
+        low_table, high_table = pick(low_table), pick(high_table)
+        low_start, high_start, own_start = (
+            pick(x) * PART for x in (low_slot, high_slot, own_slot)
+        )
+        take = lambda start, rows: lax.dynamic_slice_in_dim(kv, start, rows, 0)
+        near, far = gather_keys(jnp.stack([take(low_start, PART), take(high_start, PART)]))
+        own = take(own_start, 2 * PART)
+        partner = swap(own, count // 2)
+        low_keys = (near[0], far[0])
+        high_keys = (near[1], far[1], own, partner)
+    else:
+        base = me * block
+        bases = base + jnp.arange(block // ROWS, dtype=jnp.int32) * ROWS
+        gathered = lax.all_gather(kv, "ctx", axis=0, tiled=True)
+        segment = jnp.maximum(base, PROMPT) // CLEN * CLEN
+        own = lax.dynamic_slice_in_dim(gathered, segment, CLEN, 0)
+        quarter = HALF // 2
+        low_keys = (gathered[:quarter], gathered[quarter:HALF])
+        high_keys = (
+            gathered[HALF : HALF + quarter], gathered[HALF + quarter : PROMPT],
+            own[: CLEN // 2], own[CLEN // 2 :],
+        )
+        low_table = jnp.arange(HALF // PART, dtype=jnp.int32)
+        high_table = jnp.arange((HALF + CLEN) // PART, dtype=jnp.int32)
+
+    qt, q, gate = query_call(shard, first, query_weight, query_other, router, index, head)
+    split = output_weight.shape[0]
+    stacked = jnp.concatenate([output_weight, down_weight], axis=0)
+    stacked_other = other_half(after(stacked, query_other))
+    up_other = other_half(after(up_weight, query_other))
+    weights = (
+        output_weight, stacked_other[:split], up_weight, up_other, down_weight, stacked_other[split:]
+    )
     grad = out_grad[0]
-    index = expert_index[0].T
-    first, kv = first_call(flat, gain_one, shift_one, kv_weight)
-    gathered = lax.all_gather(kv, "ctx", axis=0, tiled=True)
-    qt, q, gate = query_call(first, query_all, router, index, head)
-    base = lax.axis_index("ctx") * block
-    bases = base + jnp.arange(block // ROWS, dtype=jnp.int32) * ROWS
-    segment = jnp.maximum(base, PROMPT) // CLEN * CLEN
-    keys = jnp.concatenate(
-        [gathered[:PROMPT], lax.dynamic_slice_in_dim(gathered, segment, CLEN, 0)], axis=0
-    )
-    attended, lse = attend_call(bases, keys, qt)
+    if plan:
+        grad = exchange(after(grad, near, far, partner), plan)
+    state = attend_call(0, low_keys, low_table, bases, qt)
+    attended, lse = attend_call(HALF, high_keys, high_table, bases, qt, state, last=True)
     (
-        layer_out, middle_grad, grad_t, grad_rows, delta, logit_grad,
-        output_weight_grad, up_weight_grad, down_weight_grad,
+        layer_out, middle_grad, grad_t, grad_rows, delta, logit_grad, keep, send,
         second_gain_grad, second_shift_grad, up_bias_grad, down_bias_grad,
     ) = middle_call(
-        flat, grad, index, gate, attended, output_all, up_all, down_all,
+        shard, flat, grad, index, gate, attended, weights,
         gain_two, shift_two, up_bias_all, down_bias_all, padded,
     )
-    output_weight_grad = reduce_parameter(output_weight_grad)
-    up_weight_grad = reduce_parameter(up_weight_grad)
-    down_weight_grad = reduce_parameter(down_weight_grad)
-    dq, dkeys = attend_back_call(bases, keys, qt, q, grad_t, grad_rows, lse, delta)
-    dall = jnp.concatenate(
-        [dkeys[:PROMPT], jnp.zeros((gathered.shape[0] - PROMPT, 2 * head), f32)], axis=0
-    )
-    dall = lax.dynamic_update_slice_in_dim(
-        dall, jnp.where(base >= PROMPT, dkeys[PROMPT:], 0.0), segment, 0
-    )
-    dkv = lax.psum_scatter(dall.astype(bf16), "ctx", scatter_dimension=0, tiled=True)
-    partial, query_weight_grad, router_grad = query_back_call(
-        first, index, dq, query_all, logit_grad, router
-    )
-    query_weight_grad = reduce_parameter(query_weight_grad)
+
+    arrived = other_half(send)
+    kinds = (f32, bf16) if plan else (bf16, bf16)
+    shared = (qt, q, grad_t, grad_rows, lse, delta)
+    dq, *high_grads = attend_back_call(
+        HALF, high_keys, kinds + (f32, bf16), high_table, bases, *shared
+    )
+    keep, arrived, dq, *high_grads = lax.optimization_barrier((keep, arrived, dq, *high_grads))
+    early = add_low(keep, arrived)
+    early_sum = lax.psum(early, "ctx")
+    if plan:
+        layer_out = exchange_back(after(layer_out, arrived), plan)
+        own_grad = high_grads[2] + swap(high_grads[3], count // 2).astype(f32)
+        high_grad = high_grads[0] + swap(high_grads[1], 1).astype(f32)
+    dq, *low_grads = attend_back_call(
+        0, low_keys, kinds, low_table, after(bases, early), *shared, dq=dq
+    )
+    core = me % 2
+    partial, keep, send, router_grad = query_back_call(
+        jnp.stack([shard[0], core]), first, index, dq, query_weight, query_other, logit_grad, router
+    )
+    if plan:
+        low_grad = low_grads[0] + swap(low_grads[1], 1).astype(f32)
+        low_high = scatter_keys(jnp.stack([low_grad, high_grad]))
+        dkv = jnp.zeros((block, pair), bf16)
+        pieces = ((own_grad, own_start), (low_high[1], high_start), (low_high[0], low_start))
+        for piece, start in pieces:
+            dkv = lax.dynamic_update_slice_in_dim(dkv, piece.astype(bf16), start, 0)
+    else:
+        rest = count * block - PROMPT
+        dall = jnp.concatenate(
+            [x.astype(bf16) for x in low_grads + high_grads[:2]] + [jnp.zeros((rest, pair), bf16)]
+        )
+        own_grad = jnp.concatenate([x.astype(bf16) for x in high_grads[2:]])
+        own_grad = jnp.where(base >= PROMPT, own_grad, jnp.zeros_like(own_grad))
+        dall = lax.dynamic_update_slice_in_dim(dall, own_grad, segment, 0)
+        dkv = lax.psum_scatter(dall, "ctx", scatter_dimension=0, tiled=True)
+
+    query_weight_grad = reduce_quarters(keep, send, 1)
     tokens_grad, kv_weight_grad, first_gain_grad, first_shift_grad = first_back_call(
         flat, first, partial, middle_grad, dkv, kv_weight, gain_one
     )
@@ -820,25 +1115,37 @@
         down_bias_grad[0],
     ]
     small_grad = jnp.concatenate(
-        [kv_weight_grad, router_grad] + [v[:, None] for v in vector_grads], axis=1
-    )
-    small_grad = reduce_parameter(small_grad)
-    up_bias_grad = reduce_parameter(jnp.sum(up_bias_grad, axis=1))
-    at = 2 * head + padded
+        [kv_weight_grad, router_grad]
+        + [v[:, None] for v in vector_grads]
+        + [jnp.sum(up_bias_grad, axis=1).reshape(width, -1)],
+        axis=1,
+    ).astype(bf16)
+    quarters = small_grad.reshape(2, 2, width // 4, -1)
+    keep = lax.dynamic_index_in_dim(quarters, core, 1, keepdims=False)
+    send = lax.dynamic_index_in_dim(quarters, 1 - core, 1, keepdims=False)
+    small_grad = reduce_quarters(keep, send, 0)
+    if plan:
+        tokens_grad = exchange_back(tokens_grad, plan)
+    early_sum = early_sum.astype(f32)
+    cuts = [split, split + down_weight.shape[0]]
+    output_weight_grad, down_weight_grad, up_weight_grad = jnp.split(early_sum, cuts)
+    up_weight_grad = jnp.concatenate(
+        jnp.split(up_weight_grad, up_weight_grad.shape[0] // half_width), axis=1
+    )
     return (
         layer_out[None],
         tokens_grad[None],
         small_grad[:, at],
         small_grad[:, at + 1],
-        small_grad[:, 2 * head : 2 * head + experts],
+        small_grad[:, pair : pair + experts],
         query_weight_grad,
         small_grad[:, :head],
-        small_grad[:, head : 2 * head],
+        small_grad[:, head:pair],
         output_weight_grad,
         small_grad[:, at + 2],
         small_grad[:, at + 3],
         up_weight_grad,
-        up_bias_grad,
+        small_grad[:, end:].reshape(-1),
         down_weight_grad,
         small_grad[:, at + 4],
     )

time: 837 us -> 578 us (0.69); the launches traced: 836 us -> 569 us
  waiting for transfers between devices: 593 us -> 96.1 us
  Pallas kernels: 118 us -> 309 us
  starting transfers between devices: 9.21 us -> 59.4 us
  blocking collectives: 37.8 us -> 0 us
  between operations: 15.1 us -> 33.1 us
    reduce_scatter x6 -> x0, waiting for transfers between devices: 440 us -> none  [the longest x1 312 us: per_device(): lax.psum_scatter(dall.astype(bf16), 'ctx', scatter_dimension=0, tiled=True)]
    pallas_call x5 -> x7, Pallas kernels: 107 us -> 298 us  [the longest x2 164 us: attend_back_call(): pl.pallas_call(functools.partial(attend_back_kernel, origin, len(sources)...]
    psum x1, waiting for transfers between devices: 73.9 us -> 0.01 us  [per_device(): early_sum = lax.psum(early, 'ctx')]
    ppermute x6 -> x41, starting transfers between devices: 8.89 us -> 59.4 us  [the longest x22 21 us: swap(): return lax.ppermute(value, 'ctx', [(i, i ^ mask) for i in range(count)])]
    psum x1 -> x0, blocking collectives: 32.8 us -> none  [reduce_parameter(): return lax.psum(part, 'ctx').astype(f32)]
    ppermute x6 -> x41, waiting for transfers between devices: 78.1 us -> 96.1 us  [the longest x22 67.5 us: swap(): return lax.ppermute(value, 'ctx', [(i, i ^ mask) for i in range(count)])]
    concatenate x3 -> x1, local copies, waits for them, and re-layouts: 9 us -> 0.08 us  [exchange(): pieces[k] = jnp.concatenate([pieces[k], part, blank], axis=0)]
  transfers between devices with their start and end apart: 14 -> 42, of which waited for: 9 -> 15; matrix products, arithmetic and copies ran while one was open for 2% -> 11% of each run, Pallas kernels for 3% -> 46%
where the time goes in v2:
time: 578 us; the launch traced here: 569 us
  Pallas kernels  309 us (53%)
  waiting for transfers between devices  96.1 us (17%)
  starting transfers between devices  59.4 us (10%)
  local copies, waits for them, and re-layouts  36.2 us (6%)
  other arithmetic  35.2 us (6%)
  between operations  33.1 us (6%)
    pallas_call x2, Pallas kernels, attend_back_call(): pl.pallas_call(functools.partial(attend_back_kernel, origin, len(sources)...  164 us
    pallas_call x2, Pallas kernels, attend_call(): pl.pallas_call(body, grid_spec=pltpu.PrefetchScalarGridSpec(num_scalar_pr...  67.7 us
    ppermute x22, waiting for transfers between devices, swap(): return lax.ppermute(value, 'ctx', [(i, i ^ mask) for i in range(count)])  67.5 us
    pallas_call x1, Pallas kernels, middle_call(): pl.pallas_call(middle_kernel, grid_spec=pltpu.PrefetchScalarGridSpec(num_...  44.9 us
    ppermute x22, starting transfers between devices, swap(): return lax.ppermute(value, 'ctx', [(i, i ^ mask) for i in range(count)])  21 us
    ppermute x6, waiting for transfers between devices, exchange(): got = [lax.ppermute(pieces[k + 1], 'ctx', hops[k]) for k in range(3)]  20.4 us
    ppermute x6, starting transfers between devices, exchange(): got = [lax.ppermute(pieces[k + 1], 'ctx', hops[k]) for k in range(3)]  18.1 us
    ppermute x6, starting transfers between devices, exchange_back(): lax.ppermute(pieces[k + 1], 'ctx', [(t, s) for s, t in hops[k]])  13.1 us
  transfers between devices with their start and end apart: 42, of which 15 were waited for; matrix products, arithmetic and copies ran while one was open for 11% of the time, Pallas kernels for 46%

profile of v2, /device:TPU:0, one launch (start us, length us, event | category | flops | bytes accessed | tf_op | source)
XLA Modules:
  0.0 568.9 jit_solution(6643538108784207919)
XLA Ops:
  17.2 2.3 dynamic-slice_bitcast_fusion.3
  20.5 5.3 collective-permute-start
  27.2 1.6 collective-permute-start.3
  31.9 1.3 pad_maximum_fusion.1
  33.2 1.4 broadcast_select_fusion.2
  34.6 5.2 collective-permute-start.2
  40.5 1.3 fusion.19
  41.8 15.2 %collective-permute-done.1 = bf16[272,512]{1,0:T(8,128)(2,1)S(1)} collective-permute-done((bf16[272,512]{1,0:T(8,128)(2,1)S(1)}, bf16[272,512]{1,0:T(8,128)(2,1)S(1)}, u32[]{:S(2)}, u32[]{:S(2)}) %collective-permute-start.1) | collective-permute-done | bytes 278560 | tf_op jit(solution)/shard_map/ppermute | solution.py:921
  57.0 5.1 collective-permute-done.2
  63.9 4.7 first_norm.1
  69.5 2.1 collective-permute-start.4
  72.9 3.7 collective-permute-done.4
  76.7 1.2 fusion.27.base_ref
  87.0 1.2 fusion.29.table_ref
  88.2 1.2 fusion.28.table_ref
  90.2 2.3 collective-permute-start.6
  93.2 1.2 reshape.182.up_bias_ref
  98.3 1.3 collective-permute-start.14
  99.7 5.1 collective-permute-done.6
  104.7 1.1 pad_maximum_fusion.4
  105.9 9.8 %queries.1 = (bf16[8,64,1024]{2,1,0:T(8,128)(2,1)}, bf16[8,1024,64]{2,1,0:T(8,128)(2,1)}, f32[8,1024]{1,0:T(8,128)}) custom-call(s32[1]{0:T(128)} %bitcast.shard_ref, bf16[512,1024]{1,0:T(8,128)(2,1)} %get-tuple-element.67.first_ref, bf16[256,1536]{1,0:T(8,128)(2,1)} %own_ref.3, bf16[256,1536]{1,0:T(8,128)(2,1)} %collective-permute-done.12.other_ref, ...), custom_call_target="tpu_custom_call" | custom-call | flops 11500000256 | tf_op jit(solution)/shard_map/queries/pallas_call | solution.py:156
  117.5 4.9 collective-permute-start.9
  122.5 2.6 collective-permute-start.11
  126.1 30.8 %attend.2 = (f32[8,80,1024]{2,1,0:T(8,128)}, f32[8,1,1024]{2,1,0:T(1,128)}) custom-call(s32[8]{0:T(128)} %fusion.27.base_ref, s32[16]{0:T(128)} %fusion.29.table_ref, bf16[2048,128]{1,0:T(8,128)(2,1)} %get-tuple-element.137.refs_0_, bf16[2048,128]{1,0:T(8,128)(2,1)} %get-tuple-element.135.refs_1_, bf16[8,64,1024]{2,1,0:T(8,128)(2,1)} %get-tuple-element.70.refs_2_.refs_4_), custom_call_target="tpu_custom_call" | custom-call | flops 37950001152 | tf_op jit(solution)/shard_map/attend/pallas_call | solution.py:312
  156.9 36.9 %attend.3 = (f32[8,64,1024]{2,1,0:T(8,128)}, f32[8,1,1024]{2,1,0:T(1,128)}) custom-call(s32[8]{0:T(128)} %fusion.27.base_ref, s32[20]{0:T(128)} %fusion.28.table_ref, bf16[2048,128]{1,0:T(8,128)(2,1)} %get-tuple-element.138.refs_0_, bf16[2048,128]{1,0:T(8,128)(2,1)} %get-tuple-element.136.refs_1_, bf16[512,128]{1,0:T(8,128)(2,1)} %copy-done.19, ...), custom_call_target="tpu_custom_call" | custom-call | flops 37950001152 | tf_op jit(solution)/shard_map/attend/pallas_call | solution.py:312
  193.9 2.3 slice.292.down_other_ref
  196.2 2.1 slice.291.output_other_ref
  199.3 2.1 pad_maximum_fusion.5.grad_ref
  201.3 44.9 %middle.1 = (bf16[1024,512]{1,0:T(8,128)(2,1)}, f32[512,1024]{1,0:T(8,128)}, bf16[8,64,1024]{2,1,0:T(8,128)(2,1)}, bf16[8,1024,64]{2,1,0:T(8,128)(2,1)}, f32[8,1...) custom-call(s32[1]{0:T(128)} %bitcast.shard_ref, ...), custom_call_target="tpu_custom_call" | custom-call | flops 50600001536 | tf_op jit(solution)/shard_map/middle/pallas_call | solution.py:603
  246.3 1.6 collective-permute-start.15
  247.9 87.5 %attend_back.2 = (f32[8,64,1024]{2,1,0:T(8,128)}, f32[2048,128]{1,0:T(8,128)}, bf16[2048,128]{1,0:T(8,128)(2,1)}, f32[512,128]{1,0:T(8,128)}, bf16[512,128]{1,0:T(8,128)(2,1)}) custom-call(s32[8]{0:T(128)} %fusion.27.base_ref, s32[20]{0:T(128)} %fusion.28.table_ref, bf16[2048,128]{1,0:T(8,128)(2,1)} %get-tuple-element.138.refs_0_, ...), custom_call_target="tpu_custom_call" | custom-call | flops 92000002048 | tf_op jit(solution)/shard_map/attend_back/pallas_call | solution.py:408
  335.4 1.6 reduce_sum.49
  340.2 4.2 add_convert_fusion
  344.4 76.9 %attend_back.3 = (f32[8,64,1024]{2,1,0:T(8,128)}, f32[2048,128]{1,0:T(8,128)}, bf16[2048,128]{1,0:T(8,128)(2,1)}) custom-call(s32[8]{0:T(128)} %fusion.27.base_ref, s32[16]{0:T(128)} %fusion.29.table_ref, bf16[2048,128]{1,0:T(8,128)(2,1)} %get-tuple-element.137.refs_0_, bf16[2048,128]{1,0:T(8,128)(2,1)} %get-tuple-element.135.refs_1_, ...), custom_call_target="tpu_custom_call" | custom-call | flops 92000002048 | tf_op jit(solution)/shard_map/attend_back/pallas_call | solution.py:408
  421.3 6.2 %collective-permute-start.20 = (bf16[2048,128]{1,0:T(8,128)(2,1)}, bf16[2048,128]{1,0:T(8,128)(2,1)S(1)}, u32[]{:S(2)}, u32[]{:S(2)}) collective-permute-start(bf16[2048,128]{1,0:T(8,128)(2,1)} %get-tuple-element.101), channel_id=1, source_target_pairs={{0,2},{2,0},{4,6},{6,4},{8,10},{10,8},{12,14},{14,12},{16,18},{18,... | collective-permute-start | bytes 1572872 | tf_op jit(solution)/shard_map/ppermute | solution.py:830
  427.6 3.7 collective-permute-start.16
  431.3 10.7 %query_back.1 = (f32[512,1024]{1,0:T(8,128)}, bf16[2,128,1536]{2,1,0:T(8,128)(2,1)}, bf16[2,128,1536]{2,1,0:T(8,128)(2,1)}, f32[512,32]{1,0:T(8,128)}) custom-call(s32[2]{0:T(128)} %pad_add_fusion.place_ref, bf16[512,1024]{1,0:T(8,128)(2,1)} %get-tuple-element.67.first_ref, s32[8,1024]{1,0:T(8,128)} %maximum_convert_fusion.2.index_ref, ...), custom_call_target="tpu_custom_call" | custom-call | flops 11500000256 | tf_op jit(solution)/shard_map/query_back/pallas_call | solution.py:720
  443.3 3.2 collective-permute-done.16
  446.7 2.9 collective-permute-start.18
  451.0 17.9 %collective-permute-done.22 = bf16[2,1024,128]{2,1,0:T(8,128)(2,1)S(1)} collective-permute-done((bf16[2,1024,128]{2,1,0:T(8,128)(2,1)S(1)}, bf16[2,1024,128]{2,1,0:T(8,128)(2,1)S(1)}, u32[]{:S(2)}, u32[]{:S(2)}) %collective-permute-start.22) | collective-permute-done | bytes 524320 | tf_op jit(solution)/shard_map/ppermute | solution.py:830
  469.9 6.1 %collective-permute-done.23 = bf16[2,512,128]{2,1,0:T(8,128)(2,1)S(1)} collective-permute-done((bf16[2,512,128]{2,1,0:T(8,128)(2,1)S(1)}, bf16[2,512,128]{2,1,0:T(8,128)(2,1)S(1)}, u32[]{:S(2)}, u32[]{:S(2)}) %collective-permute-start.23) | collective-permute-done | bytes 262176 | tf_op jit(solution)/shard_map/ppermute | solution.py:830
  476.8 2.1 collective-permute-done.35
  479.0 4.8 collective-permute-done.24
  484.6 6.6 %first_back.1 = (bf16[1024,512]{1,0:T(8,128)(2,1)}, f32[512,128]{1,0:T(8,128)}, f32[512,128]{1,0:T(8,128)}, f32[512,128]{1,0:T(8,128)}) custom-call(bf16[1024,512]{1,0:T(8,128)(2,1)} %pad_maximum_fusion.3.tokens_ref, bf16[512,1024]{1,0:T(8,128)(2,1)} %get-tuple-element.67.first_ref, f32[512,1024]{1,0:T(8,128)} %get-tuple-element.96.partial_ref, ...), custom_call_target="tpu_custom_call" | custom-call | flops 8049999872 | tf_op jit(solution)/shard_map/first_back/pallas_call | solution.py:790
  491.2 1.1 reduce_sum.45
  493.1 1.2 reduce_sum.46
  496.1 1.3 concatenate.107
  497.6 1.4 collective-permute-start.36
  500.0 4.9 collective-permute-done.36
  505.3 3.5 collective-permute-start.25
  509.7 1.5 fusion.31
  511.2 7.2 %collective-permute-done.30 = bf16[128,169]{0,1:T(8,128)(2,1)S(1)} collective-permute-done((bf16[128,169]{0,1:T(8,128)(2,1)S(1)}, bf16[128,169]{0,1:T(8,128)(2,1)S(1)}, u32[]{:S(2)}, u32[]{:S(2)}) %collective-permute-start.30) | collective-permute-done | bytes 43296 | tf_op jit(solution)/shard_map/ppermute | solution.py:830
  519.3 1.5 pad_maximum_fusion
  520.8 1.1 copy-done
  521.8 1.6 split.30
  523.4 1.4 split.25
  525.0 3.0 collective-permute-start.38
  527.9 7.2 %collective-permute-done.32 = bf16[128,169]{0,1:T(8,128)(2,1)S(1)} collective-permute-done((bf16[128,169]{0,1:T(8,128)(2,1)S(1)}, bf16[128,169]{0,1:T(8,128)(2,1)S(1)}, u32[]{:S(2)}, u32[]{:S(2)}) %collective-permute-start.32) | collective-permute-done | bytes 43296 | tf_op jit(solution)/shard_map/ppermute | solution.py:830
  536.0 2.9 collective-permute-start.27
  541.1 9.6 %collective-permute-done.38 = bf16[64,1536]{1,0:T(8,128)(2,1)} collective-permute-done((bf16[64,1536]{1,0:T(8,128)(2,1)S(1)}, bf16[64,1536]{1,0:T(8,128)(2,1)}, u32[]{:S(2)}, u32[]{:S(2)}) %collective-permute-start.38) | collective-permute-done | bytes 196640 | tf_op jit(solution)/shard_map/ppermute | solution.py:830
  551.7 1.1 collective-permute-start.39
  553.4 2.8 collective-permute-done.26
  556.3 1.1 collective-permute-done.39
  560.3 1.3 maximum_convert_fusion
  (232 shorter events, 43.3 us)
Async XLA Ops:
  7.2 18.7 %copy-start.25 = (bf16[256]{0:T(256)(128)(2,1)S(1)}, bf16[256]{0:T(256)(128)(2,1)}, u32[]{:S(2)}) copy-start(bf16[256]{0:T(256)(128)(2,1)} %param.28) | copy-start | bytes 1540
  7.2 18.8 %copy-start.26 = (bf16[256]{0:T(256)(128)(2,1)S(1)}, bf16[256]{0:T(256)(128)(2,1)}, u32[]{:S(2)}) copy-start(bf16[256]{0:T(256)(128)(2,1)} %param.29) | copy-start | bytes 1540
  7.2 18.9 %copy-start.27 = (bf16[256]{0:T(256)(128)(2,1)S(1)}, bf16[256]{0:T(256)(128)(2,1)}, u32[]{:S(2)}) copy-start(bf16[256]{0:T(256)(128)(2,1)} %param.35) | copy-start | bytes 1540
  7.2 19.0 %copy-start.28 = (bf16[256]{0:T(256)(128)(2,1)S(1)}, bf16[256]{0:T(256)(128)(2,1)}, u32[]{:S(2)}) copy-start(bf16[256]{0:T(256)(128)(2,1)} %param.36) | copy-start | bytes 1540
  7.2 19.1 %copy-start.29 = (bf16[256]{0:T(256)(128)(2,1)S(1)}, bf16[256]{0:T(256)(128)(2,1)}, u32[]{:S(2)}) copy-start(bf16[256]{0:T(256)(128)(2,1)} %param.40) | copy-start | bytes 1540
  7.2 19.2 %copy-start.20 = (bf16[256,64]{0,1:T(8,128)(2,1)S(1)}, bf16[256,64]{0,1:T(8,128)(2,1)}, u32[]{:S(2)}) copy-start(bf16[256,64]{0,1:T(8,128)(2,1)} %param.32) | copy-start | bytes 98308
  7.2 19.3 %copy-start.21 = (bf16[256,64]{0,1:T(8,128)(2,1)S(1)}, bf16[256,64]{0,1:T(8,128)(2,1)}, u32[]{:S(2)}) copy-start(bf16[256,64]{0,1:T(8,128)(2,1)} %param.33) | copy-start | bytes 98308
  7.3 19.4 %copy-start.22 = (bf16[256,24]{0,1:T(8,128)(2,1)S(1)}, bf16[256,24]{0,1:T(8,128)(2,1)}, u32[]{:S(2)}) copy-start(bf16[256,24]{0,1:T(8,128)(2,1)} %param.30) | copy-start | bytes 36868
  7.3 19.5 %copy-start.23 = (bf16[1024]{0:T(1024)(128)(2,1)S(1)}, bf16[1024]{0:T(1024)(128)(2,1)}, u32[]{:S(2)}) copy-start(bf16[1024]{0:T(1024)(128)(2,1)} %param.38) | copy-start | bytes 6148
  7.3 502.4 %all-reduce.2.cloned.1.call-start = ((), (), s32[]{:S(2)}) async-start(), calls=%async_computation | async-start | bytes 5767168 | tf_op jit(solution)/shard_map/psum | solution.py:1077
  17.2 13.4 %copy-start.32 = (s32[16]{0:T(128)S(1)}, s32[16]{0:T(128)}, u32[]{:S(2)}) copy-start(s32[16]{0:T(128)} %constant.118.clone) | copy-start | bytes 196
  17.2 14.7 %copy-start.4 = (bf16[1024,512]{1,0:T(8,128)(2,1)S(1)}, bf16[1024,512]{1,0:T(8,128)(2,1)}, u32[]{:S(2)}) copy-start(bf16[1024,512]{1,0:T(8,128)(2,1)} %down_own_ref.1) | copy-start | bytes 3145732
  20.5 12.6 %collective-permute-start = (bf16[272,512]{1,0:T(8,128)(2,1)}, bf16[272,512]{1,0:T(8,128)(2,1)}, u32[]{:S(2)}, u32[]{:S(2)}) collective-permute-start(bf16[272,512]{1,0:T(8,128)(2,1)} %maximum_maximum_fusion), channel_id=1, source_target_pairs={{0,14},{14,0},{2,12},{12,2},{4,10},{10,4},{6,8},{8,6},{1,15},{15,1... | collective-permute-start | bytes 835592 | tf_op jit(solution)/shard_map/ppermute | solution.py:921
  27.2 12.5 %collective-permute-start.3 = (bf16[256,169]{1,0:T(8,128)(2,1)S(1)}, bf16[256,169]{1,0:T(8,128)(2,1)S(1)}, u32[]{:S(2)}, u32[]{:S(2)}) collective-permute-start(bf16[256,169]{1,0:T(8,128)(2,1)S(1)} %concatenate.87), channel_id=1, source_target_pairs={{0,1},{1,0},{2,3},{3,2},{4,5},{5,4},{6,7},{7,6},{8,9},{9,8},{10,11... | collective-permute-start | bytes 259592 | tf_op jit(solution)/shard_map/ppermute | solution.py:820
  28.8 68.8 %collective-permute-start.12 = (bf16[256,1536]{1,0:T(8,128)(2,1)}, bf16[256,1536]{1,0:T(8,128)(2,1)}, u32[]{:S(2)}, u32[]{:S(2)}) collective-permute-start(bf16[256,1536]{1,0:T(8,128)(2,1)} %own_ref.3), channel_id=1, source_target_pairs={{0,1},{1,0},{2,3},{3,2},{4,5},{5,4},{6,7},{7,6},{8,9},{9,8},{10,11... | collective-permute-start | bytes 2359304 | tf_op jit(solution)/shard_map/ppermute | solution.py:820
  34.5 28.3 %copy-start.8 = (bf16[256,512]{1,0:T(8,128)(2,1)S(1)}, bf16[256,512]{1,0:T(8,128)(2,1)}, u32[]{:S(2)}) copy-start(bf16[256,512]{1,0:T(8,128)(2,1)} %get-tuple-element.143) | copy-start | bytes 786436
  34.5 22.4 %collective-permute-start.1 = (bf16[272,512]{1,0:T(8,128)(2,1)S(1)}, bf16[272,512]{1,0:T(8,128)(2,1)S(1)}, u32[]{:S(2)}, u32[]{:S(2)}) collective-permute-start(bf16[272,512]{1,0:T(8,128)(2,1)S(1)} %get-tuple-element.176), channel_id=1, source_target_pairs={{0,16},{16,0},{14,30},{30,14},{2,18},{18,2},{12,28},{28,12},{4,20}... | collective-permute-start | bytes 835592 | tf_op jit(solution)/shard_map/ppermute | solution.py:921
  34.6 27.5 %collective-permute-start.2 = (bf16[272,512]{1,0:T(8,128)(2,1)S(1)}, bf16[272,512]{1,0:T(8,128)(2,1)S(1)}, u32[]{:S(2)}, u32[]{:S(2)}) collective-permute-start(bf16[272,512]{1,0:T(8,128)(2,1)S(1)} %get-tuple-element.177), channel_id=1, source_target_pairs={{0,30},{14,16},{16,0},{30,14},{2,28},{12,18},{18,2},{28,12},{4,26}... | collective-permute-start | bytes 835592 | tf_op jit(solution)/shard_map/ppermute | solution.py:921
  63.9 14.0 %copy-start.31 = (s32[16]{0:T(128)S(1)}, s32[16]{0:T(128)}, u32[]{:S(2)}) copy-start(s32[16]{0:T(128)} %constant.119.clone) | copy-start | bytes 196
  69.5 25.7 %slice-start = ((bf16[272,512]{1,0:T(8,128)(2,1)}), bf16[4,512]{1,0:T(4,128)(2,1)S(1)}, s32[]{:S(2)}) async-start(bf16[272,512]{1,0:T(8,128)(2,1)} %copy-done.17), calls=%async_computation.1 | async-start | bytes 8192 | tf_op jit(solution)/shard_map/slice | solution.py:927
  69.5 25.7 %slice-start.1 = ((bf16[272,512]{1,0:T(8,128)(2,1)}), bf16[4,512]{1,0:T(4,128)(2,1)S(1)}, s32[]{:S(2)}) async-start(bf16[272,512]{1,0:T(8,128)(2,1)} %copy-done.18), calls=%async_computation.2 | async-start | bytes 8192 | tf_op jit(solution)/shard_map/slice | solution.py:927
  69.5 7.0 %collective-permute-start.4 = (bf16[2,256,128]{2,1,0:T(8,128)(2,1)S(1)}, bf16[2,256,128]{2,1,0:T(8,128)(2,1)S(1)}, u32[]{:S(2)}, u32[]{:S(2)}) collective-permute-start(bf16[2,256,128]{2,1,0:T(8,128)(2,1)S(1)} %pad_maximum_fusion.12), channel_id=1, source_target_pairs={{0,16},{2,18},{4,20},{6,22},{8,24},{10,26},{12,28},{14,30},{16,0},... | collective-permute-start | bytes 393224 | tf_op jit(solution)/shard_map/ppermute | solution.py:830
  76.6 12.8 %collective-permute-start.5 = (bf16[2,512,128]{2,1,0:T(8,128)(2,1)S(1)}, bf16[2,512,128]{2,1,0:T(8,128)(2,1)S(1)}, u32[]{:S(2)}, u32[]{:S(2)}) collective-permute-start(bf16[2,512,128]{2,1,0:T(8,128)(2,1)S(1)} %pad_maximum_fusion.11), channel_id=1, source_target_pairs={{0,8},{2,10},{4,12},{6,14},{8,0},{10,2},{12,4},{14,6},{16,24},{18,... | collective-permute-start | bytes 786440 | tf_op jit(solution)/shard_map/ppermute | solution.py:830
  90.2 14.5 %collective-permute-start.6 = (bf16[2,1024,128]{2,1,0:T(8,128)(2,1)}, bf16[2,1024,128]{2,1,0:T(8,128)(2,1)}, u32[]{:S(2)}, u32[]{:S(2)}) collective-permute-start(bf16[2,1024,128]{2,1,0:T(8,128)(2,1)} %pad_maximum_fusion.9), channel_id=1, source_target_pairs={{0,4},{2,6},{4,0},{6,2},{8,12},{10,14},{12,8},{14,10},{16,20},{18,... | collective-permute-start | bytes 1572872 | tf_op jit(solution)/shard_map/ppermute | solution.py:830
  96.1 19.6 %copy-start.19 = (bf16[512,128]{1,0:T(8,128)(2,1)}, bf16[512,128]{1,0:T(8,128)(2,1)S(1)}, u32[]{:S(2)}) copy-start(bf16[512,128]{1,0:T(8,128)(2,1)S(1)} %constant_dynamic-slice_fusion.21.refs_2_) | copy-start | bytes 393220
  96.1 20.6 %collective-permute-start.8 = (bf16[512,128]{1,0:T(8,128)(2,1)S(1)}, bf16[512,128]{1,0:T(8,128)(2,1)}, u32[]{:S(2)}, u32[]{:S(2)}) collective-permute-start(bf16[512,128]{1,0:T(8,128)(2,1)S(1)} %constant_dynamic-slice_fusion.21.refs_2_), channel_id=1, source_target_pairs={{0,16},{2,18},{4,20},{6,22},{8,24},{10,26},{12,28},{14,30},{16,0},... | collective-permute-start | bytes 393224 | tf_op jit(solution)/shard_map/ppermute | solution.py:830
  97.6 96.3 %collective-permute-start.13 = (bf16[1792,512]{1,0:T(8,128)(2,1)S(1)}, bf16[1792,512]{1,0:T(8,128)(2,1)}, u32[]{:S(2)}, u32[]{:S(2)}) collective-permute-start(bf16[1792,512]{1,0:T(8,128)(2,1)S(1)} %pad_maximum_fusion.1), channel_id=1, source_target_pairs={{0,1},{1,0},{2,3},{3,2},{4,5},{5,4},{6,7},{7,6},{8,9},{9,8},{10,11... | collective-permute-start | bytes 5505032 | tf_op jit(solution)/shard_map/ppermute | solution.py:820
  98.3 103.0 %collective-permute-start.14 = (bf16[256,2048]{1,0:T(8,128)(2,1)}, bf16[256,2048]{1,0:T(8,128)(2,1)}, u32[]{:S(2)}, u32[]{:S(2)}) collective-permute-start(bf16[256,2048]{1,0:T(8,128)(2,1)} %up_own_ref.1), channel_id=1, source_target_pairs={{0,1},{1,0},{2,3},{3,2},{4,5},{5,4},{6,7},{7,6},{8,9},{9,8},{10,11... | collective-permute-start | bytes 3145736 | tf_op jit(solution)/shard_map/ppermute | solution.py:820
  105.9 10.9 %collective-permute-start.7 = (bf16[2,2048,128]{2,1,0:T(8,128)(2,1)S(1)}, bf16[2,2048,128]{2,1,0:T(8,128)(2,1)S(1)}, u32[]{:S(2)}, u32[]{:S(2)}) collective-permute-start(bf16[2,2048,128]{2,1,0:T(8,128)(2,1)S(1)} %pad_maximum_fusion.4), channel_id=1, source_target_pairs={{0,2},{2,0},{4,6},{6,4},{8,10},{10,8},{12,14},{14,12},{16,18},{18,... | collective-permute-start | bytes 3145736 | tf_op jit(solution)/shard_map/ppermute | solution.py:830
  117.5 80.7 %collective-permute-start.9 = (bf16[256,512]{1,0:T(8,128)(2,1)S(1)}, bf16[256,512]{1,0:T(8,128)(2,1)}, u32[]{:S(2)}, u32[]{:S(2)}) collective-permute-start(bf16[256,512]{1,0:T(8,128)(2,1)S(1)} %get-tuple-element.142), channel_id=1, source_target_pairs={{0,14},{14,0},{2,12},{12,2},{4,10},{10,4},{6,8},{8,6},{1,15},{15,1... | collective-permute-start | bytes 786440 | tf_op jit(solution)/shard_map/ppermute | solution.py:921
  122.4 76.8 %collective-permute-start.10 = (bf16[256,512]{1,0:T(8,128)(2,1)S(1)}, bf16[256,512]{1,0:T(8,128)(2,1)}, u32[]{:S(2)}, u32[]{:S(2)}) collective-permute-start(bf16[256,512]{1,0:T(8,128)(2,1)S(1)} %get-tuple-element.141), channel_id=1, source_target_pairs={{0,16},{16,0},{14,30},{30,14},{2,18},{18,2},{12,28},{28,12},{4,20}... | collective-permute-start | bytes 786440 | tf_op jit(solution)/shard_map/ppermute | solution.py:921
  122.5 76.7 %collective-permute-start.11 = (bf16[256,512]{1,0:T(8,128)(2,1)S(1)}, bf16[256,512]{1,0:T(8,128)(2,1)}, u32[]{:S(2)}, u32[]{:S(2)}) collective-permute-start(bf16[256,512]{1,0:T(8,128)(2,1)S(1)} %get-tuple-element.140), channel_id=1, source_target_pairs={{0,30},{14,16},{16,0},{30,14},{2,28},{12,18},{18,2},{28,12},{4,26}... | collective-permute-start | bytes 786440 | tf_op jit(solution)/shard_map/ppermute | solution.py:921
  246.3 93.9 %collective-permute-start.15 = (bf16[2816,512]{1,0:T(8,128)(2,1)}, bf16[2816,512]{1,0:T(8,128)(2,1)}, u32[]{:S(2)}, u32[]{:S(2)}) collective-permute-start(bf16[2816,512]{1,0:T(8,128)(2,1)} %get-tuple-element.78), channel_id=1, source_target_pairs={{0,1},{1,0},{2,3},{3,2},{4,5},{5,4},{6,7},{7,6},{8,9},{9,8},{10,11... | collective-permute-start | bytes 8650760 | tf_op jit(solution)/shard_map/ppermute | solution.py:820
  247.8 89.4 %copy-start.24 = (f32[1,512]{1,0:T(1,128)S(1)}, f32[1,512]{1,0:T(1,128)}, u32[]{:S(2)}) copy-start(f32[1,512]{1,0:T(1,128)} %get-tuple-element.111) | copy-start | bytes 6148
  247.8 90.4 %copy-start.15 = (f32[512,128]{1,0:T(8,128)S(1)}, f32[512,128]{1,0:T(8,128)}, u32[]{:S(2)}) copy-start(f32[512,128]{1,0:T(8,128)} %get-tuple-element.109) | copy-start | bytes 786436
  247.8 91.3 %copy-start.14 = (f32[512,128]{1,0:T(8,128)S(1)}, f32[512,128]{1,0:T(8,128)}, u32[]{:S(2)}) copy-start(f32[512,128]{1,0:T(8,128)} %get-tuple-element.110) | copy-start | bytes 786436
  247.8 92.3 %copy-start.1 = (bf16[2816,512]{1,0:T(8,128)(2,1)S(1)}, bf16[2816,512]{1,0:T(8,128)(2,1)}, u32[]{:S(2)}) copy-start(bf16[2816,512]{1,0:T(8,128)(2,1)} %get-tuple-element.91) | copy-start | bytes 8650756
  340.2 109.4 %collective-permute-start.21 = (bf16[2048,128]{1,0:T(8,128)(2,1)}, bf16[2048,128]{1,0:T(8,128)(2,1)S(1)}, u32[]{:S(2)}, u32[]{:S(2)}) collective-permute-start(bf16[2048,128]{1,0:T(8,128)(2,1)} %get-tuple-element.103), channel_id=1, source_target_pairs={{0,2},{2,0},{4,6},{6,4},{8,10},{10,8},{12,14},{14,12},{16,18},{18,... | collective-permute-start | bytes 1572872 | tf_op jit(solution)/shard_map/ppermute | solution.py:830
  344.4 83.1 %copy-start.30 = (bf16[512,128]{1,0:T(8,128)(2,1)S(1)}, bf16[512,128]{1,0:T(8,128)(2,1)}, u32[]{:S(2)}) copy-start(bf16[512,128]{1,0:T(8,128)(2,1)} %get-tuple-element.99) | copy-start | bytes 393220
  344.4 83.2 %copy-start.3 = (bf16[1024,512]{1,0:T(8,128)(2,1)S(1)}, bf16[1024,512]{1,0:T(8,128)(2,1)}, u32[]{:S(2)}) copy-start(bf16[1024,512]{1,0:T(8,128)(2,1)} %get-tuple-element.90) | copy-start | bytes 3145732
  421.3 28.3 %collective-permute-start.20 = (bf16[2048,128]{1,0:T(8,128)(2,1)}, bf16[2048,128]{1,0:T(8,128)(2,1)S(1)}, u32[]{:S(2)}, u32[]{:S(2)}) collective-permute-start(bf16[2048,128]{1,0:T(8,128)(2,1)} %get-tuple-element.101), channel_id=1, source_target_pairs={{0,2},{2,0},{4,6},{6,4},{8,10},{10,8},{12,14},{14,12},{16,18},{18,... | collective-permute-start | bytes 1572872 | tf_op jit(solution)/shard_map/ppermute | solution.py:830
  427.5 15.7 %collective-permute-start.19 = (bf16[512,128]{1,0:T(8,128)(2,1)S(1)}, bf16[512,128]{1,0:T(8,128)(2,1)S(1)}, u32[]{:S(2)}, u32[]{:S(2)}) collective-permute-start(bf16[512,128]{1,0:T(8,128)(2,1)S(1)} %copy-done.30), channel_id=1, source_target_pairs={{0,16},{2,18},{4,20},{6,22},{8,24},{10,26},{12,28},{14,30},{16,0},... | collective-permute-start | bytes 393224 | tf_op jit(solution)/shard_map/ppermute | solution.py:830
  427.6 18.9 %collective-permute-start.16 = (bf16[256,512]{1,0:T(8,128)(2,1)S(1)}, bf16[256,512]{1,0:T(8,128)(2,1)S(1)}, u32[]{:S(2)}, u32[]{:S(2)}) collective-permute-start(bf16[256,512]{1,0:T(8,128)(2,1)S(1)} %slice.241), channel_id=1, source_target_pairs={{14,0},{0,14},{12,2},{2,12},{10,4},{4,10},{8,6},{6,8},{15,1},{1,15... | collective-permute-start | bytes 786440 | tf_op jit(solution)/shard_map/ppermute | solution.py:937
  443.0 7.7 %collective-permute-start.34 = (bf16[2,128,1536]{2,1,0:T(8,128)(2,1)}, bf16[2,128,1536]{2,1,0:T(8,128)(2,1)S(1)}, u32[]{:S(2)}, u32[]{:S(2)}) collective-permute-start(bf16[2,128,1536]{2,1,0:T(8,128)(2,1)} %get-tuple-element.114), channel_id=1, source_target_pairs={{0,2},{2,0},{4,6},{6,4},{8,10},{10,8},{12,14},{14,12},{16,18},{18,... | collective-permute-start | bytes 2359304 | tf_op jit(solution)/shard_map/ppermute | solution.py:830
  446.6 23.3 %collective-permute-start.17 = (bf16[256,512]{1,0:T(8,128)(2,1)S(1)}, bf16[256,512]{1,0:T(8,128)(2,1)S(1)}, u32[]{:S(2)}, u32[]{:S(2)}) collective-permute-start(bf16[256,512]{1,0:T(8,128)(2,1)S(1)} %get-tuple-element.134), channel_id=1, source_target_pairs={{16,0},{0,16},{30,14},{14,30},{18,2},{2,18},{28,12},{12,28},{20,4}... | collective-permute-start | bytes 786440 | tf_op jit(solution)/shard_map/ppermute | solution.py:937
  446.7 23.2 %collective-permute-start.18 = (bf16[256,512]{1,0:T(8,128)(2,1)S(1)}, bf16[256,512]{1,0:T(8,128)(2,1)S(1)}, u32[]{:S(2)}, u32[]{:S(2)}) collective-permute-start(bf16[256,512]{1,0:T(8,128)(2,1)S(1)} %get-tuple-element.133), channel_id=1, source_target_pairs={{30,0},{16,14},{0,16},{14,30},{28,2},{18,12},{2,18},{12,28},{26,4}... | collective-permute-start | bytes 786440 | tf_op jit(solution)/shard_map/ppermute | solution.py:937
  449.9 19.1 %collective-permute-start.22 = (bf16[2,1024,128]{2,1,0:T(8,128)(2,1)S(1)}, bf16[2,1024,128]{2,1,0:T(8,128)(2,1)S(1)}, u32[]{:S(2)}, u32[]{:S(2)}) collective-permute-start(bf16[2,1024,128]{2,1,0:T(8,128)(2,1)S(1)} %fusion.2), channel_id=1, source_target_pairs={{0,4},{2,6},{4,0},{6,2},{8,12},{10,14},{12,8},{14,10},{16,20},{18,... | collective-permute-start | bytes 1572872 | tf_op jit(solution)/shard_map/ppermute | solution.py:830
  469.1 6.9 %collective-permute-start.23 = (bf16[2,512,128]{2,1,0:T(8,128)(2,1)S(1)}, bf16[2,512,128]{2,1,0:T(8,128)(2,1)S(1)}, u32[]{:S(2)}, u32[]{:S(2)}) collective-permute-start(bf16[2,512,128]{2,1,0:T(8,128)(2,1)S(1)} %slice.397), channel_id=1, source_target_pairs={{0,8},{2,10},{4,12},{6,14},{8,0},{10,2},{12,4},{14,6},{16,24},{18,... | collective-permute-start | bytes 786440 | tf_op jit(solution)/shard_map/ppermute | solution.py:830
  469.2 9.7 %collective-permute-start.35 = (bf16[128,1536]{1,0:T(8,128)(2,1)S(1)}, bf16[128,1536]{1,0:T(8,128)(2,1)S(1)}, u32[]{:S(2)}, u32[]{:S(2)}) collective-permute-start(bf16[128,1536]{1,0:T(8,128)(2,1)S(1)} %constant_dynamic-slice_fusion.16), channel_id=1, source_target_pairs={{0,1},{1,0},{2,3},{3,2},{4,5},{5,4},{6,7},{7,6},{8,9},{9,8},{10,11... | collective-permute-start | bytes 1179656 | tf_op jit(solution)/shard_map/ppermute | solution.py:820
  476.1 7.7 %collective-permute-start.24 = (bf16[2,256,128]{2,1,0:T(8,128)(2,1)S(1)}, bf16[2,256,128]{2,1,0:T(8,128)(2,1)S(1)}, u32[]{:S(2)}, u32[]{:S(2)}) collective-permute-start(bf16[2,256,128]{2,1,0:T(8,128)(2,1)S(1)} %slice.398), channel_id=1, source_target_pairs={{0,16},{2,18},{4,20},{6,22},{8,24},{10,26},{12,28},{14,30},{16,0},... | collective-permute-start | bytes 393224 | tf_op jit(solution)/shard_map/ppermute | solution.py:830
  497.5 1.5 collective-permute-start.28
  497.6 7.4 %collective-permute-start.36 = (bf16[64,1536]{1,0:T(8,128)(2,1)S(1)}, bf16[64,1536]{1,0:T(8,128)(2,1)S(1)}, u32[]{:S(2)}, u32[]{:S(2)}) collective-permute-start(bf16[64,1536]{1,0:T(8,128)(2,1)S(1)} %constant_dynamic-slice_fusion.20), channel_id=1, source_target_pairs={{0,4},{2,6},{4,0},{6,2},{8,12},{10,14},{12,8},{14,10},{16,20},{18,... | collective-permute-start | bytes 589832 | tf_op jit(solution)/shard_map/ppermute | solution.py:830
  499.2 9.8 %collective-permute-start.29 = (bf16[128,169]{0,1:T(8,128)(2,1)S(1)}, bf16[128,169]{0,1:T(8,128)(2,1)S(1)}, u32[]{:S(2)}, u32[]{:S(2)}) collective-permute-start(bf16[128,169]{0,1:T(8,128)(2,1)S(1)} %copy.65), channel_id=1, source_target_pairs={{0,1},{1,0},{2,3},{3,2},{4,5},{5,4},{6,7},{7,6},{8,9},{9,8},{10,11... | collective-permute-start | bytes 129800 | tf_op jit(solution)/shard_map/ppermute | solution.py:820
  505.0 19.9 %collective-permute-start.37 = (bf16[64,1536]{1,0:T(8,128)(2,1)S(1)}, bf16[64,1536]{1,0:T(8,128)(2,1)S(1)}, u32[]{:S(2)}, u32[]{:S(2)}) collective-permute-start(bf16[64,1536]{1,0:T(8,128)(2,1)S(1)} %add_convert_fusion.5), channel_id=1, source_target_pairs={{0,8},{2,10},{4,12},{6,14},{8,0},{10,2},{12,4},{14,6},{16,24},{18,... | collective-permute-start | bytes 589832 | tf_op jit(solution)/shard_map/ppermute | solution.py:830
  505.3 29.9 %collective-permute-start.25 = (bf16[256,512]{1,0:T(8,128)(2,1)S(1)}, bf16[256,512]{1,0:T(8,128)(2,1)S(1)}, u32[]{:S(2)}, u32[]{:S(2)}) collective-permute-start(bf16[256,512]{1,0:T(8,128)(2,1)S(1)} %slice.257), channel_id=1, source_target_pairs={{14,0},{0,14},{12,2},{2,12},{10,4},{4,10},{8,6},{6,8},{15,1},{1,15... | collective-permute-start | bytes 786440 | tf_op jit(solution)/shard_map/ppermute | solution.py:937
  508.9 9.4 %collective-permute-start.30 = (bf16[128,169]{0,1:T(8,128)(2,1)S(1)}, bf16[128,169]{0,1:T(8,128)(2,1)S(1)}, u32[]{:S(2)}, u32[]{:S(2)}) collective-permute-start(bf16[128,169]{0,1:T(8,128)(2,1)S(1)} %add_convert_fusion.10), channel_id=1, source_target_pairs={{0,4},{2,6},{4,0},{6,2},{8,12},{10,14},{12,8},{14,10},{16,20},{18,... | collective-permute-start | bytes 129800 | tf_op jit(solution)/shard_map/ppermute | solution.py:830
  518.4 6.4 %collective-permute-start.31 = (bf16[128,169]{0,1:T(8,128)(2,1)S(1)}, bf16[128,169]{0,1:T(8,128)(2,1)S(1)}, u32[]{:S(2)}, u32[]{:S(2)}) collective-permute-start(bf16[128,169]{0,1:T(8,128)(2,1)S(1)} %add_convert_fusion.9), channel_id=1, source_target_pairs={{0,8},{2,10},{4,12},{6,14},{8,0},{10,2},{12,4},{14,6},{16,24},{18,... | collective-permute-start | bytes 129800 | tf_op jit(solution)/shard_map/ppermute | solution.py:830
  524.8 10.3 %collective-permute-start.32 = (bf16[128,169]{0,1:T(8,128)(2,1)S(1)}, bf16[128,169]{0,1:T(8,128)(2,1)S(1)}, u32[]{:S(2)}, u32[]{:S(2)}) collective-permute-start(bf16[128,169]{0,1:T(8,128)(2,1)S(1)} %add_convert_fusion.8), channel_id=1, source_target_pairs={{0,16},{2,18},{4,20},{6,22},{8,24},{10,26},{12,28},{14,30},{16,0},... | collective-permute-start | bytes 129800 | tf_op jit(solution)/shard_map/ppermute | solution.py:830
  525.0 25.7 %collective-permute-start.38 = (bf16[64,1536]{1,0:T(8,128)(2,1)S(1)}, bf16[64,1536]{1,0:T(8,128)(2,1)}, u32[]{:S(2)}, u32[]{:S(2)}) collective-permute-start(bf16[64,1536]{1,0:T(8,128)(2,1)S(1)} %add_convert_fusion.4), channel_id=1, source_target_pairs={{0,16},{2,18},{4,20},{6,22},{8,24},{10,26},{12,28},{14,30},{16,0},... | collective-permute-start | bytes 589832 | tf_op jit(solution)/shard_map/ppermute | solution.py:830
  535.1 3.8 collective-permute-start.33
  536.0 20.2 %collective-permute-start.26 = (bf16[256,512]{1,0:T(8,128)(2,1)}, bf16[256,512]{1,0:T(8,128)(2,1)S(1)}, u32[]{:S(2)}, u32[]{:S(2)}) collective-permute-start(bf16[256,512]{1,0:T(8,128)(2,1)} %get-tuple-element.126), channel_id=1, source_target_pairs={{16,0},{0,16},{30,14},{14,30},{18,2},{2,18},{28,12},{12,28},{20,4}... | collective-permute-start | bytes 786440 | tf_op jit(solution)/shard_map/ppermute | solution.py:937
  536.0 20.2 %collective-permute-start.27 = (bf16[256,512]{1,0:T(8,128)(2,1)S(1)}, bf16[256,512]{1,0:T(8,128)(2,1)S(1)}, u32[]{:S(2)}, u32[]{:S(2)}) collective-permute-start(bf16[256,512]{1,0:T(8,128)(2,1)S(1)} %get-tuple-element.125), channel_id=1, source_target_pairs={{30,0},{16,14},{0,16},{14,30},{28,2},{18,12},{2,18},{12,28},{26,4}... | collective-permute-start | bytes 786440 | tf_op jit(solution)/shard_map/ppermute | solution.py:937
  551.7 5.7 %collective-permute-start.39 = (bf16[64,1536]{1,0:T(8,128)(2,1)S(1)}, bf16[64,1536]{1,0:T(8,128)(2,1)S(1)}, u32[]{:S(2)}, u32[]{:S(2)}) collective-permute-start(bf16[64,1536]{1,0:T(8,128)(2,1)S(1)} %add_convert_fusion.3), channel_id=1, source_target_pairs={{0,4},{2,6},{4,0},{6,2},{8,12},{10,14},{12,8},{14,10},{16,20},{18,... | collective-permute-start | bytes 589832 | tf_op jit(solution)/shard_map/ppermute | solution.py:830
  557.5 2.7 collective-permute-start.40
  (14 other events, 96.7 us)
Sparse Core Ops, SparseCore 0:
  344.5 104.2 all-reduce.1

commit v3 on v2

v3 whole, which is shorter than its diff:
```python
import functools
import math

import jax
import jax.numpy as jnp
from jax import lax
from jax.experimental import pallas as pl
from jax.experimental.pallas import tpu as pltpu
from jax.sharding import PartitionSpec as P

PROMPT = 8192
CLEN = 1024
ROWS = 128
TILE = 256
FULL = 1024
PART = 256
HALF = PROMPT // 2
VMEM = 60 << 20

PIECES, IS_PROMPT, LOW_SLOT, HIGH_SLOT, OWN_SLOT, SHARD, CORE, SIDE, BASES = 0, 4, 5, 6, 7, 8, 9, 10, 11
norm_eps = 1e-05
mask_fill = -1e30
LOG2E = math.log2(math.e)
bf16 = jnp.bfloat16
f32 = jnp.float32


def dot(a, b):
    return lax.dot_general(a, b, (((1,), (0,)), ((), ())), preferred_element_type=f32)


def dot_tn(a, b):
    return lax.dot_general(a, b, (((0,), (0,)), ((), ())), preferred_element_type=f32)


def dot_nt(a, b):
    return lax.dot_general(a, b, (((1,), (1,)), ((), ())), preferred_element_type=f32)


def params(**kw):
    return pltpu.CompilerParams(vmem_limit_bytes=VMEM, **kw)


def cost(us):
    return pl.CostEstimate(flops=int(us * 1.15e9), transcendentals=0, bytes_accessed=0)


def whole(shape):
    return pl.BlockSpec(shape, lambda i: tuple(0 for _ in shape))


def column_norm(values):
    center = jnp.mean(values, axis=0, keepdims=True)
    centred = values - center
    spread = jnp.mean(centred * centred, axis=0, keepdims=True)
    inverse = lax.rsqrt(spread + norm_eps)
    return centred * inverse, inverse


def column_norm_back(grad, unit, inverse, gain):
    scaled = grad * gain
    inner = (
        scaled
        - jnp.mean(scaled, axis=0, keepdims=True)
        - unit * jnp.mean(scaled * unit, axis=0, keepdims=True)
    )
    return inner * inverse


def fold_lanes(values):
    width = values.shape[1]
    total = values[:, :128]
    for start in range(128, width, 128):
        total = total + values[:, start : start + 128]
    return total


def pick_piece(step, table_ref, sources, target_ref):
    if len(sources) == 1:
        target_ref[...] = sources[0][...]
        return
    keep, own, *got = sources
    rows = target_ref.shape[0]
    prompt = table_ref[IS_PROMPT] == 1
    which = ((step == 0), (step == 1) & jnp.logical_not(prompt), (step == 1) & prompt)
    for chosen, ref in zip(which + ((step == 2), (step == 3)), (keep, own, *got)):

        @pl.when(chosen)
        def _():
            target_ref[...] = ref[:rows, :]


def store_piece(step, targets, value):
    if len(targets) == 1:
        targets[0][...] = value
        return
    for k, ref in enumerate(targets):

        @pl.when(step == k)
        def _():
            ref[...] = value


def piece_specs(pieces):
    if len(pieces) == 1:
        return [pl.BlockSpec((TILE, pieces[0].shape[1]), lambda i, t: (i, 0))]
    return [pl.BlockSpec(x.shape, lambda i, t: (0, 0)) for x in pieces]


def pack_kernel(table_ref, *refs):
    rows_ref, *refs = refs
    index = refs.pop(0) if len(refs) > 4 else None
    for k, ref in enumerate(refs):
        span = pl.ds(pl.multiple_of(table_ref[PIECES + k] * PART, PART), PART)
        ref[:PART, :] = rows_ref[span, :]
        if index is not None:
            chosen = index[:, span].astype(f32)
            blank = jnp.zeros((16 - index.shape[0], PART), f32)
            ref[PART:, :] = jnp.concatenate(
                [jnp.concatenate([chosen, blank], axis=0)] * (ref.shape[1] // PART), axis=1
            ).astype(bf16)


def pack_call(table, rows, index=None):
    count, width = rows.shape
    out = (count // 4 + (0 if index is None else 16), width)
    inputs = (rows,) if index is None else (rows, index)
    return pl.pallas_call(
        pack_kernel,
        grid_spec=pltpu.PrefetchScalarGridSpec(
            num_scalar_prefetch=1,
            grid=(1,),
            in_specs=[pl.BlockSpec(x.shape, lambda i, t: (0, 0)) for x in inputs],
            out_specs=[pl.BlockSpec(out, lambda i, t: (0, 0))] * 4,
        ),
        out_shape=[jax.ShapeDtypeStruct(out, bf16)] * 4,
        compiler_params=params(),
        cost_estimate=cost(2),
        name="pack",
    )(table, *inputs)


def unpack_kernel(table_ref, keep_ref, own_ref, *refs):
    *got, out_ref = refs
    prompt = table_ref[IS_PROMPT] == 1
    place_of = lambda k: pl.ds(pl.multiple_of(table_ref[PIECES + k] * PART, PART), PART)
    out_ref[place_of(0), :] = keep_ref[...]
    out_ref[place_of(2), :] = got[1][...]
    out_ref[place_of(3), :] = got[2][...]

    @pl.when(prompt)
    def _():
        out_ref[place_of(1), :] = got[0][...]

    @pl.when(jnp.logical_not(prompt))
    def _():
        out_ref[place_of(1), :] = own_ref[...]


def unpack_call(table, pieces):
    rows, width = pieces[0].shape
    return pl.pallas_call(
        unpack_kernel,
        grid_spec=pltpu.PrefetchScalarGridSpec(
            num_scalar_prefetch=1,
            grid=(1,),
            in_specs=[pl.BlockSpec((rows, width), lambda i, t: (0, 0))] * 5,
            out_specs=pl.BlockSpec((4 * rows, width), lambda i, t: (0, 0)),
        ),
        out_shape=jax.ShapeDtypeStruct((4 * rows, width), bf16),
        compiler_params=params(),
        cost_estimate=cost(2),
        name="unpack",
    )(table, *pieces)


def first_kernel(pieces, table_ref, *refs):
    sources = refs[:pieces]
    gain_ref, shift_ref, kv_weight_ref = refs[pieces : pieces + 3]
    refs = refs[pieces + 3 :]
    step = pl.program_id(0)
    first_ref = refs[0]
    tokens_ref = refs[-1]
    pick_piece(step, table_ref, sources, tokens_ref)
    unit, _ = column_norm(tokens_ref[...].astype(f32).T)
    first = (unit * gain_ref[...] + shift_ref[...]).astype(bf16)
    first_ref[...] = first
    kv = dot_tn(kv_weight_ref[...], first).T.astype(bf16)
    if pieces == 1:
        refs[1][...] = kv
        return
    shared_ref, own_ref, index_ref, flat_ref, _ = refs[1:]
    flat_ref[...] = tokens_ref[...]
    topk, rows = index_ref.shape
    keep, own, *got = sources
    prompt = table_ref[IS_PROMPT] == 1
    which = ((step == 0), (step == 1) & jnp.logical_not(prompt), (step == 1) & prompt)
    for chosen, ref in zip(which + ((step == 2), (step == 3)), (keep, own, *got)):

        @pl.when(chosen)
        def _():
            index_ref[...] = ref[PART:, :rows][:topk, :].astype(f32).astype(jnp.int32)

    for slot, half in ((LOW_SLOT, 0), (HIGH_SLOT, 1)):

        @pl.when(step == table_ref[slot])
        def _():
            shared_ref[half * PART : (half + 1) * PART, :] = kv

    for half in range(2):

        @pl.when(step == table_ref[OWN_SLOT] + half)
        def _():
            own_ref[half * PART : (half + 1) * PART, :] = kv


def first_call(table, sources, count, topk, gain, shift, kv_weight):
    width, pair = kv_weight.shape
    keep = lambda shape: pl.BlockSpec(shape, lambda i, t: (0, 0))
    shape = jax.ShapeDtypeStruct
    split = len(sources) > 1
    outs = [(pl.BlockSpec((width, TILE), lambda i, t: (0, i)), shape((width, count), bf16))]
    rows = lambda n: pl.BlockSpec((TILE, n), lambda i, t: (i, 0))
    if split:
        outs += [
            (keep((2 * PART, pair)), shape((2 * PART, pair), bf16)),
            (keep((2 * PART, pair)), shape((2 * PART, pair), bf16)),
            (pl.BlockSpec((topk, TILE), lambda i, t: (0, i)), shape((topk, count), jnp.int32)),
            (rows(width), shape((count, width), bf16)),
        ]
    else:
        outs += [(rows(pair), shape((count, pair), bf16))]
    return pl.pallas_call(
        functools.partial(first_kernel, len(sources)),
        grid_spec=pltpu.PrefetchScalarGridSpec(
            num_scalar_prefetch=1,
            grid=(count // TILE,),
            in_specs=piece_specs(sources)
            + [keep((width, 1)), keep((width, 1)), keep((width, pair))],
            out_specs=[x for x, _ in outs],
            scratch_shapes=[pltpu.VMEM((TILE, width), bf16)],
        ),
        out_shape=[x for _, x in outs],
        compiler_params=params(),
        cost_estimate=cost(5),
        name="first_norm",
    )(table, *sources, gain, shift, kv_weight)


def join_rows(shard, own_ref, other_ref, all_ref, start=0):
    half = own_ref.shape[0]
    all_ref[pl.ds(pl.multiple_of(shard * half, half), half), :] = own_ref[...]
    rows = pl.ds(pl.multiple_of((1 - shard) * half, half), half)
    all_ref[rows, :] = other_ref[start : start + half, :]


def query_kernel(
    table_ref, first_ref, own_ref, other_ref, router_ref, index_ref,
    qt_ref, q_ref, gate_ref, query_weight_ref,
):
    topk = index_ref.shape[0]

    @pl.when(pl.program_id(0) == 0)
    def _():
        join_rows(table_ref[SHARD], own_ref, other_ref, query_weight_ref)

    head = qt_ref.shape[1]
    experts = query_weight_ref.shape[1] // head
    first = first_ref[...]
    projected = dot_tn(query_weight_ref[...], first)
    logits = dot_tn(router_ref[...], first)
    index = index_ref[...]
    picked = jnp.zeros(index.shape, f32)
    for expert in range(experts):
        picked = jnp.where(index == expert, logits[expert : expert + 1, :], picked)
    picked = jnp.exp(picked - jnp.max(picked, axis=0, keepdims=True))
    gate_ref[...] = picked / jnp.sum(picked, axis=0, keepdims=True)
    for part in range(TILE // ROWS):
        lanes = slice(part * ROWS, (part + 1) * ROWS)
        for j in range(topk):
            row = index[j : j + 1, lanes]
            chosen = jnp.zeros((head, ROWS), f32)
            for expert in range(experts):
                chosen = jnp.where(
                    row == expert, projected[expert * head : (expert + 1) * head, lanes], chosen
                )
            qt_ref[part, :, j * ROWS : (j + 1) * ROWS] = chosen.astype(bf16)
            q_ref[part, j * ROWS : (j + 1) * ROWS, :] = chosen.T.astype(bf16)


def query_call(table, first, own, other, router, index, head):
    width, count = first.shape
    topk = index.shape[0]
    tiles = count // ROWS
    per = TILE // ROWS
    keep = lambda shape: pl.BlockSpec(shape, lambda i, s: (0, 0))
    return pl.pallas_call(
        query_kernel,
        grid_spec=pltpu.PrefetchScalarGridSpec(
            num_scalar_prefetch=1,
            grid=(count // TILE,),
            in_specs=[
                pl.BlockSpec((width, TILE), lambda i, s: (0, i)),
                keep(own.shape),
                keep(other.shape),
                keep(router.shape),
                pl.BlockSpec((topk, TILE), lambda i, s: (0, i)),
            ],
            out_specs=[
                pl.BlockSpec((per, head, topk * ROWS), lambda i, s: (i, 0, 0)),
                pl.BlockSpec((per, topk * ROWS, head), lambda i, s: (i, 0, 0)),
                pl.BlockSpec((topk, TILE), lambda i, s: (0, i)),
            ],
            scratch_shapes=[pltpu.VMEM((width, own.shape[1]), bf16)],
        ),
        out_shape=[
            jax.ShapeDtypeStruct((tiles, head, topk * ROWS), bf16),
            jax.ShapeDtypeStruct((tiles, topk * ROWS, head), bf16),
            jax.ShapeDtypeStruct((topk, count), f32),
        ],
        compiler_params=params(),
        cost_estimate=cost(10),
        name="queries",
    )(table, first, own, other, router, index)


def tile_ranges(base):
    prompt = base < PROMPT
    begin = jnp.where(prompt, base // FULL * FULL, PROMPT)
    position = jnp.where(prompt, begin, PROMPT + (base - PROMPT) // CLEN * CLEN)
    parts = (base + ROWS - position + PART - 1) // PART
    return begin // FULL, begin, position, parts


def allowed_mask(position, base, width):
    key_pos = position + lax.broadcasted_iota(jnp.int32, (PART, width), 0)
    query_pos = base + lax.rem(lax.broadcasted_iota(jnp.int32, (PART, width), 1), ROWS)
    return key_pos <= query_pos


def for_slots(refs, table_ref, start, visit):
    slot = 0
    for ref in refs:
        for row in range(0, ref.shape[0], PART):
            place_of = pl.multiple_of(table_ref[start + slot] * PART, PART)
            visit(ref, row, pl.ds(place_of, PART))
            slot += 1


def attend_kernel(start, buffers, table_ref, *refs):
    sources = refs[:buffers]
    qt_ref = refs[buffers]
    refs = refs[buffers + 1 :]
    out_ref, lse_ref, kv_ref, vt_ref, knorm_ref, acc_ref, max_ref = refs
    tile = pl.program_id(0)
    head, width = qt_ref.shape[1:]
    factor = LOG2E * head ** (-0.5)

    @pl.when(tile == 0)
    def _():
        knorm_ref[0] = 0.0

        def turn(ref, row, span):
            rows = ref[row : row + PART, :]
            kv_ref[span, :] = rows
            both = rows.T
            vt_ref[:head, span] = both[head:, :]
            vt_ref[head:, span] = jnp.ones((vt_ref.shape[0] - head, PART), bf16)
            keys = both[:head, :].astype(f32)
            most = jnp.max(jnp.sum(keys * keys, axis=0, keepdims=True))
            knorm_ref[0] = jnp.maximum(knorm_ref[0], most)

        for_slots(sources, table_ref, start, turn)

    base = table_ref[BASES + tile]
    steps, begin, position, parts = tile_ranges(base)
    query = qt_ref[0].astype(f32)
    qnorm = jnp.max(jnp.sum(query * query, axis=0, keepdims=True))
    narrow = qnorm * knorm_ref[0] * (factor * factor) < 100.0 * 100.0
    acc_ref[...] = jnp.zeros(acc_ref.shape, f32)
    max_ref[...] = jnp.full(max_ref.shape, jnp.where(narrow, 0.0, mask_fill), f32)

    def plain(offset, size, mask):
        span = pl.ds(pl.multiple_of(offset, size), size)
        scores = dot(kv_ref[span, :head], qt_ref[0]) * factor
        if mask is not None:
            scores = jnp.where(mask, scores, mask_fill)
        probs = jnp.exp2(scores).astype(bf16)
        acc_ref[...] += dot(vt_ref[:, span], probs)

    @pl.when(narrow)
    def _():
        def step(i, carry):
            plain(i * FULL, FULL, None)
            return carry

        def part(i, carry):
            plain(begin + i * PART, PART, allowed_mask(position + i * PART, base, width))
            return carry

        lax.fori_loop(0, steps, step, 0)
        lax.fori_loop(0, parts, part, 0)

    @pl.when(jnp.logical_not(narrow))
    def _():
        def part(i, carry):
            before = i < steps * (FULL // PART)
            offset = i * PART
            span = pl.ds(pl.multiple_of(offset, PART), PART)
            shifted = jnp.where(before, -(1 << 24), position + offset - begin)
            mask = allowed_mask(shifted, base, width)
            scores = dot(kv_ref[span, :head], qt_ref[0]) * factor
            scores = jnp.where(mask, scores, mask_fill)
            old = max_ref[...]
            new = jnp.maximum(old, jnp.max(scores, axis=0, keepdims=True))
            probs = jnp.where(mask, jnp.exp2(scores - new), 0.0).astype(bf16)
            acc_ref[...] = acc_ref[...] * jnp.exp2(old - new) + dot(vt_ref[:, span], probs)
            max_ref[...] = new
            return carry

        lax.fori_loop(0, steps * (FULL // PART) + parts, part, 0)

    total = acc_ref[head : head + 1, :]
    out_ref[0] = acc_ref[:head, :] / total
    lse_ref[0] = max_ref[...] + jnp.log2(total)


def attend_call(start, sources, table, qt):
    tiles, head, width = qt.shape
    total_keys = sum(x.shape[0] for x in sources)
    pair = sources[0].shape[1]
    one = lambda shape: pl.BlockSpec((1,) + shape, lambda i, t: (i, 0, 0))
    keep = lambda x: pl.BlockSpec(x.shape, lambda i, t: (0, 0))
    return pl.pallas_call(
        functools.partial(attend_kernel, start, len(sources)),
        grid_spec=pltpu.PrefetchScalarGridSpec(
            num_scalar_prefetch=1,
            grid=(tiles,),
            in_specs=[keep(x) for x in sources] + [one((head, width))],
            out_specs=[one((head, width)), one((1, width))],
            scratch_shapes=[
                pltpu.VMEM((total_keys, pair), bf16),
                pltpu.VMEM((head + 16, total_keys), bf16),
                pltpu.SMEM((1,), f32),
                pltpu.VMEM((head + 16, width), f32),
                pltpu.VMEM((1, width), f32),
            ],
        ),
        out_shape=[
            jax.ShapeDtypeStruct((tiles, head, width), f32),
            jax.ShapeDtypeStruct((tiles, 1, width), f32),
        ],
        compiler_params=params(),
        cost_estimate=cost(64),
        name="attend",
    )(table, *sources, qt)


def attend_back_kernel(start, buffers, table_ref, *refs):
    sources = refs[:buffers]
    qt_ref, q_ref, dot_ref, do_ref, lse_ref, delta_ref = refs[buffers : buffers + 6]
    refs = refs[buffers + 6 :]
    dq_ref = refs[0]
    outs = refs[1 : 1 + buffers]
    kv_ref, kt_ref, dkv_ref = refs[1 + buffers :]
    tile = pl.program_id(0)
    head, width = qt_ref.shape[1:]
    scale = head ** (-0.5)

    @pl.when(tile == 0)
    def _():
        def turn(ref, row, span):
            rows = ref[row : row + PART, :]
            kv_ref[span, :] = rows
            kt_ref[:, span] = rows.T[:head, :]
            dkv_ref[span, :] = jnp.zeros((PART, 2 * head), f32)

        for_slots(sources, table_ref, start, turn)

    base = table_ref[BASES + tile]
    steps, begin, position, parts = tile_ranges(base)
    dq_ref[...] = jnp.zeros(dq_ref.shape, f32)

    def block(offset, size, mask):
        span = pl.ds(pl.multiple_of(offset, size), size)
        scores = dot(kv_ref[span, :head], qt_ref[0]) * (LOG2E * scale) - lse_ref[0]
        probs = jnp.exp2(scores)
        if mask is not None:
            probs = jnp.where(mask, probs, 0.0)
        prob_grad = dot(kv_ref[span, head:], dot_ref[0])
        score_grad = (probs * (prob_grad - delta_ref[0])).astype(bf16)
        dq_ref[0] += dot(kt_ref[:, span], score_grad) * scale
        dkv_ref[span, :head] += dot(score_grad, q_ref[0])
        dkv_ref[span, head:] += dot(probs.astype(bf16), do_ref[0])

    def step(i, carry):
        block(i * FULL, FULL, None)
        return carry

    def part(i, carry):
        block(begin + i * PART, PART, allowed_mask(position + i * PART, base, width))
        return carry

    lax.fori_loop(0, steps, step, 0)
    lax.fori_loop(0, parts, part, 0)

    @pl.when(tile == pl.num_programs(0) - 1)
    def _():
        lane = lax.broadcasted_iota(jnp.int32, (PART, 2 * head), 1)
        both = jnp.where(lane < head, scale, 1.0)

        def finish(ref, row, span):
            ref[row : row + PART, :] = (dkv_ref[span, :] * both).astype(ref.dtype)

        for_slots(outs, table_ref, start, finish)


def attend_back_call(start, sources, kinds, table, qt, q, grad_t, grad, lse, delta):
    tiles, head, width = qt.shape
    total_keys = sum(x.shape[0] for x in sources)
    pair = sources[0].shape[1]
    one = lambda shape: pl.BlockSpec((1,) + shape, lambda i, t: (i, 0, 0))
    keep = lambda x: pl.BlockSpec(x.shape, lambda i, t: (0, 0))
    return pl.pallas_call(
        functools.partial(attend_back_kernel, start, len(sources)),
        grid_spec=pltpu.PrefetchScalarGridSpec(
            num_scalar_prefetch=1,
            grid=(tiles,),
            in_specs=[keep(x) for x in sources]
            + [
                one((head, width)),
                one((width, head)),
                one((head, width)),
                one((width, head)),
                one((1, width)),
                one((1, width)),
            ],
            out_specs=[one((head, width))] + [keep(x) for x in sources],
            scratch_shapes=[
                pltpu.VMEM((total_keys, pair), bf16),
                pltpu.VMEM((head, total_keys), bf16),
                pltpu.VMEM((total_keys, pair), f32),
            ],
        ),
        out_shape=[jax.ShapeDtypeStruct((tiles, head, width), f32)]
        + [jax.ShapeDtypeStruct(x.shape, kind) for x, kind in zip(sources, kinds)],
        compiler_params=params(),
        cost_estimate=cost(160),
        name="attend_back",
    )(table, *sources, qt, q, grad_t, grad, lse, delta)


def place(index, pieces, expert):
    total = jnp.zeros(pieces[0].shape, f32)
    for j, piece in enumerate(pieces):
        total = jnp.where(index[j : j + 1, :] == expert, piece, total)
    return total


def middle_kernel(pieces, table_ref, *refs):
    sources = refs[:pieces]
    refs = refs[pieces:]
    outs = 4 if pieces > 1 else 1
    layer_out_refs = refs[MIDDLE_INPUTS : MIDDLE_INPUTS + outs]
    refs = refs[:MIDDLE_INPUTS] + refs[MIDDLE_INPUTS + outs :]
    middle_body(table_ref, sources, layer_out_refs, *refs)


MIDDLE_INPUTS = 13


def middle_body(
    table_ref,
    sources,
    layer_out_refs,
    tokens_ref,
    index_ref,
    gate_ref,
    attended_ref,
    output_own_ref,
    down_own_ref,
    both_other_ref,
    up_own_ref,
    up_other_ref,
    gain_ref,
    shift_ref,
    up_bias_ref,
    down_bias_ref,
    middle_grad_ref,
    grad_t_ref,
    grad_rows_ref,
    delta_ref,
    logit_grad_ref,
    output_weight_grad_ref,
    up_weight_grad_ref,
    down_weight_grad_ref,
    gain_grad_ref,
    shift_grad_ref,
    up_bias_grad_ref,
    down_bias_grad_ref,
    grad_ref,
    output_weight_ref,
    up_weight_ref,
    down_weight_ref,
    spread_ref,
    chosen_ref,
    dwo_ref,
    dup_ref,
    ddown_ref,
):
    step = pl.program_id(0)
    topk = index_ref.shape[0]
    head = attended_ref.shape[1]
    experts = output_weight_ref.shape[0] // head
    per = TILE // ROWS

    @pl.when(step == 0)
    def _():
        shard = table_ref[SHARD]
        join_rows(shard, output_own_ref, both_other_ref, output_weight_ref)
        join_rows(shard, down_own_ref, both_other_ref, down_weight_ref, output_own_ref.shape[0])
        join_rows(shard, up_own_ref, up_other_ref, up_weight_ref)
        for ref in (
            dwo_ref,
            dup_ref,
            ddown_ref,
            gain_grad_ref,
            shift_grad_ref,
            up_bias_grad_ref,
            down_bias_grad_ref,
        ):
            ref[...] = jnp.zeros(ref.shape, ref.dtype)

    pick_piece(step, table_ref, sources, grad_ref)
    index = index_ref[...]
    gate = gate_ref[...]
    for part in range(per):
        lanes = slice(part * ROWS, (part + 1) * ROWS)
        pieces = [
            attended_ref[part, :, j * ROWS : (j + 1) * ROWS] * gate[j : j + 1, lanes]
            for j in range(topk)
        ]
        for expert in range(experts):
            spread_ref[expert * head : (expert + 1) * head, lanes] = place(
                index[:, lanes], pieces, expert
            ).astype(bf16)

    middle = tokens_ref[...].astype(f32).T + dot_tn(output_weight_ref[...], spread_ref[...])
    unit, inverse = column_norm(middle)
    second = (unit * gain_ref[...] + shift_ref[...]).astype(bf16)
    pre = dot_tn(up_weight_ref[...], second) + up_bias_ref[...]
    coeff = math.sqrt(2.0 / math.pi)
    square = pre * pre
    wave = jnp.tanh(coeff * pre * (1.0 + 0.044715 * square))
    half = 0.5 * (1.0 + wave)
    hidden = (pre * half).astype(bf16)
    slope = half + 0.5 * pre * (1.0 - wave * wave) * (coeff * (1.0 + 3 * 0.044715 * square))
    result = middle + dot_tn(down_weight_ref[...], hidden) + down_bias_ref[...]
    store_piece(step, layer_out_refs, result.T.astype(bf16))

    grad_rows = grad_ref[...]
    grad_wide = grad_rows.astype(f32)
    grad_t = grad_wide.T
    ddown_ref[...] += dot(hidden, grad_rows)
    down_bias_grad_ref[...] += jnp.sum(grad_wide, axis=0, keepdims=True)
    pre_grad = (dot(down_weight_ref[...], grad_t.astype(bf16)) * slope).astype(bf16)
    dup_ref[...] += dot_nt(second, pre_grad)
    up_bias_grad_ref[...] += fold_lanes(pre_grad.astype(f32))
    second_grad = dot(up_weight_ref[...], pre_grad)
    gain_grad_ref[...] += fold_lanes(second_grad * unit)
    shift_grad_ref[...] += fold_lanes(second_grad)
    middle_grad = grad_t + column_norm_back(second_grad, unit, inverse, gain_ref[...])
    middle_grad_ref[...] = middle_grad
    middle_low = middle_grad.astype(bf16)
    dwo_ref[...] += dot_nt(spread_ref[...], middle_low)
    chosen_ref[...] = dot(output_weight_ref[...], middle_low)

    for part in range(per):
        lanes = slice(part * ROWS, (part + 1) * ROWS)
        picks = []
        for j in range(topk):
            span = slice(j * ROWS, (j + 1) * ROWS)
            row = index[j : j + 1, lanes]
            chosen = jnp.zeros((head, ROWS), f32)
            for expert in range(experts):
                chosen = jnp.where(
                    row == expert, chosen_ref[expert * head : (expert + 1) * head, lanes], chosen
                )
            attended = attended_ref[part, :, span]
            picks.append(jnp.sum(chosen * attended, axis=0, keepdims=True))
            back = (chosen * gate[j : j + 1, lanes]).astype(bf16)
            grad_t_ref[part, :, span] = back
            back = back.astype(f32)
            grad_rows_ref[part, span, :] = back.T.astype(bf16)
            delta_ref[part, :, span] = jnp.sum(back * attended, axis=0, keepdims=True)
        gates = [gate[j : j + 1, lanes] for j in range(topk)]
        mean = sum(g * p for g, p in zip(gates, picks))
        rows = [g * (p - mean) for g, p in zip(gates, picks)]
        spare = logit_grad_ref.shape[0] - experts
        logit = [place(index[:, lanes], rows, expert) for expert in range(experts)]
        logit.append(jnp.zeros((spare, ROWS), f32))
        logit_grad_ref[:, lanes] = jnp.concatenate(logit, axis=0).astype(bf16)

    @pl.when(step == pl.num_programs(0) - 1)
    def _():
        output_weight_grad_ref[...] = dwo_ref[...].astype(bf16)
        up_weight_grad_ref[...] = dup_ref[...].astype(bf16)
        down_weight_grad_ref[...] = ddown_ref[...].astype(bf16)


def middle_call(
    table, sources, tokens, index, gate, attended, weights, gain, shift, up_bias, down_bias, padded
):
    count, width = tokens.shape
    topk = index.shape[0]
    tiles, head, wide = attended.shape
    per = TILE // ROWS
    spread = 2 * weights[0].shape[0]
    hidden = 2 * weights[1].shape[0]
    keep = lambda shape: pl.BlockSpec(shape, lambda i, s: tuple(0 for _ in shape))
    rows = pl.BlockSpec((TILE, width), lambda i, s: (i, 0))
    columns = lambda n: pl.BlockSpec((n, TILE), lambda i, s: (0, i))
    tile = lambda shape: pl.BlockSpec((per,) + shape, lambda i, s: (i, 0, 0))
    shape = jax.ShapeDtypeStruct
    if len(sources) > 1:
        outs = [(keep((TILE, width)), shape((TILE, width), bf16))] * 4
    else:
        outs = [(rows, shape((count, width), bf16))]
    outs += [
        (columns(width), shape((width, count), f32)),
        (tile((head, wide)), shape((tiles, head, wide), bf16)),
        (tile((wide, head)), shape((tiles, wide, head), bf16)),
        (tile((1, wide)), shape((tiles, 1, wide), f32)),
        (columns(padded), shape((padded, count), bf16)),
        (keep((spread, width)), shape((spread, width), bf16)),
        (keep((width, hidden)), shape((width, hidden), bf16)),
        (keep((hidden, width)), shape((hidden, width), bf16)),
        (keep((width, 128)), shape((width, 128), f32)),
        (keep((width, 128)), shape((width, 128), f32)),
        (keep((hidden, 128)), shape((hidden, 128), f32)),
        (keep((1, width)), shape((1, width), f32)),
    ]
    return pl.pallas_call(
        functools.partial(middle_kernel, len(sources)),
        grid_spec=pltpu.PrefetchScalarGridSpec(
            num_scalar_prefetch=1,
            grid=(count // TILE,),
            in_specs=piece_specs(sources)
            + [rows, columns(topk), columns(topk), tile((head, wide))]
            + [keep(w.shape) for w in weights]
            + [keep((width, 1)), keep((width, 1)), keep((hidden, 1)), keep((width, 1))],
            out_specs=[x for x, _ in outs],
            scratch_shapes=[
                pltpu.VMEM((TILE, width), bf16),
                pltpu.VMEM((spread, width), bf16),
                pltpu.VMEM((width, hidden), bf16),
                pltpu.VMEM((hidden, width), bf16),
                pltpu.VMEM((spread, TILE), bf16),
                pltpu.VMEM((spread, TILE), f32),
                pltpu.VMEM((spread, width), f32),
                pltpu.VMEM((width, hidden), f32),
                pltpu.VMEM((hidden, width), f32),
            ],
        ),
        out_shape=[x for _, x in outs],
        compiler_params=params(),
        cost_estimate=cost(44),
        name="middle",
    )(table, *sources, tokens, index, gate, attended, *weights, gain, shift, up_bias, down_bias)


def query_back_kernel(
    table_ref,
    first_ref,
    index_ref,
    dq_ref,
    own_ref,
    other_ref,
    logit_grad_ref,
    router_ref,
    partial_ref,
    keep_ref,
    send_ref,
    router_grad_ref,
    query_weight_ref,
    placed_ref,
    dwq_ref,
    dr_ref,
):
    step = pl.program_id(0)
    topk = index_ref.shape[0]
    head = dq_ref.shape[1]
    experts = query_weight_ref.shape[1] // head

    @pl.when(step == 0)
    def _():
        join_rows(table_ref[SHARD], own_ref, other_ref, query_weight_ref)
        dwq_ref[...] = jnp.zeros(dwq_ref.shape, f32)
        dr_ref[...] = jnp.zeros(dr_ref.shape, f32)

    index = index_ref[...]
    for part in range(TILE // ROWS):
        lanes = slice(part * ROWS, (part + 1) * ROWS)
        pieces = [dq_ref[part, :, j * ROWS : (j + 1) * ROWS] for j in range(topk)]
        for expert in range(experts):
            placed_ref[expert * head : (expert + 1) * head, lanes] = place(
                index[:, lanes], pieces, expert
            ).astype(bf16)
    first = first_ref[...]
    dwq_ref[...] += dot_nt(first, placed_ref[...])
    dr_ref[...] += dot_nt(first, logit_grad_ref[...])
    partial_ref[...] = dot(query_weight_ref[...], placed_ref[...]) + dot(
        router_ref[...], logit_grad_ref[...]
    )

    @pl.when(step == pl.num_programs(0) - 1)
    def _():
        router_grad_ref[...] = dr_ref[...]
        size = keep_ref.shape[2]
        shard, core, side = table_ref[SHARD], table_ref[CORE], table_ref[SIDE]
        for target, last in ((keep_ref, core), (send_ref, 1 - core)):
            for i, half in enumerate((shard, 1 - shard)):
                for j, part in enumerate((side, 1 - side)):
                    at = ((half * 2 + last) * 2 + part) * size
                    rows = pl.ds(pl.multiple_of(at, size), size)
                    target[i, j] = dwq_ref[rows, :].astype(bf16)


def query_back_call(table, first, index, dq, own, other, logit_grad, router):
    width, count = first.shape
    topk = index.shape[0]
    tiles, head, wide = dq.shape
    padded = router.shape[1]
    spread = own.shape[1]
    keep = lambda shape: pl.BlockSpec(shape, lambda i, s: tuple(0 for _ in shape))
    columns = lambda n: pl.BlockSpec((n, TILE), lambda i, s: (0, i))
    shape = jax.ShapeDtypeStruct
    quarters = (2, 2, width // 8, spread)
    return pl.pallas_call(
        query_back_kernel,
        grid_spec=pltpu.PrefetchScalarGridSpec(
            num_scalar_prefetch=1,
            grid=(count // TILE,),
            in_specs=[
                columns(width),
                columns(topk),
                pl.BlockSpec((TILE // ROWS, head, wide), lambda i, s: (i, 0, 0)),
                keep(own.shape),
                keep(other.shape),
                columns(padded),
                keep(router.shape),
            ],
            out_specs=[columns(width), keep(quarters), keep(quarters), keep(router.shape)],
            scratch_shapes=[
                pltpu.VMEM((width, spread), bf16),
                pltpu.VMEM((spread, TILE), bf16),
                pltpu.VMEM((width, spread), f32),
                pltpu.VMEM(router.shape, f32),
            ],
        ),
        out_shape=[
            shape((width, count), f32),
            shape(quarters, bf16),
            shape(quarters, bf16),
            shape(router.shape, f32),
        ],
        compiler_params=params(),
        cost_estimate=cost(0),
        name="query_back",
    )(table, first, index, dq, own, other, logit_grad, router)


def first_back_kernel(pieces, table_ref, *refs):
    tokens_ref, first_ref, partial_ref, middle_grad_ref = refs[:4]
    sources = refs[4 : 4 + pieces]
    kv_weight_ref, gain_ref, rest_ref = refs[4 + pieces : 7 + pieces]
    refs = refs[7 + pieces :]
    outs = 4 if pieces > 1 else 1
    tokens_grad_refs = refs[:outs]
    keep_ref, send_ref, total_ref, gain_grad_ref, shift_grad_ref, dkv_ref = refs[outs:]
    step = pl.program_id(0)
    pair = kv_weight_ref.shape[1]

    @pl.when(step == 0)
    def _():
        total_ref[:, :pair] = jnp.zeros((total_ref.shape[0], pair), f32)
        for ref in (gain_grad_ref, shift_grad_ref):
            ref[...] = jnp.zeros(ref.shape, ref.dtype)

    unit, inverse = column_norm(tokens_ref[...].astype(f32).T)
    if pieces == 1:
        dkv_ref[...] = sources[0][...]
    else:
        low_ref, high_ref, own_ref = sources
        own = table_ref[OWN_SLOT]
        for chosen, ref, half in (
            (table_ref[LOW_SLOT], low_ref, 0),
            (table_ref[HIGH_SLOT], high_ref, 0),
            (own, own_ref, 0),
            (own + 1, own_ref, 1),
        ):

            @pl.when(step == chosen)
            def _():
                dkv_ref[...] = ref[half * PART : (half + 1) * PART, :]

    dkv = dkv_ref[...]
    total_ref[:, :pair] += dot(first_ref[...], dkv)
    first_grad = partial_ref[...] + dot_nt(kv_weight_ref[...], dkv)
    gain_grad_ref[...] += fold_lanes(first_grad * unit)
    shift_grad_ref[...] += fold_lanes(first_grad)
    total = middle_grad_ref[...] + column_norm_back(first_grad, unit, inverse, gain_ref[...])
    store_piece(step, tokens_grad_refs, total.T.astype(bf16))

    @pl.when(step == pl.num_programs(0) - 1)
    def _():
        lane = lax.broadcasted_iota(jnp.int32, rest_ref.shape, 1)
        gains = jnp.sum(gain_grad_ref[...], axis=1, keepdims=True)
        shifts = jnp.sum(shift_grad_ref[...], axis=1, keepdims=True)
        rest = jnp.where(lane == 0, gains, jnp.where(lane == 1, shifts, rest_ref[...]))
        total_ref[:, pair:] = rest
        size = keep_ref.shape[1]
        shard, core = table_ref[SHARD], table_ref[CORE]
        for target, last in ((keep_ref, core), (send_ref, 1 - core)):
            for i, half in enumerate((shard, 1 - shard)):
                rows = pl.ds(pl.multiple_of((half * 2 + last) * size, size), size)
                target[i] = total_ref[rows, :].astype(bf16)


def first_back_call(table, tokens, first, partial, middle_grad, dkv, kv_weight, gain, rest):
    count, width = tokens.shape
    pair = kv_weight.shape[1]
    wide = pair + rest.shape[1]
    columns = lambda n: pl.BlockSpec((n, TILE), lambda i, t: (0, i))
    rows = lambda n: pl.BlockSpec((TILE, n), lambda i, t: (i, 0))
    keep = lambda shape: pl.BlockSpec(shape, lambda i, t: tuple(0 for _ in shape))
    shape = jax.ShapeDtypeStruct
    quarters = (2, width // 4, wide)
    if len(dkv) > 1:
        outs = [(keep((TILE, width)), shape((TILE, width), bf16))] * 4
    else:
        outs = [(rows(width), shape((count, width), bf16))]
    outs += [(keep(quarters), shape(quarters, bf16))] * 2
    return pl.pallas_call(
        functools.partial(first_back_kernel, len(dkv)),
        grid_spec=pltpu.PrefetchScalarGridSpec(
            num_scalar_prefetch=1,
            grid=(count // TILE,),
            in_specs=[rows(width), columns(width), columns(width), columns(width)]
            + piece_specs(dkv)
            + [keep(kv_weight.shape), keep((width, 1)), keep(rest.shape)],
            out_specs=[x for x, _ in outs],
            scratch_shapes=[
                pltpu.VMEM((width, wide), f32),
                pltpu.VMEM((width, 128), f32),
                pltpu.VMEM((width, 128), f32),
                pltpu.VMEM((TILE, pair), bf16),
            ],
        ),
        out_shape=[x for _, x in outs],
        compiler_params=params(),
        cost_estimate=cost(7),
        name="first_back",
    )(table, tokens, first, partial, middle_grad, *dkv, kv_weight, gain, rest)


def after(value, *others):
    return lax.optimization_barrier((value,) + others)[0]


def other_half(value):
    return lax.ppermute(value, "shard", [(0, 1), (1, 0)])


def join(value, other):
    low = lax.axis_index("shard") == 0
    return jnp.concatenate([jnp.where(low, value, other), jnp.where(low, other, value)], axis=0)


def swap(value, mask):
    count = lax.axis_size("ctx")
    return lax.ppermute(value, "ctx", [(i, i ^ mask) for i in range(count)])


def bit_masks(count):
    return [1 << k for k in reversed(range(count.bit_length() - 1))]


def key_orders(count):
    masks = bit_masks(count)
    return masks, masks[:1] + masks[1:-1][::-1] + masks[-1:]


def slots_of(masks):
    return [sum(m for k, m in enumerate(masks) if j >> k & 1) for j in range(1 << len(masks))]


def gather_keys(shared):
    low_order, high_order = key_orders(lax.axis_size("ctx"))
    got = swap(shared, low_order[0])
    low = jnp.concatenate([shared[:PART], got[:PART]], axis=0)
    high = jnp.concatenate([shared[PART:], got[PART:]], axis=0)
    for low_mask, high_mask in zip(low_order[1:-1], high_order[1:-1]):
        low_got, high_got = swap(low, low_mask), swap(high, high_mask)
        low = jnp.concatenate([low, low_got], axis=0)
        high = jnp.concatenate([high, high_got], axis=0)
    return (low, swap(low, low_order[-1])), (high, swap(high, high_order[-1]))


def add_low(a, b):
    return (a.astype(f32) + b.astype(f32)).astype(bf16)


def step_down(total, mask):
    half = total.shape[0] // 2
    return total[:half], swap(total[half:].astype(bf16), mask)


def double(total, mask):
    other = swap(total, mask)
    low = (lax.axis_index("ctx") // mask) % 2 == 0
    return jnp.concatenate([jnp.where(low, total, other), jnp.where(low, other, total)], axis=0)


def home_plan(count, block):
    half = count // 2
    if block != 4 * PART or block * half != PROMPT or block != CLEN or half % 2:
        return None
    sends = [None] * count
    hops = [[], [], []]
    for a in range(half // 2):
        b = half - 1 - a
        p, q = a + half, b + half
        sends[a], sends[b] = (0, 1, 2, 3), (2, 3, 0, 1)
        sends[p] = sends[q] = (0, 3, 1, 2)
        hops[0] += [(a, b), (b, a)]
        hops[1] += [(a, p), (p, a), (b, q), (q, b)]
        hops[2] += [(a, q), (b, p), (p, a), (q, b)]
    places = [[(i, sends[i][0]), (i, sends[i][1]), None, None] for i in range(count)]
    for k, hop in enumerate(hops):
        for source, target in hop:
            places[target][k + 1] = (source, sends[source][k + 1])
    return sends, hops, places


def plan_rows(plan, count):
    sends, _, places = plan
    lower, prompt = HALF // PART, PROMPT // PART
    where = [[source * 4 + quarter for source, quarter in row] for row in places]
    low_slot = [next(k for k in range(4) if row[k] < lower) for row in where]
    high_slot = [next(k for k in range(4) if lower <= row[k] < prompt) for row in where]
    own_slot = [2 if i < count // 2 else 0 for i in range(count)]
    own_at = [[row[k] % 4, row[k + 1] % 4] for row, k in zip(where, own_slot)]
    low_slots, high_slots = (slots_of(masks) for masks in key_orders(count))
    rows = []
    for i in range(count):
        row = list(sends[i]) + [int(i < count // 2), low_slot[i], high_slot[i], own_slot[i]]
        row += [0, i % 2, i // 2 % 2]
        row += [x * PART + r for x in where[i] for r in range(0, PART, ROWS)]
        row += [where[i ^ m][low_slot[i ^ m]] for m in low_slots]
        row += [where[i ^ m][high_slot[i ^ m]] for m in high_slots]
        row += [prompt + x for x in own_at[i] + own_at[i ^ (count // 2)]]
        rows.append(row)
    return rows


def send_pieces(pieces, plan):
    got = [lax.ppermute(piece, "ctx", hop) for piece, hop in zip(pieces[1:], plan[1])]
    return pieces[0], pieces[1], *got


def send_back(pieces, plan):
    hops = [[(t, s) for s, t in hop] for hop in plan[1]]
    got = [lax.ppermute(piece, "ctx", hop) for piece, hop in zip(pieces[1:], hops)]
    return pieces[0], pieces[1], *got


def per_device(
    tokens,
    expert_index,
    first_gain,
    first_shift,
    router_weight,
    query_weight,
    key_weight,
    value_weight,
    output_weight,
    second_gain,
    second_shift,
    up_weight,
    up_bias,
    down_weight,
    down_bias,
    out_grad,
):
    groups, block, width = tokens.shape
    assert groups == 1 and lax.axis_size("shard") == 2
    count = lax.axis_size("ctx")
    me = lax.axis_index("ctx")
    shard = lax.axis_index("shard")
    experts = router_weight.shape[1]
    topk = expert_index.shape[-1]
    head = key_weight.shape[1]
    pair = 2 * head
    padded = 32
    tiles = block // ROWS
    key_table = BASES + tiles
    plan = home_plan(count, block)
    if plan:
        table = jnp.array(plan_rows(plan, count), jnp.int32)[me]
        table = table + shard * (jnp.arange(table.shape[0], dtype=jnp.int32) == SHARD)
        packed = pack_call(table, tokens[0], expert_index[0].T)
        sources = send_pieces(packed, plan)
        key_weight, packed = lax.optimization_barrier((key_weight, packed))
    else:
        base = me * block
        numbers = [0, 0, 0, 0, 0, 0, 0, 0, shard, me % 2, me // 2 % 2]
        table = jnp.concatenate(
            [
                jnp.stack([jnp.int32(x) for x in numbers]),
                base + jnp.arange(tiles, dtype=jnp.int32) * ROWS,
                jnp.arange((PROMPT + CLEN) // PART, dtype=jnp.int32),
            ]
        )
        sources = (tokens[0],)

    spare = jnp.zeros((key_weight.shape[0], padded - experts), bf16)
    vectors = [first_gain, first_shift, second_gain, second_shift, down_bias]
    half_width = width // 2
    small = jnp.concatenate(
        [key_weight, value_weight, router_weight, spare]
        + [v[:, None] for v in vectors]
        + [up_bias.reshape(half_width, -1)],
        axis=1,
    )
    small = join(small, other_half(small))
    query_other = other_half(after(query_weight, small))
    kv_weight = small[:, :pair]
    router = small[:, pair : pair + padded]
    at = pair + padded
    columns = [small[:, at + i : at + i + 1].astype(f32) for i in range(len(vectors))]
    gain_one, shift_one, gain_two, shift_two, down_bias_all = columns
    up_bias_all = small[:, at + len(vectors) :].reshape(-1, 1).astype(f32)

    both_weights = jnp.concatenate([output_weight, down_weight], axis=0)
    early_work = (both_weights, router, up_bias_all, *columns)
    if plan:
        grads = pack_call(after(table, small), out_grad[0])
        early_work += tuple(grads)
    table, early_work = lax.optimization_barrier((table, early_work))
    both_weights, router, up_bias_all, *rest = early_work
    gain_one, shift_one, gain_two, shift_two, down_bias_all = rest[: len(vectors)]
    grads = rest[len(vectors) :]
    first_out = first_call(table, sources, block, topk, gain_one, shift_one, kv_weight)
    if plan:
        first, shared, own, index, flat = first_out
        low_keys, high_keys = gather_keys(shared)
        partner = swap(own, count // 2)
        high_keys += (own, partner)
    else:
        first, kv = first_out
        flat = tokens[0]
        index = expert_index[0].T
        gathered = lax.all_gather(kv, "ctx", axis=0, tiled=True)
        segment = jnp.maximum(base, PROMPT) // CLEN * CLEN
        own = lax.dynamic_slice_in_dim(gathered, segment, CLEN, 0)
        quarter = HALF // 2
        low_keys = (gathered[:quarter], gathered[quarter:HALF])
        high_keys = (
            gathered[HALF : HALF + quarter], gathered[HALF + quarter : PROMPT],
            own[: CLEN // 2], own[CLEN // 2 :],
        )

    qt, q, gate = query_call(table, first, query_weight, query_other, router, index, head)
    both_other = other_half(after(both_weights, query_other))
    weights = (
        output_weight, down_weight, both_other, up_weight, other_half(after(up_weight, query_other))
    )
    if plan:
        grads = send_pieces(after(tuple(grads), *low_keys, *high_keys), plan)
    else:
        grads = (out_grad[0],)
    keys = low_keys + high_keys
    attended, lse = attend_call(key_table, keys, table, qt)
    outs = 4 if plan else 1
    middle = middle_call(
        table, grads, flat, index, gate, attended, weights,
        gain_two, shift_two, up_bias_all, down_bias_all, padded,
    )
    layer_out = middle[:outs]
    (
        middle_grad, grad_t, grad_rows, delta, logit_grad,
        output_weight_grad, up_weight_grad, down_weight_grad,
        second_gain_grad, second_shift_grad, up_bias_grad, down_bias_grad,
    ) = middle[outs:]

    early = lax.psum((output_weight_grad, up_weight_grad, down_weight_grad), ("ctx", "shard"))
    if plan:
        layer_out = send_back(layer_out, plan)
    kinds = (f32, bf16, f32, bf16, f32, bf16) if plan else (bf16,) * 6
    dq, *key_grads = attend_back_call(
        key_table, keys, kinds, table, qt, q, grad_t, grad_rows, lse, delta
    )
    dq, key_grads, layer_out = lax.optimization_barrier((dq, key_grads, layer_out))
    if plan:
        low_near, low_far, high_near, high_far, own_near, own_far = key_grads
        low_got, high_got = swap(low_far, 1), swap(high_far, 1)
    partial, keep, send, router_grad = query_back_call(
        table, first, index, dq, query_weight, query_other, logit_grad, router
    )
    keep, send, router_grad, partial, *early = lax.optimization_barrier(
        (keep, send, router_grad, partial, *early)
    )
    total = add_low(keep, swap(send, 1))
    if plan:
        low_order, high_order = key_orders(count)
        low_keep, low_got = step_down(low_near + low_got.astype(f32), low_order[2])
        high_keep, high_got = step_down(high_near + high_got.astype(f32), high_order[2])
        query_got = other_half(total[1])
    sums = (second_gain_grad, second_shift_grad, down_bias_grad, up_bias_grad)
    total, layer_out, *sums = lax.optimization_barrier((total, layer_out, *sums))
    second_gain_grad, second_shift_grad, down_bias_grad, up_bias_grad = sums
    rest = jnp.concatenate(
        [
            jnp.zeros((width, 2), f32),
            jnp.sum(second_gain_grad, axis=1)[:, None],
            jnp.sum(second_shift_grad, axis=1)[:, None],
            down_bias_grad[0][:, None],
            jnp.sum(up_bias_grad, axis=1).reshape(width, -1),
        ],
        axis=1,
    )
    bias_columns = rest.shape[1] - 5
    rest = jnp.pad(rest, ((0, 0), (0, padded - rest.shape[1])))
    rest = jnp.concatenate([rest, router_grad, jnp.zeros((width, 128 - 2 * padded), f32)], axis=1)
    if plan:
        low_got, high_got, total, own_far = lax.optimization_barrier(
            (low_got, high_got, total, own_far)
        )
        own_got = swap(own_far, count // 2)
        low_keep, low_got = step_down(low_keep + low_got.astype(f32), low_order[1])
        high_keep, high_got = step_down(high_keep + high_got.astype(f32), high_order[1])
        low_got, high_got = lax.optimization_barrier((low_got, high_got))
        low_sum = low_keep + low_got.astype(f32)
        high_sum = high_keep + high_got.astype(f32)
        both = jnp.concatenate([low_sum[PART:], high_sum[PART:]], axis=0).astype(bf16)
        both = swap(both, low_order[0])
        total = add_low(total[0], query_got)
        query_got = swap(total[1], 2)
        both, total = lax.optimization_barrier((both, total))
        dkv = (
            add_low(low_sum[:PART], both[:PART]),
            add_low(high_sum[:PART], both[PART:]),
            add_low(own_near, own_got),
        )
    else:
        rows = count * block - PROMPT
        dall = jnp.concatenate(key_grads[:4] + [jnp.zeros((rows, pair), bf16)])
        own_grad = jnp.concatenate(key_grads[4:])
        own_grad = jnp.where(base >= PROMPT, own_grad, jnp.zeros_like(own_grad))
        dall = lax.dynamic_update_slice_in_dim(dall, own_grad, segment, 0)
        dkv = (lax.psum_scatter(dall, "ctx", scatter_dimension=0, tiled=True),)
        total = add_low(total[0], other_half(total[1]))
        query_got = swap(total[1], 2)
    done = first_back_call(
        table, flat, first, partial, middle_grad, dkv, kv_weight, gain_one, rest
    )
    tokens_grad = done[:outs]
    keep, send = done[outs:]
    small_sum = add_low(keep, swap(send, 1))
    small_sum = add_low(small_sum[0], other_half(small_sum[1]))
    small_sum = add_low(small_sum, swap(small_sum, 2))
    total = add_low(total[0], query_got)
    for mask in bit_masks(count)[:-2][::-1]:
        got, small_got = swap(total, mask), swap(small_sum, mask)
        total, small_sum = add_low(total, got), add_low(small_sum, small_got)
    if plan:
        tokens_grad = send_back(tokens_grad, plan)
    query_weight_grad = double(double(total, 2), 1).astype(f32)
    small_grad = double(small_sum, 1).astype(f32)
    layer_out = unpack_call(table, layer_out) if plan else layer_out[0]
    tokens_grad = unpack_call(table, tokens_grad) if plan else tokens_grad[0]
    output_weight_grad, up_weight_grad, down_weight_grad = (
        lax.dynamic_slice_in_dim(x, shard * (x.shape[0] // 2), x.shape[0] // 2, 0).astype(f32)
        for x in early
    )
    return (
        layer_out[None],
        tokens_grad[None],
        small_grad[:, pair],
        small_grad[:, pair + 1],
        small_grad[:, pair + padded : pair + padded + experts],
        query_weight_grad,
        small_grad[:, :head],
        small_grad[:, head:pair],
        output_weight_grad,
        small_grad[:, pair + 2],
        small_grad[:, pair + 3],
        up_weight_grad,
        small_grad[:, pair + 5 : pair + 5 + bias_columns].reshape(-1),
        down_weight_grad,
        small_grad[:, pair + 4],
    )


def solution(mesh):
    split = P("shard", "ctx", None)
    vector = P("shard")
    matrix = P("shard", None)
    in_specs = (
        split, split, vector, vector, matrix, matrix, matrix, matrix, matrix,
        vector, vector, matrix, vector, matrix, vector, split,
    )
    out_specs = (
        split, split, vector, vector, matrix, matrix, matrix, matrix, matrix,
        vector, vector, matrix, vector, matrix, vector,
    )
    return jax.shard_map(
        per_device, mesh=mesh, in_specs=in_specs, out_specs=out_specs, check_vma=False
    )
```

time: 578 us -> 494 us (0.85); the launches traced: 569 us -> 492 us
  waiting for transfers between devices: 96.1 us -> 68.9 us
  local copies, waits for them, and re-layouts: 36.2 us -> 14.8 us
  between operations: 33.1 us -> 15 us
  other arithmetic: 35.2 us -> 24.8 us
  Pallas kernels: 309 us -> 317 us
  starting transfers between devices: 59.4 us -> 52.2 us
    ppermute x22 -> x27, waiting for transfers between devices: 67.5 us -> 52.4 us  [swap(): return lax.ppermute(value, 'ctx', [(i, i ^ mask) for i in range(count)])]
    ppermute x12, waiting for transfers between devices: 26.4 us -> 12.5 us  [the longest x6 12.5 us: send_pieces(): lax.ppermute(piece, 'ctx', hop)]
    pallas_call x7 -> x9, Pallas kernels: 288 us -> 296 us  [the longest x1 159 us: attend_back_call(): pl.pallas_call(functools.partial(attend_back_kernel, start, len(sources))...]
    ppermute x12, starting transfers between devices: 31.1 us -> 24.3 us  [the longest x6 14.3 us: send_pieces(): lax.ppermute(piece, 'ctx', hop)]
    dynamic_slice x11 -> x0, local copies, waits for them, and re-layouts: 5.95 us -> none  [the longest x2 2.58 us: exchange(): lax.dynamic_slice_in_dim(value, starts[k], size, 0)]
    ppermute x22 -> x27, starting transfers between devices: 21 us -> 19.9 us  [swap(): return lax.ppermute(value, 'ctx', [(i, i ^ mask) for i in range(count)])]
  transfers between devices with their start and end apart: 42 -> 46, of which waited for: 15 -> 16; matrix products, arithmetic and copies ran while one was open for 11% -> 6% of each run, Pallas kernels for 46% -> 51%
where the time goes in v3:
time: 494 us; the launch traced here: 492 us
  Pallas kernels  317 us (64%)
  waiting for transfers between devices  68.9 us (14%)
  starting transfers between devices  52.2 us (11%)
  other arithmetic  24.8 us (5%)
  between operations  15 us (3%)
  local copies, waits for them, and re-layouts  14.8 us (3%)
    pallas_call x1, Pallas kernels, attend_back_call(): pl.pallas_call(functools.partial(attend_back_kernel, start, len(sources))...  159 us
    pallas_call x1, Pallas kernels, attend_call(): pl.pallas_call(functools.partial(attend_kernel, start, len(sources)), gri...  62.3 us
    ppermute x27, waiting for transfers between devices, swap(): return lax.ppermute(value, 'ctx', [(i, i ^ mask) for i in range(count)])  52.4 us
    pallas_call x1, Pallas kernels, middle_call(): pl.pallas_call(functools.partial(middle_kernel, len(sources)), grid_spec=...  48.5 us
    ppermute x27, starting transfers between devices, swap(): return lax.ppermute(value, 'ctx', [(i, i ^ mask) for i in range(count)])  19.9 us
    ppermute x6, starting transfers between devices, send_pieces(): lax.ppermute(piece, 'ctx', hop)  14.3 us
    ppermute x6, waiting for transfers between devices, send_pieces(): lax.ppermute(piece, 'ctx', hop)  12.5 us
    pallas_call x1, Pallas kernels, query_back_call(): pl.pallas_call(query_back_kernel, grid_spec=pltpu.PrefetchScalarGridSpec(...  10.4 us
  transfers between devices with their start and end apart: 46, of which 16 were waited for; matrix products, arithmetic and copies ran while one was open for 6% of the time, Pallas kernels for 51%

profile of v3, /device:TPU:0, one launch (start us, length us, event | category | flops | bytes accessed | tf_op | source)
XLA Modules:
  0.0 492.3 jit_solution(5413053957392511832)
XLA Ops:
  7.2 1.2 fusion.21.table_ref
  8.5 3.1 pack.2
  11.6 5.4 %collective-permute-start.1 = (bf16[272,512]{1,0:T(8,128)(2,1)}, bf16[272,512]{1,0:T(8,128)(2,1)S(1)}, u32[]{:S(2)}, u32[]{:S(2)}) collective-permute-start(bf16[272,512]{1,0:T(8,128)(2,1)} %get-tuple-element.126.refs_1_), channel_id=1, source_target_pairs={{0,14},{14,0},{2,12},{12,2},{4,10},{10,4},{6,8},{8,6},{1,15},{15,1... | collective-permute-start | bytes 835592 | tf_op jit(solution)/shard_map/ppermute | solution.py:1068
  17.1 2.1 collective-permute-start.3
  20.6 2.3 collective-permute-start
  22.8 1.3 pad_maximum_fusion
  24.1 2.9 collective-permute-done
  27.1 2.9 pack.3
  30.9 1.3 fusion.15
  32.9 6.5 %collective-permute-done.2.refs_3_ = bf16[272,512]{1,0:T(8,128)(2,1)} collective-permute-done((bf16[272,512]{1,0:T(8,128)(2,1)}, bf16[272,512]{1,0:T(8,128)(2,1)}, u32[]{:S(2)}, u32[]{:S(2)}) %collective-permute-start.2) | collective-permute-done | bytes 278560 | tf_op jit(solution)/shard_map/ppermute | solution.py:1068
  39.4 5.9 %collective-permute-done.3.refs_4_ = bf16[272,512]{1,0:T(8,128)(2,1)} collective-permute-done((bf16[272,512]{1,0:T(8,128)(2,1)}, bf16[272,512]{1,0:T(8,128)(2,1)}, u32[]{:S(2)}, u32[]{:S(2)}) %collective-permute-start.3) | collective-permute-done | bytes 278560 | tf_op jit(solution)/shard_map/ppermute | solution.py:1068
  45.3 6.0 %first_norm.1 = (bf16[512,1024]{1,0:T(8,128)(2,1)}, bf16[512,128]{1,0:T(8,128)(2,1)}, bf16[512,128]{1,0:T(8,128)(2,1)}, s32[8,1024]{1,0:T(8,128)}, bf16[1024,512]{1,0:T(8,128)(2,1)}) custom-call(s32[55]{0:T(128)} %fusion.21.table_ref, bf16[272,512]{1,0:T(8,128)(2,1)} %get-tuple-element.125.refs_0_, bf16[272,512]{1,0:T(8,128)(2,1)} %get-tuple-element.126.refs_1_, ...), custom_call_target="tpu_custom_call" | custom-call | flops 5750000128 | tf_op jit(solution)/shard_map/first_norm/pallas_call | solution.py:233
  52.4 5.7 %collective-permute-done.4 = bf16[512,128]{1,0:T(8,128)(2,1)S(1)} collective-permute-done((bf16[512,128]{1,0:T(8,128)(2,1)}, bf16[512,128]{1,0:T(8,128)(2,1)S(1)}, u32[]{:S(2)}, u32[]{:S(2)}) %collective-permute-start.4) | collective-permute-done | bytes 131104 | tf_op jit(solution)/shard_map/ppermute | solution.py:982
  58.2 1.6 collective-permute-start.12
  60.4 2.7 collective-permute-done.5
  63.3 2.5 collective-permute-done.8
  66.5 2.4 collective-permute-start.9
  68.9 1.3 copy.76.refs_16_
  70.5 1.0 pad_maximum_fusion.2.refs_0_
  71.6 3.1 collective-permute-done.9
  74.8 1.0 pad_maximum_fusion.3.refs_2_
  75.9 1.2 collective-permute-done.12.other_ref
  77.0 1.5 collective-permute-start.16
  79.1 10.4 %queries.1 = (bf16[8,64,1024]{2,1,0:T(8,128)(2,1)}, bf16[8,1024,64]{2,1,0:T(8,128)(2,1)}, f32[8,1024]{1,0:T(8,128)}) custom-call(s32[55]{0:T(128)} %fusion.21.table_ref, bf16[512,1024]{1,0:T(8,128)(2,1)} %get-tuple-element.138.first_ref.refs_1_, bf16[256,1536]{1,0:T(8,128)(2,1)} %own_ref.3, bf16[256,1536]{1,0:T(8,128)(2,1)} %collective-permute-done.12.other_ref, ...), custom_call_target="tpu_custom_call" | custom-call | flops 11500000256 | tf_op jit(solution)/shard_map/queries/pallas_call | solution.py:297
  89.5 1.9 collective-permute-start.13
  91.5 4.7 collective-permute-start.15
  96.2 62.3 %attend.1 = (f32[8,64,1024]{2,1,0:T(8,128)}, f32[8,1,1024]{2,1,0:T(1,128)}) custom-call(s32[55]{0:T(128)} %fusion.21.table_ref, bf16[2048,128]{1,0:T(8,128)(2,1)} %copy-done.7, bf16[2048,128]{1,0:T(8,128)(2,1)} %collective-permute-done.7.refs_1_, bf16[2048,128]{1,0:T(8,128)(2,1)} %copy-done.8, bf16[2048,128]{1,0:T(8,128)(2,1)} %collective-permute-done.10.refs_3_, ...), custom_call_target="tpu_custom_call" | custom-call | flops 73600000000 | tf_op jit(solution)/shard_map/attend/pallas_call | solution.py:434
  159.8 48.5 %middle.1 = (bf16[256,512]{1,0:T(8,128)(2,1)}, bf16[256,512]{1,0:T(8,128)(2,1)}, bf16[256,512]{1,0:T(8,128)(2,1)}, bf16[256,512]{1,0:T(8,128)(2,1)}, f32[512,102...) custom-call(s32[55]{0:T(128)} %fusion.21.table_ref, ...), custom_call_target="tpu_custom_call" | custom-call | flops 50600001536 | tf_op jit(solution)/shard_map/middle/pallas_call | solution.py:743
  208.3 1.9 collective-permute-start.18
  210.3 2.9 collective-permute-start.20
  213.3 158.9 %attend_back.1 = (f32[8,64,1024]{2,1,0:T(8,128)}, f32[2048,128]{1,0:T(8,128)}, bf16[2048,128]{1,0:T(8,128)(2,1)}, f32[2048,128]{1,0:T(8,128)}, bf16[2048,128]{1,...) custom-call(s32[55]{0:T(128)} %fusion.21.table_ref, bf16[2048,128]{1,0:T(8,128)(2,1)} %copy-done.7, ...), custom_call_target="tpu_custom_call" | custom-call | flops 184000004096 | tf_op jit(solution)/shard_map/attend_back/pallas_call | solution.py:524
  372.9 10.4 %query_back.1 = (f32[512,1024]{1,0:T(8,128)}, bf16[2,2,64,1536]{3,2,1,0:T(8,128)(2,1)}, bf16[2,2,64,1536]{3,2,1,0:T(8,128)(2,1)}, f32[512,32]{1,0:T(8,128)}) custom-call(s32[55]{0:T(128)} %fusion.21.table_ref, bf16[512,1024]{1,0:T(8,128)(2,1)} %get-tuple-element.138.first_ref.refs_1_, s32[8,1024]{1,0:T(8,128)} %get-tuple-element.139.index_ref.refs_6_, ...), custom_call_target="tpu_custom_call" | custom-call | tf_op jit(solution)/shard_map/query_back/pallas_call | solution.py:839
  383.3 1.2 convert_add_fusion.1
  386.4 1.7 collective-permute-start.25
  388.1 1.4 dynamic-slice_convert_fusion.2
  389.5 1.6 dynamic-slice_convert_fusion
  391.9 1.6 dynamic-slice_convert_fusion.1
  395.1 1.0 slice_add_fusion.1
  396.8 1.6 collective-permute-start.26
  399.1 1.0 collective-permute-start.27
  400.1 1.5 collective-permute-start.29
  401.6 1.0 collective-permute-start.30
  403.4 1.6 reduce_sum.29
  405.6 1.8 fusion.2.refs_9_
  407.5 1.0 slice_add_fusion.2
  408.5 2.0 collective-permute-start.28
  410.5 1.6 add_convert_fusion.4.refs_6_
  412.1 1.1 fusion
  413.1 3.1 collective-permute-done.28
  416.9 7.9 %first_back.1 = (bf16[256,512]{1,0:T(8,128)(2,1)}, bf16[256,512]{1,0:T(8,128)(2,1)}, bf16[256,512]{1,0:T(8,128)(2,1)}, bf16[256,512]{1,0:T(8,128)(2,1)}, bf16[2,...) custom-call(s32[55]{0:T(128)} %fusion.21.table_ref, bf16[1024,512]{1,0:T(8,128)(2,1)} %get-tuple-element.154.refs_5_.refs_0_, ...), custom_call_target="tpu_custom_call" | custom-call | flops 8049999872 | tf_op jit(solution)/shard_map/first_back/pallas_call | solution.py:944
  425.0 3.1 unpack.2
  428.7 2.2 collective-permute-start.31
  431.0 2.9 collective-permute-start.33
  434.3 1.7 collective-permute-start.36
  436.0 15.9 %collective-permute-done.40 = bf16[64,1536]{1,0:T(8,128)(2,1)S(1)} collective-permute-done((bf16[64,1536]{1,0:T(8,128)(2,1)S(1)}, bf16[64,1536]{1,0:T(8,128)(2,1)S(1)}, u32[]{:S(2)}, u32[]{:S(2)}) %collective-permute-start.40) | collective-permute-done | bytes 196640 | tf_op jit(solution)/shard_map/ppermute | solution.py:982
  452.7 1.5 collective-permute-start.37
  455.1 3.0 unpack.3
  458.5 1.9 collective-permute-start.38
  460.4 1.2 collective-permute-start.42
  461.6 8.4 %collective-permute-done.38 = bf16[128,256]{1,0:T(8,128)(2,1)S(1)} collective-permute-done((bf16[128,256]{1,0:T(8,128)(2,1)S(1)}, bf16[128,256]{1,0:T(8,128)(2,1)S(1)}, u32[]{:S(2)}, u32[]{:S(2)}) %collective-permute-start.38) | collective-permute-done | bytes 65568 | tf_op jit(solution)/shard_map/ppermute | solution.py:982
  470.1 3.3 collective-permute-done.42
  473.9 5.9 %collective-permute-done.43 = bf16[64,1536]{1,0:T(8,128)(2,1)S(1)} collective-permute-done((bf16[64,1536]{1,0:T(8,128)(2,1)S(1)}, bf16[64,1536]{1,0:T(8,128)(2,1)S(1)}, u32[]{:S(2)}, u32[]{:S(2)}) %collective-permute-start.43) | collective-permute-done | bytes 196640 | tf_op jit(solution)/shard_map/ppermute | solution.py:982
  483.1 1.0 slice_reduce_fusion
  484.2 1.3 maximum_convert_fusion
  (196 shorter events, 23.4 us)
Async XLA Ops:
  7.2 379.0 %all-reduce.4.cloned.1.call-start = ((), (), s32[]{:S(2)}) async-start(), calls=%async_computation | async-start | bytes 11534336 | tf_op jit(solution)/shard_map/psum | solution.py:1197
  8.4 10.7 %copy-start.15 = (bf16[256,64]{0,1:T(8,128)(2,1)S(1)}, bf16[256,64]{0,1:T(8,128)(2,1)}, u32[]{:S(2)}) copy-start(bf16[256,64]{0,1:T(8,128)(2,1)} %param.23) | copy-start | bytes 98308
  8.4 10.9 %copy-start.16 = (bf16[256,64]{0,1:T(8,128)(2,1)S(1)}, bf16[256,64]{0,1:T(8,128)(2,1)}, u32[]{:S(2)}) copy-start(bf16[256,64]{0,1:T(8,128)(2,1)} %param.24) | copy-start | bytes 98308
  8.4 11.0 %copy-start.17 = (bf16[256,24]{0,1:T(8,128)(2,1)S(1)}, bf16[256,24]{0,1:T(8,128)(2,1)}, u32[]{:S(2)}) copy-start(bf16[256,24]{0,1:T(8,128)(2,1)} %param.21) | copy-start | bytes 36868
  8.4 11.1 %copy-start.20 = (bf16[256]{0:T(256)(128)(2,1)S(1)}, bf16[256]{0:T(256)(128)(2,1)}, u32[]{:S(2)}) copy-start(bf16[256]{0:T(256)(128)(2,1)} %param.19) | copy-start | bytes 1540
  8.4 11.2 %copy-start.21 = (bf16[256]{0:T(256)(128)(2,1)S(1)}, bf16[256]{0:T(256)(128)(2,1)}, u32[]{:S(2)}) copy-start(bf16[256]{0:T(256)(128)(2,1)} %param.20) | copy-start | bytes 1540
  8.5 11.3 %copy-start.22 = (bf16[256]{0:T(256)(128)(2,1)S(1)}, bf16[256]{0:T(256)(128)(2,1)}, u32[]{:S(2)}) copy-start(bf16[256]{0:T(256)(128)(2,1)} %param.26) | copy-start | bytes 1540
  8.5 11.4 %copy-start.23 = (bf16[256]{0:T(256)(128)(2,1)S(1)}, bf16[256]{0:T(256)(128)(2,1)}, u32[]{:S(2)}) copy-start(bf16[256]{0:T(256)(128)(2,1)} %param.27) | copy-start | bytes 1540
  8.5 11.5 %copy-start.24 = (bf16[256]{0:T(256)(128)(2,1)S(1)}, bf16[256]{0:T(256)(128)(2,1)}, u32[]{:S(2)}) copy-start(bf16[256]{0:T(256)(128)(2,1)} %param.31) | copy-start | bytes 1540
  8.5 11.6 %copy-start.19 = (bf16[1024]{0:T(1024)(128)(2,1)S(1)}, bf16[1024]{0:T(1024)(128)(2,1)}, u32[]{:S(2)}) copy-start(bf16[1024]{0:T(1024)(128)(2,1)} %param.29) | copy-start | bytes 6148
  11.6 11.3 %copy-start = (bf16[1024,512]{1,0:T(8,128)(2,1)S(1)}, bf16[1024,512]{1,0:T(8,128)(2,1)}, u32[]{:S(2)}) copy-start(bf16[1024,512]{1,0:T(8,128)(2,1)} %refs_10_.1) | copy-start | bytes 3145732
  11.6 21.3 %collective-permute-start.1 = (bf16[272,512]{1,0:T(8,128)(2,1)}, bf16[272,512]{1,0:T(8,128)(2,1)S(1)}, u32[]{:S(2)}, u32[]{:S(2)}) collective-permute-start(bf16[272,512]{1,0:T(8,128)(2,1)} %get-tuple-element.126.refs_1_), channel_id=1, source_target_pairs={{0,14},{14,0},{2,12},{12,2},{4,10},{10,4},{6,8},{8,6},{1,15},{15,1... | collective-permute-start | bytes 835592 | tf_op jit(solution)/shard_map/ppermute | solution.py:1068
  17.0 22.4 %collective-permute-start.2 = (bf16[272,512]{1,0:T(8,128)(2,1)}, bf16[272,512]{1,0:T(8,128)(2,1)}, u32[]{:S(2)}, u32[]{:S(2)}) collective-permute-start(bf16[272,512]{1,0:T(8,128)(2,1)} %get-tuple-element.127), channel_id=1, source_target_pairs={{0,16},{16,0},{14,30},{30,14},{2,18},{18,2},{12,28},{28,12},{4,20}... | collective-permute-start | bytes 835592 | tf_op jit(solution)/shard_map/ppermute | solution.py:1068
  17.1 28.2 %collective-permute-start.3 = (bf16[272,512]{1,0:T(8,128)(2,1)}, bf16[272,512]{1,0:T(8,128)(2,1)}, u32[]{:S(2)}, u32[]{:S(2)}) collective-permute-start(bf16[272,512]{1,0:T(8,128)(2,1)} %get-tuple-element.128), channel_id=1, source_target_pairs={{0,30},{14,16},{16,0},{30,14},{2,28},{12,18},{18,2},{28,12},{4,26}... | collective-permute-start | bytes 835592 | tf_op jit(solution)/shard_map/ppermute | solution.py:1068
  20.6 6.4 %collective-permute-start = (bf16[256,169]{1,0:T(8,128)(2,1)S(1)}, bf16[256,169]{1,0:T(8,128)(2,1)S(1)}, u32[]{:S(2)}, u32[]{:S(2)}) collective-permute-start(bf16[256,169]{1,0:T(8,128)(2,1)S(1)} %concatenate.51), channel_id=1, source_target_pairs={{0,1},{1,0},{2,3},{3,2},{4,5},{5,4},{6,7},{7,6},{8,9},{9,8},{10,11... | collective-permute-start | bytes 259592 | tf_op jit(solution)/shard_map/ppermute | solution.py:972
  32.9 25.3 %copy-start.3 = (bf16[256,1536]{1,0:T(8,128)(2,1)S(1)}, bf16[256,1536]{1,0:T(8,128)(2,1)}, u32[]{:S(2)}) copy-start(bf16[256,1536]{1,0:T(8,128)(2,1)} %own_ref.3) | copy-start | bytes 2359300
  32.9 12.5 %copy-start.26 = (bf16[272,512]{1,0:T(8,128)(2,1)}, bf16[272,512]{1,0:T(8,128)(2,1)S(1)}, u32[]{:S(2)}) copy-start(bf16[272,512]{1,0:T(8,128)(2,1)S(1)} %collective-permute-done.1.refs_2_) | copy-start | bytes 835588
  51.4 6.7 %collective-permute-start.4 = (bf16[512,128]{1,0:T(8,128)(2,1)}, bf16[512,128]{1,0:T(8,128)(2,1)S(1)}, u32[]{:S(2)}, u32[]{:S(2)}) collective-permute-start(bf16[512,128]{1,0:T(8,128)(2,1)} %get-tuple-element.140), channel_id=1, source_target_pairs={{0,16},{2,18},{4,20},{6,22},{8,24},{10,26},{12,28},{14,30},{16,0},... | collective-permute-start | bytes 393224 | tf_op jit(solution)/shard_map/ppermute | solution.py:982
  58.1 5.0 %collective-permute-start.5 = (bf16[512,128]{1,0:T(8,128)(2,1)S(1)}, bf16[512,128]{1,0:T(8,128)(2,1)S(1)}, u32[]{:S(2)}, u32[]{:S(2)}) collective-permute-start(bf16[512,128]{1,0:T(8,128)(2,1)S(1)} %pad_maximum_fusion.7), channel_id=1, source_target_pairs={{0,8},{2,10},{4,12},{6,14},{8,0},{10,2},{12,4},{14,6},{16,24},{18,... | collective-permute-start | bytes 393224 | tf_op jit(solution)/shard_map/ppermute | solution.py:982
  58.2 18.9 %collective-permute-start.12 = (bf16[256,1536]{1,0:T(8,128)(2,1)S(1)}, bf16[256,1536]{1,0:T(8,128)(2,1)}, u32[]{:S(2)}, u32[]{:S(2)}) collective-permute-start(bf16[256,1536]{1,0:T(8,128)(2,1)S(1)} %copy-done.3), channel_id=1, source_target_pairs={{0,1},{1,0},{2,3},{3,2},{4,5},{5,4},{6,7},{7,6},{8,9},{9,8},{10,11... | collective-permute-start | bytes 2359304 | tf_op jit(solution)/shard_map/ppermute | solution.py:972
  59.8 6.0 %collective-permute-start.8 = (bf16[512,128]{1,0:T(8,128)(2,1)S(1)}, bf16[512,128]{1,0:T(8,128)(2,1)S(1)}, u32[]{:S(2)}, u32[]{:S(2)}) collective-permute-start(bf16[512,128]{1,0:T(8,128)(2,1)S(1)} %pad_maximum_fusion.8), channel_id=1, source_target_pairs={{0,4},{2,6},{4,0},{6,2},{8,12},{10,14},{12,8},{14,10},{16,20},{18,... | collective-permute-start | bytes 393224 | tf_op jit(solution)/shard_map/ppermute | solution.py:982
  63.1 7.4 %collective-permute-start.6 = (bf16[1024,128]{1,0:T(8,128)(2,1)S(1)}, bf16[1024,128]{1,0:T(8,128)(2,1)}, u32[]{:S(2)}, u32[]{:S(2)}) collective-permute-start(bf16[1024,128]{1,0:T(8,128)(2,1)S(1)} %pad_maximum_fusion.5), channel_id=1, source_target_pairs={{0,4},{2,6},{4,0},{6,2},{8,12},{10,14},{12,8},{14,10},{16,20},{18,... | collective-permute-start | bytes 786440 | tf_op jit(solution)/shard_map/ppermute | solution.py:982
  66.5 8.3 %collective-permute-start.9 = (bf16[1024,128]{1,0:T(8,128)(2,1)}, bf16[1024,128]{1,0:T(8,128)(2,1)}, u32[]{:S(2)}, u32[]{:S(2)}) collective-permute-start(bf16[1024,128]{1,0:T(8,128)(2,1)} %pad_maximum_fusion.6), channel_id=1, source_target_pairs={{0,8},{2,10},{4,12},{6,14},{8,0},{10,2},{12,4},{14,6},{16,24},{18,... | collective-permute-start | bytes 786440 | tf_op jit(solution)/shard_map/ppermute | solution.py:982
  70.3 19.2 %collective-permute-start.11 = (bf16[512,128]{1,0:T(8,128)(2,1)}, bf16[512,128]{1,0:T(8,128)(2,1)}, u32[]{:S(2)}, u32[]{:S(2)}) collective-permute-start(bf16[512,128]{1,0:T(8,128)(2,1)} %get-tuple-element.141.refs_4_), channel_id=1, source_target_pairs={{0,16},{2,18},{4,20},{6,22},{8,24},{10,26},{12,28},{14,30},{16,0},... | collective-permute-start | bytes 393224 | tf_op jit(solution)/shard_map/ppermute | solution.py:982
  71.5 17.9 %copy-start.7 = (bf16[2048,128]{1,0:T(8,128)(2,1)}, bf16[2048,128]{1,0:T(8,128)(2,1)S(1)}, u32[]{:S(2)}) copy-start(bf16[2048,128]{1,0:T(8,128)(2,1)S(1)} %pad_maximum_fusion.2.refs_0_) | copy-start | bytes 1572868
  71.6 17.9 %collective-permute-start.7 = (bf16[2048,128]{1,0:T(8,128)(2,1)S(1)}, bf16[2048,128]{1,0:T(8,128)(2,1)}, u32[]{:S(2)}, u32[]{:S(2)}) collective-permute-start(bf16[2048,128]{1,0:T(8,128)(2,1)S(1)} %pad_maximum_fusion.2.refs_0_), channel_id=1, source_target_pairs={{0,2},{2,0},{4,6},{6,4},{8,10},{10,8},{12,14},{14,12},{16,18},{18,... | collective-permute-start | bytes 1572872 | tf_op jit(solution)/shard_map/ppermute | solution.py:982
  75.8 13.7 %copy-start.8 = (bf16[2048,128]{1,0:T(8,128)(2,1)}, bf16[2048,128]{1,0:T(8,128)(2,1)S(1)}, u32[]{:S(2)}) copy-start(bf16[2048,128]{1,0:T(8,128)(2,1)S(1)} %pad_maximum_fusion.3.refs_2_) | copy-start | bytes 1572868
  75.8 13.7 %collective-permute-start.10 = (bf16[2048,128]{1,0:T(8,128)(2,1)S(1)}, bf16[2048,128]{1,0:T(8,128)(2,1)}, u32[]{:S(2)}, u32[]{:S(2)}) collective-permute-start(bf16[2048,128]{1,0:T(8,128)(2,1)S(1)} %pad_maximum_fusion.3.refs_2_), channel_id=1, source_target_pairs={{0,2},{2,0},{4,6},{6,4},{8,10},{10,8},{12,14},{14,12},{16,18},{18,... | collective-permute-start | bytes 1572872 | tf_op jit(solution)/shard_map/ppermute | solution.py:982
  77.0 81.5 %collective-permute-start.16 = (bf16[1792,512]{1,0:T(8,128)(2,1)S(1)}, bf16[1792,512]{1,0:T(8,128)(2,1)}, u32[]{:S(2)}, u32[]{:S(2)}) collective-permute-start(bf16[1792,512]{1,0:T(8,128)(2,1)S(1)} %pad_maximum_fusion), channel_id=1, source_target_pairs={{0,1},{1,0},{2,3},{3,2},{4,5},{5,4},{6,7},{7,6},{8,9},{9,8},{10,11... | collective-permute-start | bytes 5505032 | tf_op jit(solution)/shard_map/ppermute | solution.py:972
  78.6 80.0 %collective-permute-start.17 = (bf16[256,2048]{1,0:T(8,128)(2,1)}, bf16[256,2048]{1,0:T(8,128)(2,1)S(1)}, u32[]{:S(2)}, u32[]{:S(2)}) collective-permute-start(bf16[256,2048]{1,0:T(8,128)(2,1)} %refs_12_.1), channel_id=1, source_target_pairs={{0,1},{1,0},{2,3},{3,2},{4,5},{5,4},{6,7},{7,6},{8,9},{9,8},{10,11... | collective-permute-start | bytes 3145736 | tf_op jit(solution)/shard_map/ppermute | solution.py:972
  89.5 69.0 %collective-permute-start.13 = (bf16[256,512]{1,0:T(8,128)(2,1)}, bf16[256,512]{1,0:T(8,128)(2,1)S(1)}, u32[]{:S(2)}, u32[]{:S(2)}) collective-permute-start(bf16[256,512]{1,0:T(8,128)(2,1)} %get-tuple-element.151.refs_1_), channel_id=1, source_target_pairs={{0,14},{14,0},{2,12},{12,2},{4,10},{10,4},{6,8},{8,6},{1,15},{15,1... | collective-permute-start | bytes 786440 | tf_op jit(solution)/shard_map/ppermute | solution.py:1068
  91.4 67.1 %collective-permute-start.14 = (bf16[256,512]{1,0:T(8,128)(2,1)}, bf16[256,512]{1,0:T(8,128)(2,1)S(1)}, u32[]{:S(2)}, u32[]{:S(2)}) collective-permute-start(bf16[256,512]{1,0:T(8,128)(2,1)} %get-tuple-element.152), channel_id=1, source_target_pairs={{0,16},{16,0},{14,30},{30,14},{2,18},{18,2},{12,28},{28,12},{4,20}... | collective-permute-start | bytes 786440 | tf_op jit(solution)/shard_map/ppermute | solution.py:1068
  91.5 67.0 %collective-permute-start.15 = (bf16[256,512]{1,0:T(8,128)(2,1)}, bf16[256,512]{1,0:T(8,128)(2,1)S(1)}, u32[]{:S(2)}, u32[]{:S(2)}) collective-permute-start(bf16[256,512]{1,0:T(8,128)(2,1)} %get-tuple-element.153), channel_id=1, source_target_pairs={{0,30},{14,16},{16,0},{30,14},{2,28},{12,18},{18,2},{28,12},{4,26}... | collective-permute-start | bytes 786440 | tf_op jit(solution)/shard_map/ppermute | solution.py:1068
  208.3 163.9 %collective-permute-start.18 = (bf16[256,512]{1,0:T(8,128)(2,1)}, bf16[256,512]{1,0:T(8,128)(2,1)}, u32[]{:S(2)}, u32[]{:S(2)}) collective-permute-start(bf16[256,512]{1,0:T(8,128)(2,1)} %get-tuple-element.200.own_ref), channel_id=1, source_target_pairs={{14,0},{0,14},{12,2},{2,12},{10,4},{4,10},{8,6},{6,8},{15,1},{1,15... | collective-permute-start | bytes 786440 | tf_op jit(solution)/shard_map/ppermute | solution.py:1074
  210.2 161.9 %collective-permute-start.19 = (bf16[256,512]{1,0:T(8,128)(2,1)}, bf16[256,512]{1,0:T(8,128)(2,1)}, u32[]{:S(2)}, u32[]{:S(2)}) collective-permute-start(bf16[256,512]{1,0:T(8,128)(2,1)} %get-tuple-element.177), channel_id=1, source_target_pairs={{16,0},{0,16},{30,14},{14,30},{18,2},{2,18},{28,12},{12,28},{20,4}... | collective-permute-start | bytes 786440 | tf_op jit(solution)/shard_map/ppermute | solution.py:1074
  210.3 161.9 %collective-permute-start.20 = (bf16[256,512]{1,0:T(8,128)(2,1)}, bf16[256,512]{1,0:T(8,128)(2,1)}, u32[]{:S(2)}, u32[]{:S(2)}) collective-permute-start(bf16[256,512]{1,0:T(8,128)(2,1)} %get-tuple-element.178), channel_id=1, source_target_pairs={{30,0},{16,14},{0,16},{14,30},{28,2},{18,12},{2,18},{12,28},{26,4}... | collective-permute-start | bytes 786440 | tf_op jit(solution)/shard_map/ppermute | solution.py:1074
  372.2 11.1 %collective-permute-start.22 = (bf16[2048,128]{1,0:T(8,128)(2,1)}, bf16[2048,128]{1,0:T(8,128)(2,1)}, u32[]{:S(2)}, u32[]{:S(2)}) collective-permute-start(bf16[2048,128]{1,0:T(8,128)(2,1)} %get-tuple-element.207), channel_id=1, source_target_pairs={{0,2},{2,0},{4,6},{6,4},{8,10},{10,8},{12,14},{14,12},{16,18},{18,... | collective-permute-start | bytes 1572872 | tf_op jit(solution)/shard_map/ppermute | solution.py:982
  372.3 14.0 %collective-permute-start.24 = (bf16[2048,128]{1,0:T(8,128)(2,1)}, bf16[2048,128]{1,0:T(8,128)(2,1)S(1)}, u32[]{:S(2)}, u32[]{:S(2)}) collective-permute-start(bf16[2048,128]{1,0:T(8,128)(2,1)} %get-tuple-element.209), channel_id=1, source_target_pairs={{0,2},{2,0},{4,6},{6,4},{8,10},{10,8},{12,14},{14,12},{16,18},{18,... | collective-permute-start | bytes 1572872 | tf_op jit(solution)/shard_map/ppermute | solution.py:982
  372.9 10.4 %copy-start.2 = (f32[2048,128]{1,0:T(8,128)S(1)}, f32[2048,128]{1,0:T(8,128)}, u32[]{:S(2)}) copy-start(f32[2048,128]{1,0:T(8,128)} %get-tuple-element.206) | copy-start | bytes 3145732
  385.3 9.1 %collective-permute-start.23 = (bf16[1024,128]{1,0:T(8,128)(2,1)}, bf16[1024,128]{1,0:T(8,128)(2,1)}, u32[]{:S(2)}, u32[]{:S(2)}) collective-permute-start(bf16[1024,128]{1,0:T(8,128)(2,1)} %slice.305), channel_id=1, source_target_pairs={{0,4},{2,6},{4,0},{6,2},{8,12},{10,14},{12,8},{14,10},{16,20},{18,... | collective-permute-start | bytes 786440 | tf_op jit(solution)/shard_map/ppermute | solution.py:982
  386.2 7.3 %collective-permute-start.21 = (bf16[2,2,64,1536]{3,2,1,0:T(8,128)(2,1)}, bf16[2,2,64,1536]{3,2,1,0:T(8,128)(2,1)S(1)}, u32[]{:S(2)}, u32[]{:S(2)}) collective-permute-start(bf16[2,2,64,1536]{3,2,1,0:T(8,128)(2,1)} %get-tuple-element.189), channel_id=1, source_target_pairs={{0,2},{2,0},{4,6},{6,4},{8,10},{10,8},{12,14},{14,12},{16,18},{18,... | collective-permute-start | bytes 2359304 | tf_op jit(solution)/shard_map/ppermute | solution.py:982
  386.4 8.6 %collective-permute-start.25 = (bf16[1024,128]{1,0:T(8,128)(2,1)S(1)}, bf16[1024,128]{1,0:T(8,128)(2,1)S(1)}, u32[]{:S(2)}, u32[]{:S(2)}) collective-permute-start(bf16[1024,128]{1,0:T(8,128)(2,1)S(1)} %slice.304), channel_id=1, source_target_pairs={{0,8},{2,10},{4,12},{6,14},{8,0},{10,2},{12,4},{14,6},{16,24},{18,... | collective-permute-start | bytes 786440 | tf_op jit(solution)/shard_map/ppermute | solution.py:982
  393.6 9.0 %copy-start.13 = (f32[512,128]{1,0:T(8,128)S(1)}, f32[512,128]{1,0:T(8,128)}, u32[]{:S(2)}) copy-start(f32[512,128]{1,0:T(8,128)} %get-tuple-element.220) | copy-start | bytes 786436
  393.6 9.3 %copy-start.11 = (f32[512,128]{1,0:T(8,128)S(1)}, f32[512,128]{1,0:T(8,128)}, u32[]{:S(2)}) copy-start(f32[512,128]{1,0:T(8,128)} %get-tuple-element.221) | copy-start | bytes 786436
  394.4 8.8 %copy-start.18 = (f32[1,512]{1,0:T(1,128)S(1)}, f32[1,512]{1,0:T(1,128)}, u32[]{:S(2)}) copy-start(f32[1,512]{1,0:T(1,128)} %get-tuple-element.222) | copy-start | bytes 6148
  396.8 10.6 %collective-permute-start.26 = (bf16[512,128]{1,0:T(8,128)(2,1)}, bf16[512,128]{1,0:T(8,128)(2,1)S(1)}, u32[]{:S(2)}, u32[]{:S(2)}) collective-permute-start(bf16[512,128]{1,0:T(8,128)(2,1)} %slice.307), channel_id=1, source_target_pairs={{0,8},{2,10},{4,12},{6,14},{8,0},{10,2},{12,4},{14,6},{16,24},{18,... | collective-permute-start | bytes 393224 | tf_op jit(solution)/shard_map/ppermute | solution.py:982
  399.1 8.4 %collective-permute-start.27 = (bf16[512,128]{1,0:T(8,128)(2,1)}, bf16[512,128]{1,0:T(8,128)(2,1)}, u32[]{:S(2)}, u32[]{:S(2)}) collective-permute-start(bf16[512,128]{1,0:T(8,128)(2,1)} %slice.306), channel_id=1, source_target_pairs={{0,4},{2,6},{4,0},{6,2},{8,12},{10,14},{12,8},{14,10},{16,20},{18,... | collective-permute-start | bytes 393224 | tf_op jit(solution)/shard_map/ppermute | solution.py:982
  400.1 12.0 %collective-permute-start.29 = (bf16[2,64,1536]{2,1,0:T(8,128)(2,1)}, bf16[2,64,1536]{2,1,0:T(8,128)(2,1)}, u32[]{:S(2)}, u32[]{:S(2)}) collective-permute-start(bf16[2,64,1536]{2,1,0:T(8,128)(2,1)} %slice_bitcast_fusion), channel_id=1, source_target_pairs={{0,1},{1,0},{2,3},{3,2},{4,5},{5,4},{6,7},{7,6},{8,9},{9,8},{10,11... | collective-permute-start | bytes 1179656 | tf_op jit(solution)/shard_map/ppermute | solution.py:972
  401.6 8.9 %collective-permute-start.30 = (bf16[512,128]{1,0:T(8,128)(2,1)}, bf16[512,128]{1,0:T(8,128)(2,1)}, u32[]{:S(2)}, u32[]{:S(2)}) collective-permute-start(bf16[512,128]{1,0:T(8,128)(2,1)} %get-tuple-element.219), channel_id=1, source_target_pairs={{0,16},{2,18},{4,20},{6,22},{8,24},{10,26},{12,28},{14,30},{16,0},... | collective-permute-start | bytes 393224 | tf_op jit(solution)/shard_map/ppermute | solution.py:982
  408.5 7.8 %collective-permute-start.28 = (bf16[512,128]{1,0:T(8,128)(2,1)S(1)}, bf16[512,128]{1,0:T(8,128)(2,1)S(1)}, u32[]{:S(2)}, u32[]{:S(2)}) collective-permute-start(bf16[512,128]{1,0:T(8,128)(2,1)S(1)} %pad_maximum_fusion.9), channel_id=1, source_target_pairs={{0,16},{2,18},{4,20},{6,22},{8,24},{10,26},{12,28},{14,30},{16,0},... | collective-permute-start | bytes 393224 | tf_op jit(solution)/shard_map/ppermute | solution.py:982
  424.9 3.2 collective-permute-start.34
  428.1 6.2 %collective-permute-start.35 = (bf16[128,256]{1,0:T(8,128)(2,1)S(1)}, bf16[128,256]{1,0:T(8,128)(2,1)S(1)}, u32[]{:S(2)}, u32[]{:S(2)}) collective-permute-start(bf16[128,256]{1,0:T(8,128)(2,1)S(1)} %slice_bitcast_fusion.2), channel_id=1, source_target_pairs={{0,1},{1,0},{2,3},{3,2},{4,5},{5,4},{6,7},{7,6},{8,9},{9,8},{10,11... | collective-permute-start | bytes 196616 | tf_op jit(solution)/shard_map/ppermute | solution.py:972
  428.7 25.5 %collective-permute-start.31 = (bf16[256,512]{1,0:T(8,128)(2,1)S(1)}, bf16[256,512]{1,0:T(8,128)(2,1)S(1)}, u32[]{:S(2)}, u32[]{:S(2)}) collective-permute-start(bf16[256,512]{1,0:T(8,128)(2,1)S(1)} %copy-done.27), channel_id=1, source_target_pairs={{14,0},{0,14},{12,2},{2,12},{10,4},{4,10},{8,6},{6,8},{15,1},{1,15... | collective-permute-start | bytes 786440 | tf_op jit(solution)/shard_map/ppermute | solution.py:1074
  430.9 23.3 %collective-permute-start.32 = (bf16[256,512]{1,0:T(8,128)(2,1)S(1)}, bf16[256,512]{1,0:T(8,128)(2,1)S(1)}, u32[]{:S(2)}, u32[]{:S(2)}) collective-permute-start(bf16[256,512]{1,0:T(8,128)(2,1)S(1)} %copy-done.29), channel_id=1, source_target_pairs={{16,0},{0,16},{30,14},{14,30},{18,2},{2,18},{28,12},{12,28},{20,4}... | collective-permute-start | bytes 786440 | tf_op jit(solution)/shard_map/ppermute | solution.py:1074
  431.0 23.2 %collective-permute-start.33 = (bf16[256,512]{1,0:T(8,128)(2,1)S(1)}, bf16[256,512]{1,0:T(8,128)(2,1)S(1)}, u32[]{:S(2)}, u32[]{:S(2)}) collective-permute-start(bf16[256,512]{1,0:T(8,128)(2,1)S(1)} %copy-done.28), channel_id=1, source_target_pairs={{30,0},{16,14},{0,16},{14,30},{28,2},{18,12},{2,18},{12,28},{26,4}... | collective-permute-start | bytes 786440 | tf_op jit(solution)/shard_map/ppermute | solution.py:1074
  433.9 18.0 %collective-permute-start.40 = (bf16[64,1536]{1,0:T(8,128)(2,1)S(1)}, bf16[64,1536]{1,0:T(8,128)(2,1)S(1)}, u32[]{:S(2)}, u32[]{:S(2)}) collective-permute-start(bf16[64,1536]{1,0:T(8,128)(2,1)S(1)} %slice_bitcast_fusion.1), channel_id=1, source_target_pairs={{0,4},{2,6},{4,0},{6,2},{8,12},{10,14},{12,8},{14,10},{16,20},{18,... | collective-permute-start | bytes 589832 | tf_op jit(solution)/shard_map/ppermute | solution.py:982
  434.3 18.4 %collective-permute-start.36 = (bf16[128,256]{1,0:T(8,128)(2,1)S(1)}, bf16[128,256]{1,0:T(8,128)(2,1)S(1)}, u32[]{:S(2)}, u32[]{:S(2)}) collective-permute-start(bf16[128,256]{1,0:T(8,128)(2,1)S(1)} %fusion.19), channel_id=1, source_target_pairs={{0,4},{2,6},{4,0},{6,2},{8,12},{10,14},{12,8},{14,10},{16,20},{18,... | collective-permute-start | bytes 196616 | tf_op jit(solution)/shard_map/ppermute | solution.py:982
  452.0 8.4 %collective-permute-start.41 = (bf16[64,1536]{1,0:T(8,128)(2,1)S(1)}, bf16[64,1536]{1,0:T(8,128)(2,1)S(1)}, u32[]{:S(2)}, u32[]{:S(2)}) collective-permute-start(bf16[64,1536]{1,0:T(8,128)(2,1)S(1)} %fusion.1), channel_id=1, source_target_pairs={{0,8},{2,10},{4,12},{6,14},{8,0},{10,2},{12,4},{14,6},{16,24},{18,... | collective-permute-start | bytes 589832 | tf_op jit(solution)/shard_map/ppermute | solution.py:982
  452.7 5.8 %collective-permute-start.37 = (bf16[128,256]{1,0:T(8,128)(2,1)S(1)}, bf16[128,256]{1,0:T(8,128)(2,1)S(1)}, u32[]{:S(2)}, u32[]{:S(2)}) collective-permute-start(bf16[128,256]{1,0:T(8,128)(2,1)S(1)} %add_convert_fusion.7), channel_id=1, source_target_pairs={{0,8},{2,10},{4,12},{6,14},{8,0},{10,2},{12,4},{14,6},{16,24},{18,... | collective-permute-start | bytes 196616 | tf_op jit(solution)/shard_map/ppermute | solution.py:982
  458.5 11.5 %collective-permute-start.38 = (bf16[128,256]{1,0:T(8,128)(2,1)S(1)}, bf16[128,256]{1,0:T(8,128)(2,1)S(1)}, u32[]{:S(2)}, u32[]{:S(2)}) collective-permute-start(bf16[128,256]{1,0:T(8,128)(2,1)S(1)} %add_convert_fusion.6), channel_id=1, source_target_pairs={{0,16},{2,18},{4,20},{6,22},{8,24},{10,26},{12,28},{14,30},{16,0},... | collective-permute-start | bytes 196616 | tf_op jit(solution)/shard_map/ppermute | solution.py:982
  460.4 13.0 %collective-permute-start.42 = (bf16[64,1536]{1,0:T(8,128)(2,1)S(1)}, bf16[64,1536]{1,0:T(8,128)(2,1)S(1)}, u32[]{:S(2)}, u32[]{:S(2)}) collective-permute-start(bf16[64,1536]{1,0:T(8,128)(2,1)S(1)} %add_convert_fusion.2), channel_id=1, source_target_pairs={{0,16},{2,18},{4,20},{6,22},{8,24},{10,26},{12,28},{14,30},{16,0},... | collective-permute-start | bytes 589832 | tf_op jit(solution)/shard_map/ppermute | solution.py:982
  470.1 3.8 collective-permute-start.39
  473.5 6.2 %collective-permute-start.43 = (bf16[64,1536]{1,0:T(8,128)(2,1)S(1)}, bf16[64,1536]{1,0:T(8,128)(2,1)S(1)}, u32[]{:S(2)}, u32[]{:S(2)}) collective-permute-start(bf16[64,1536]{1,0:T(8,128)(2,1)S(1)} %add_convert_fusion.1), channel_id=1, source_target_pairs={{0,4},{2,6},{4,0},{6,2},{8,12},{10,14},{12,8},{14,10},{16,20},{18,... | collective-permute-start | bytes 589832 | tf_op jit(solution)/shard_map/ppermute | solution.py:982
  479.8 4.2 collective-permute-start.44
  (18 other events, 49.6 us)
Sparse Core Ops, SparseCore 0:
  213.4 165.3 all-reduce.3

commit v4 on v3

--- a/solution.py
+++ b/solution.py
@@ -169,7 +169,7 @@
         ),
         out_shape=jax.ShapeDtypeStruct((4 * rows, width), bf16),
         compiler_params=params(),
-        cost_estimate=cost(2),
+        cost_estimate=cost(0),
         name="unpack",
     )(table, *pieces)
 
@@ -350,8 +350,9 @@
 def attend_kernel(start, buffers, table_ref, *refs):
     sources = refs[:buffers]
     qt_ref = refs[buffers]
-    refs = refs[buffers + 1 :]
-    out_ref, lse_ref, kv_ref, vt_ref, knorm_ref, acc_ref, max_ref = refs
+    out_ref, factor_ref, probs_ref = refs[buffers + 1 : buffers + 4]
+    refs = refs[buffers + 4 :]
+    kv_ref, vt_ref, knorm_ref, acc_ref, max_ref, full_ref, part_ref, full_sem, part_sem, done_ref = refs
     tile = pl.program_id(0)
     head, width = qt_ref.shape[1:]
     factor = LOG2E * head ** (-0.5)
@@ -359,6 +360,8 @@
     @pl.when(tile == 0)
     def _():
         knorm_ref[0] = 0.0
+        done_ref[0] = 0
+        done_ref[1] = 0
 
         def turn(ref, row, span):
             rows = ref[row : row + PART, :]
@@ -376,41 +379,72 @@
     steps, begin, position, parts = tile_ranges(base)
     query = qt_ref[0].astype(f32)
     qnorm = jnp.max(jnp.sum(query * query, axis=0, keepdims=True))
-    narrow = qnorm * knorm_ref[0] * (factor * factor) < 100.0 * 100.0
+    narrow = qnorm * knorm_ref[0] * (factor * factor) < 60.0 * 60.0
     acc_ref[...] = jnp.zeros(acc_ref.shape, f32)
-    max_ref[...] = jnp.full(max_ref.shape, jnp.where(narrow, 0.0, mask_fill), f32)
-
-    def plain(offset, size, mask):
-        span = pl.ds(pl.multiple_of(offset, size), size)
-        scores = dot(kv_ref[span, :head], qt_ref[0]) * factor
-        if mask is not None:
-            scores = jnp.where(mask, scores, mask_fill)
-        probs = jnp.exp2(scores).astype(bf16)
-        acc_ref[...] += dot(vt_ref[:, span], probs)
+    max_ref[...] = jnp.zeros(max_ref.shape, f32)
+
+    def writer(kind, buffer_ref, sem, span):
+        count = done_ref[kind]
+        slot = lax.rem(count, 2)
+        copy = pltpu.make_async_copy(
+            buffer_ref.at[slot], probs_ref.at[tile, span, :], sem.at[slot]
+        )
+        done_ref[kind] = count + 1
+
+        @pl.when(count >= 2)
+        def _():
+            copy.wait()
+
+        def write(probs):
+            buffer_ref[slot] = probs
+            copy.start()
+
+        return write
+
+    def span_of(offset, size):
+        return pl.ds(pl.multiple_of(offset, size), size)
+
+    def scores_of(span):
+        return dot(kv_ref[span, :head], qt_ref[0]) * factor
 
     @pl.when(narrow)
     def _():
         def step(i, carry):
-            plain(i * FULL, FULL, None)
+            span = span_of(i * FULL, FULL)
+            write = writer(0, full_ref, full_sem, span)
+            probs = jnp.exp2(scores_of(span)).astype(bf16)
+            write(probs)
+            acc_ref[...] += dot(vt_ref[:, span], probs)
             return carry
 
         def part(i, carry):
-            plain(begin + i * PART, PART, allowed_mask(position + i * PART, base, width))
+            span = span_of(begin + i * PART, PART)
+            write = writer(1, part_ref, part_sem, span)
+            mask = allowed_mask(position + i * PART, base, width)
+            probs = jnp.exp2(jnp.where(mask, scores_of(span), mask_fill)).astype(bf16)
+            write(probs)
+            acc_ref[...] += dot(vt_ref[:, span], probs)
             return carry
 
         lax.fori_loop(0, steps, step, 0)
         lax.fori_loop(0, parts, part, 0)
+        factor_ref[0] = 1.0 / acc_ref[head : head + 1, :]
 
     @pl.when(jnp.logical_not(narrow))
     def _():
-        def part(i, carry):
+        max_ref[...] = jnp.full(max_ref.shape, mask_fill, f32)
+        count = steps * (FULL // PART) + parts
+
+        def masked(i):
             before = i < steps * (FULL // PART)
             offset = i * PART
-            span = pl.ds(pl.multiple_of(offset, PART), PART)
+            span = span_of(offset, PART)
             shifted = jnp.where(before, -(1 << 24), position + offset - begin)
             mask = allowed_mask(shifted, base, width)
-            scores = dot(kv_ref[span, :head], qt_ref[0]) * factor
-            scores = jnp.where(mask, scores, mask_fill)
+            return span, mask, jnp.where(mask, scores_of(span), mask_fill)
+
+        def part(i, carry):
+            span, mask, scores = masked(i)
             old = max_ref[...]
             new = jnp.maximum(old, jnp.max(scores, axis=0, keepdims=True))
             probs = jnp.where(mask, jnp.exp2(scores - new), 0.0).astype(bf16)
@@ -418,11 +452,31 @@
             max_ref[...] = new
             return carry
 
-        lax.fori_loop(0, steps * (FULL // PART) + parts, part, 0)
-
-    total = acc_ref[head : head + 1, :]
-    out_ref[0] = acc_ref[:head, :] / total
-    lse_ref[0] = max_ref[...] + jnp.log2(total)
+        lax.fori_loop(0, count, part, 0)
+        max_ref[...] = max_ref[...] + jnp.log2(acc_ref[head : head + 1, :])
+
+        def again(i, carry):
+            span, mask, scores = masked(i)
+            write = writer(1, part_ref, part_sem, span)
+            write(jnp.where(mask, jnp.exp2(scores - max_ref[...]), 0.0).astype(bf16))
+            return carry
+
+        lax.fori_loop(0, count, again, 0)
+        factor_ref[0] = jnp.ones(max_ref.shape, f32)
+
+    out_ref[0] = acc_ref[:head, :] / acc_ref[head : head + 1, :]
+
+    @pl.when(tile == pl.num_programs(0) - 1)
+    def _():
+        for kind, buffer_ref, sem in ((0, full_ref, full_sem), (1, part_ref, part_sem)):
+            for slot in range(2):
+
+                @pl.when(done_ref[kind] > slot)
+                def _():
+                    rows = pl.ds(0, buffer_ref.shape[1])
+                    pltpu.make_async_copy(
+                        buffer_ref.at[slot], probs_ref.at[0, rows, :], sem.at[slot]
+                    ).wait()
 
 
 def attend_call(start, sources, table, qt):
@@ -437,18 +491,24 @@
             num_scalar_prefetch=1,
             grid=(tiles,),
             in_specs=[keep(x) for x in sources] + [one((head, width))],
-            out_specs=[one((head, width)), one((1, width))],
+            out_specs=[one((head, width)), one((1, width)), pl.BlockSpec(memory_space=pl.ANY)],
             scratch_shapes=[
                 pltpu.VMEM((total_keys, pair), bf16),
                 pltpu.VMEM((head + 16, total_keys), bf16),
                 pltpu.SMEM((1,), f32),
                 pltpu.VMEM((head + 16, width), f32),
                 pltpu.VMEM((1, width), f32),
+                pltpu.VMEM((2, FULL, width), bf16),
+                pltpu.VMEM((2, PART, width), bf16),
+                pltpu.SemaphoreType.DMA((2,)),
+                pltpu.SemaphoreType.DMA((2,)),
+                pltpu.SMEM((2,), jnp.int32),
             ],
         ),
         out_shape=[
             jax.ShapeDtypeStruct((tiles, head, width), f32),
             jax.ShapeDtypeStruct((tiles, 1, width), f32),
+            jax.ShapeDtypeStruct((tiles, total_keys, width), bf16),
         ],
         compiler_params=params(),
         cost_estimate=cost(64),
@@ -458,17 +518,22 @@
 
 def attend_back_kernel(start, buffers, table_ref, *refs):
     sources = refs[:buffers]
-    qt_ref, q_ref, dot_ref, do_ref, lse_ref, delta_ref = refs[buffers : buffers + 6]
-    refs = refs[buffers + 6 :]
+    q_ref, dot_ref, do_ref, delta_ref, probs_ref = refs[buffers : buffers + 5]
+    refs = refs[buffers + 5 :]
     dq_ref = refs[0]
     outs = refs[1 : 1 + buffers]
-    kv_ref, kt_ref, dkv_ref = refs[1 + buffers :]
+    refs = refs[1 + buffers :]
+    kv_ref, kt_ref, dkv_ref, rows_ref, full_ref, part_ref, full_sem, part_sem, done_ref = refs
     tile = pl.program_id(0)
-    head, width = qt_ref.shape[1:]
+    tiles = pl.num_programs(0)
+    width, head = q_ref.shape[1:]
     scale = head ** (-0.5)
 
     @pl.when(tile == 0)
     def _():
+        done_ref[0] = 0
+        rows_ref[...] = jnp.zeros(rows_ref.shape, bf16)
+
         def turn(ref, row, span):
             rows = ref[row : row + PART, :]
             kv_ref[span, :] = rows
@@ -477,34 +542,78 @@
 
         for_slots(sources, table_ref, start, turn)
 
-    base = table_ref[BASES + tile]
-    steps, begin, position, parts = tile_ranges(base)
+    def steps_of(which):
+        return tile_ranges(table_ref[BASES + jnp.clip(which, 0, tiles - 1)])[0]
+
+    steps, begin, _, parts = tile_ranges(table_ref[BASES + tile])
+
+    def full_copy(which, i, slot):
+        rows = pl.ds(pl.multiple_of(i * FULL, FULL), FULL)
+        return pltpu.make_async_copy(
+            probs_ref.at[which, rows, :], full_ref.at[slot], full_sem.at[slot]
+        )
+
+    def part_copy(i):
+        slot = lax.rem(i, 2)
+        rows = pl.ds(pl.multiple_of(begin + i * PART, PART), PART)
+        return pltpu.make_async_copy(
+            probs_ref.at[tile, rows, :], part_ref.at[slot], part_sem.at[slot]
+        )
+
+    done = done_ref[0]
+
+    @pl.when((steps > 0) & ((tile == 0) | (steps_of(tile - 1) == 0)))
+    def _():
+        full_copy(tile, 0, lax.rem(done, 2)).start()
+
+    for i in range(2):
+
+        @pl.when(i < parts)
+        def _():
+            part_copy(i).start()
+
     dq_ref[...] = jnp.zeros(dq_ref.shape, f32)
-
-    def block(offset, size, mask):
+    rows_ref[:width, :head] = q_ref[0]
+    rows_ref[width:, head:] = do_ref[0]
+
+    def block(offset, size, probs):
         span = pl.ds(pl.multiple_of(offset, size), size)
-        scores = dot(kv_ref[span, :head], qt_ref[0]) * (LOG2E * scale) - lse_ref[0]
-        probs = jnp.exp2(scores)
-        if mask is not None:
-            probs = jnp.where(mask, probs, 0.0)
         prob_grad = dot(kv_ref[span, head:], dot_ref[0])
-        score_grad = (probs * (prob_grad - delta_ref[0])).astype(bf16)
-        dq_ref[0] += dot(kt_ref[:, span], score_grad) * scale
-        dkv_ref[span, :head] += dot(score_grad, q_ref[0])
-        dkv_ref[span, head:] += dot(probs.astype(bf16), do_ref[0])
+        score_grad = (probs.astype(f32) * (prob_grad - delta_ref[0])).astype(bf16)
+        dq_ref[0] += dot(kt_ref[:, span], score_grad)
+        dkv_ref[span, :] += dot(jnp.concatenate([score_grad, probs], axis=1), rows_ref[...])
 
     def step(i, carry):
-        block(i * FULL, FULL, None)
+        slot = lax.rem(done + i, 2)
+
+        @pl.when(i + 1 < steps)
+        def _():
+            full_copy(tile, i + 1, 1 - slot).start()
+
+        @pl.when((i + 1 == steps) & (tile + 1 < tiles) & (steps_of(tile + 1) > 0))
+        def _():
+            full_copy(tile + 1, 0, 1 - slot).start()
+
+        full_copy(tile, i, slot).wait()
+        block(i * FULL, FULL, full_ref[slot])
         return carry
 
     def part(i, carry):
-        block(begin + i * PART, PART, allowed_mask(position + i * PART, base, width))
+        part_copy(i).wait()
+        block(begin + i * PART, PART, part_ref[lax.rem(i, 2)])
+
+        @pl.when(i + 2 < parts)
+        def _():
+            part_copy(i + 2).start()
+
         return carry
 
     lax.fori_loop(0, steps, step, 0)
     lax.fori_loop(0, parts, part, 0)
-
-    @pl.when(tile == pl.num_programs(0) - 1)
+    done_ref[0] = done + steps
+    dq_ref[...] = dq_ref[...] * scale
+
+    @pl.when(tile == tiles - 1)
     def _():
         lane = lax.broadcasted_iota(jnp.int32, (PART, 2 * head), 1)
         both = jnp.where(lane < head, scale, 1.0)
@@ -515,8 +624,8 @@
         for_slots(outs, table_ref, start, finish)
 
 
-def attend_back_call(start, sources, kinds, table, qt, q, grad_t, grad, lse, delta):
-    tiles, head, width = qt.shape
+def attend_back_call(start, sources, kinds, table, q, grad_t, grad, delta, probs):
+    tiles, width, head = q.shape
     total_keys = sum(x.shape[0] for x in sources)
     pair = sources[0].shape[1]
     one = lambda shape: pl.BlockSpec((1,) + shape, lambda i, t: (i, 0, 0))
@@ -528,26 +637,31 @@
             grid=(tiles,),
             in_specs=[keep(x) for x in sources]
             + [
-                one((head, width)),
                 one((width, head)),
                 one((head, width)),
                 one((width, head)),
                 one((1, width)),
-                one((1, width)),
+                pl.BlockSpec(memory_space=pl.ANY),
             ],
             out_specs=[one((head, width))] + [keep(x) for x in sources],
             scratch_shapes=[
                 pltpu.VMEM((total_keys, pair), bf16),
                 pltpu.VMEM((head, total_keys), bf16),
                 pltpu.VMEM((total_keys, pair), f32),
+                pltpu.VMEM((2 * width, pair), bf16),
+                pltpu.VMEM((2, FULL, width), bf16),
+                pltpu.VMEM((2, PART, width), bf16),
+                pltpu.SemaphoreType.DMA((2,)),
+                pltpu.SemaphoreType.DMA((2,)),
+                pltpu.SMEM((1,), jnp.int32),
             ],
         ),
         out_shape=[jax.ShapeDtypeStruct((tiles, head, width), f32)]
         + [jax.ShapeDtypeStruct(x.shape, kind) for x, kind in zip(sources, kinds)],
         compiler_params=params(),
-        cost_estimate=cost(160),
+        cost_estimate=cost(130),
         name="attend_back",
-    )(table, *sources, qt, q, grad_t, grad, lse, delta)
+    )(table, *sources, q, grad_t, grad, delta, probs)
 
 
 def place(index, pieces, expert):
@@ -566,7 +680,7 @@
     middle_body(table_ref, sources, layer_out_refs, *refs)
 
 
-MIDDLE_INPUTS = 13
+MIDDLE_INPUTS = 14
 
 
 def middle_body(
@@ -577,6 +691,7 @@
     index_ref,
     gate_ref,
     attended_ref,
+    factor_ref,
     output_own_ref,
     down_own_ref,
     both_other_ref,
@@ -688,7 +803,8 @@
                 )
             attended = attended_ref[part, :, span]
             picks.append(jnp.sum(chosen * attended, axis=0, keepdims=True))
-            back = (chosen * gate[j : j + 1, lanes]).astype(bf16)
+            back = (chosen * gate[j : j + 1, lanes]).astype(bf16).astype(f32)
+            back = (back * factor_ref[part, :, span]).astype(bf16)
             grad_t_ref[part, :, span] = back
             back = back.astype(f32)
             grad_rows_ref[part, span, :] = back.T.astype(bf16)
@@ -709,7 +825,8 @@
 
 
 def middle_call(
-    table, sources, tokens, index, gate, attended, weights, gain, shift, up_bias, down_bias, padded
+    table, sources, tokens, index, gate, attended, factor, weights,
+    gain, shift, up_bias, down_bias, padded,
 ):
     count, width = tokens.shape
     topk = index.shape[0]
@@ -746,7 +863,7 @@
             num_scalar_prefetch=1,
             grid=(count // TILE,),
             in_specs=piece_specs(sources)
-            + [rows, columns(topk), columns(topk), tile((head, wide))]
+            + [rows, columns(topk), columns(topk), tile((head, wide)), tile((1, wide))]
             + [keep(w.shape) for w in weights]
             + [keep((width, 1)), keep((width, 1)), keep((hidden, 1)), keep((width, 1))],
             out_specs=[x for x, _ in outs],
@@ -766,7 +883,8 @@
         compiler_params=params(),
         cost_estimate=cost(44),
         name="middle",
-    )(table, *sources, tokens, index, gate, attended, *weights, gain, shift, up_bias, down_bias)
+    )(table, *sources, tokens, index, gate, attended, factor, *weights,
+      gain, shift, up_bias, down_bias)
 
 
 def query_back_kernel(
@@ -1181,10 +1299,10 @@
     else:
         grads = (out_grad[0],)
     keys = low_keys + high_keys
-    attended, lse = attend_call(key_table, keys, table, qt)
+    attended, factor, probs = attend_call(key_table, keys, table, qt)
     outs = 4 if plan else 1
     middle = middle_call(
-        table, grads, flat, index, gate, attended, weights,
+        table, grads, flat, index, gate, attended, factor, weights,
         gain_two, shift_two, up_bias_all, down_bias_all, padded,
     )
     layer_out = middle[:outs]
@@ -1199,7 +1317,7 @@
         layer_out = send_back(layer_out, plan)
     kinds = (f32, bf16, f32, bf16, f32, bf16) if plan else (bf16,) * 6
     dq, *key_grads = attend_back_call(
-        key_table, keys, kinds, table, qt, q, grad_t, grad_rows, lse, delta
+        key_table, keys, kinds, table, q, grad_t, grad_rows, delta, probs
     )
     dq, key_grads, layer_out = lax.optimization_barrier((dq, key_grads, layer_out))
     if plan:
@@ -1208,18 +1326,10 @@
     partial, keep, send, router_grad = query_back_call(
         table, first, index, dq, query_weight, query_other, logit_grad, router
     )
-    keep, send, router_grad, partial, *early = lax.optimization_barrier(
-        (keep, send, router_grad, partial, *early)
-    )
-    total = add_low(keep, swap(send, 1))
-    if plan:
-        low_order, high_order = key_orders(count)
-        low_keep, low_got = step_down(low_near + low_got.astype(f32), low_order[2])
-        high_keep, high_got = step_down(high_near + high_got.astype(f32), high_order[2])
-        query_got = other_half(total[1])
     sums = (second_gain_grad, second_shift_grad, down_bias_grad, up_bias_grad)
-    total, layer_out, *sums = lax.optimization_barrier((total, layer_out, *sums))
+    router_grad, layer_out, *sums = lax.optimization_barrier((router_grad, layer_out, *sums))
     second_gain_grad, second_shift_grad, down_bias_grad, up_bias_grad = sums
+    layer_out = unpack_call(table, layer_out) if plan else layer_out[0]
     rest = jnp.concatenate(
         [
             jnp.zeros((width, 2), f32),
@@ -1233,6 +1343,15 @@
     bias_columns = rest.shape[1] - 5
     rest = jnp.pad(rest, ((0, 0), (0, padded - rest.shape[1])))
     rest = jnp.concatenate([rest, router_grad, jnp.zeros((width, 128 - 2 * padded), f32)], axis=1)
+    total = add_low(keep, swap(send, 1))
+    if plan:
+        low_order, high_order = key_orders(count)
+        low_keep, low_got = step_down(low_near + low_got.astype(f32), low_order[2])
+        high_keep, high_got = step_down(high_near + high_got.astype(f32), high_order[2])
+        total, rest, layer_out, *early = lax.optimization_barrier(
+            (total, rest, layer_out, *early)
+        )
+        query_got = other_half(total[1])
     if plan:
         low_got, high_got, total, own_far = lax.optimization_barrier(
             (low_got, high_got, total, own_far)
@@ -1266,7 +1385,7 @@
         table, flat, first, partial, middle_grad, dkv, kv_weight, gain_one, rest
     )
     tokens_grad = done[:outs]
-    keep, send = done[outs:]
+    keep, send, *early = lax.optimization_barrier((*done[outs:], *early))
     small_sum = add_low(keep, swap(send, 1))
     small_sum = add_low(small_sum[0], other_half(small_sum[1]))
     small_sum = add_low(small_sum, swap(small_sum, 2))
@@ -1278,7 +1397,6 @@
         tokens_grad = send_back(tokens_grad, plan)
     query_weight_grad = double(double(total, 2), 1).astype(f32)
     small_grad = double(small_sum, 1).astype(f32)
-    layer_out = unpack_call(table, layer_out) if plan else layer_out[0]
     tokens_grad = unpack_call(table, tokens_grad) if plan else tokens_grad[0]
     output_weight_grad, up_weight_grad, down_weight_grad = (
         lax.dynamic_slice_in_dim(x, shard * (x.shape[0] // 2), x.shape[0] // 2, 0).astype(f32)

time: 494 us -> 481 us (0.974)
  Pallas kernels: 317 us -> 293 us
  waiting for transfers between devices: 68.9 us -> 78.1 us
  starting transfers between devices: 52.2 us -> 59 us
    pallas_call x1, Pallas kernels: 159 us -> 131 us  [attend_back_call(): pl.pallas_call(functools.partial(attend_back_kernel, start, len(sources))...]
    psum x1, waiting for transfers between devices: 0.01 us -> 12.4 us  [per_device(): lax.psum((output_weight_grad, up_weight_grad, down_weight_grad), ('ctx',...]
    ppermute x27, starting transfers between devices: 19.9 us -> 27.1 us  [swap(): return lax.ppermute(value, 'ctx', [(i, i ^ mask) for i in range(count)])]
    ppermute x27, waiting for transfers between devices: 52.4 us -> 45.9 us  [swap(): return lax.ppermute(value, 'ctx', [(i, i ^ mask) for i in range(count)])]
  transfers between devices with their start and end apart: 46 -> 46, of which waited for: 16 -> 16; matrix products, arithmetic and copies ran while one was open for 6% -> 6% of each run, Pallas kernels for 51% -> 47%
where the time goes in v4:
time: 481 us; the launch traced here: 479 us
  Pallas kernels  293 us (61%)
  waiting for transfers between devices  78.1 us (16%)
  starting transfers between devices  59 us (12%)
  other arithmetic  20.9 us (4%)
  between operations  15 us (3%)
  local copies, waits for them, and re-layouts  13.1 us (3%)
    pallas_call x1, Pallas kernels, attend_back_call(): pl.pallas_call(functools.partial(attend_back_kernel, start, len(sources))...  131 us
    pallas_call x1, Pallas kernels, attend_call(): pl.pallas_call(functools.partial(attend_kernel, start, len(sources)), gri...  65.7 us
    pallas_call x1, Pallas kernels, middle_call(): pl.pallas_call(functools.partial(middle_kernel, len(sources)), grid_spec=...  49 us
    ppermute x27, waiting for transfers between devices, swap(): return lax.ppermute(value, 'ctx', [(i, i ^ mask) for i in range(count)])  45.9 us
    ppermute x27, starting transfers between devices, swap(): return lax.ppermute(value, 'ctx', [(i, i ^ mask) for i in range(count)])  27.1 us
    ppermute x6, starting transfers between devices, send_pieces(): lax.ppermute(piece, 'ctx', hop)  14.3 us
    ppermute x6, waiting for transfers between devices, send_pieces(): lax.ppermute(piece, 'ctx', hop)  12.4 us
    psum x1, waiting for transfers between devices, per_device(): lax.psum((output_weight_grad, up_weight_grad, down_weight_grad), ('ctx',...  12.4 us
  transfers between devices with their start and end apart: 46, of which 16 were waited for; matrix products, arithmetic and copies ran while one was open for 6% of the time, Pallas kernels for 47%

profile of v4, /device:TPU:0, one launch (start us, length us, event | category | flops | bytes accessed | tf_op | source)
XLA Modules:
  0.0 479.3 jit_solution(9676890335004667299)
XLA Ops:
  7.2 1.2 fusion.21.table_ref
  8.5 3.1 pack.2
  11.6 5.4 %collective-permute-start.1 = (bf16[272,512]{1,0:T(8,128)(2,1)}, bf16[272,512]{1,0:T(8,128)(2,1)}, u32[]{:S(2)}, u32[]{:S(2)}) collective-permute-start(bf16[272,512]{1,0:T(8,128)(2,1)} %get-tuple-element.131.refs_1_), channel_id=1, source_target_pairs={{0,14},{14,0},{2,12},{12,2},{4,10},{10,4},{6,8},{8,6},{1,15},{15,1... | collective-permute-start | bytes 835592 | tf_op jit(solution)/shard_map/ppermute | solution.py:1186
  17.1 2.0 collective-permute-start.3
  20.6 2.3 collective-permute-start
  22.8 1.3 pad_maximum_fusion
  24.1 2.9 collective-permute-done
  27.1 3.0 pack.3
  31.0 1.3 fusion.15
  32.9 6.5 %collective-permute-done.2.refs_3_ = bf16[272,512]{1,0:T(8,128)(2,1)} collective-permute-done((bf16[272,512]{1,0:T(8,128)(2,1)}, bf16[272,512]{1,0:T(8,128)(2,1)}, u32[]{:S(2)}, u32[]{:S(2)}) %collective-permute-start.2) | collective-permute-done | bytes 278560 | tf_op jit(solution)/shard_map/ppermute | solution.py:1186
  39.4 5.9 %collective-permute-done.3.refs_4_ = bf16[272,512]{1,0:T(8,128)(2,1)} collective-permute-done((bf16[272,512]{1,0:T(8,128)(2,1)}, bf16[272,512]{1,0:T(8,128)(2,1)}, u32[]{:S(2)}, u32[]{:S(2)}) %collective-permute-start.3) | collective-permute-done | bytes 278560 | tf_op jit(solution)/shard_map/ppermute | solution.py:1186
  45.3 6.1 %first_norm.1 = (bf16[512,1024]{1,0:T(8,128)(2,1)}, bf16[512,128]{1,0:T(8,128)(2,1)}, bf16[512,128]{1,0:T(8,128)(2,1)}, s32[8,1024]{1,0:T(8,128)}, bf16[1024,512]{1,0:T(8,128)(2,1)}) custom-call(s32[55]{0:T(128)} %fusion.21.table_ref, bf16[272,512]{1,0:T(8,128)(2,1)} %get-tuple-element.130.refs_0_, bf16[272,512]{1,0:T(8,128)(2,1)} %get-tuple-element.131.refs_1_, ...), custom_call_target="tpu_custom_call" | custom-call | flops 5750000128 | tf_op jit(solution)/shard_map/first_norm/pallas_call | solution.py:233
  51.5 0.9 fusion.23
  52.4 5.7 %collective-permute-done.4 = bf16[512,128]{1,0:T(8,128)(2,1)S(1)} collective-permute-done((bf16[512,128]{1,0:T(8,128)(2,1)}, bf16[512,128]{1,0:T(8,128)(2,1)S(1)}, u32[]{:S(2)}, u32[]{:S(2)}) %collective-permute-start.4) | collective-permute-done | bytes 131104 | tf_op jit(solution)/shard_map/ppermute | solution.py:1100
  58.2 1.6 collective-permute-start.12
  60.6 2.5 collective-permute-done.5
  63.9 1.2 collective-permute-start.6
  65.1 2.7 collective-permute-start.9
  67.8 1.4 copy.76.refs_17_
  69.4 1.7 collective-permute-done.6
  71.1 1.0 pad_maximum_fusion.2.refs_0_
  72.2 1.7 collective-permute-done.9
  73.9 1.0 pad_maximum_fusion.3.refs_2_
  74.9 2.1 collective-permute-done.12.other_ref
  77.1 1.5 collective-permute-start.16
  79.1 10.4 %queries.1 = (bf16[8,64,1024]{2,1,0:T(8,128)(2,1)}, bf16[8,1024,64]{2,1,0:T(8,128)(2,1)}, f32[8,1024]{1,0:T(8,128)}) custom-call(s32[55]{0:T(128)} %fusion.21.table_ref, bf16[512,1024]{1,0:T(8,128)(2,1)} %get-tuple-element.143.first_ref.refs_1_, bf16[256,1536]{1,0:T(8,128)(2,1)} %own_ref.3, bf16[256,1536]{1,0:T(8,128)(2,1)} %collective-permute-done.12.other_ref, ...), custom_call_target="tpu_custom_call" | custom-call | flops 11500000256 | tf_op jit(solution)/shard_map/queries/pallas_call | solution.py:297
  89.5 2.4 collective-permute-start.13
  92.0 4.2 collective-permute-start.15
  96.3 65.7 %attend.1 = (f32[8,64,1024]{2,1,0:T(8,128)}, f32[8,1,1024]{2,1,0:T(1,128)}, bf16[8,9216,1024]{2,1,0:T(8,128)(2,1)}) custom-call(s32[55]{0:T(128)} %fusion.21.table_ref, bf16[2048,128]{1,0:T(8,128)(2,1)} %copy-done.8, bf16[2048,128]{1,0:T(8,128)(2,1)} %collective-permute-done.7.refs_1_, bf16[2048,128]{1,0:T(8,128)(2,1)} %copy-done.9, ...), custom_call_target="tpu_custom_call" | custom-call | flops 73600000000 | tf_op jit(solution)/shard_map/attend/pallas_call | solution.py:488
  163.2 49.0 %middle.1 = (bf16[256,512]{1,0:T(8,128)(2,1)}, bf16[256,512]{1,0:T(8,128)(2,1)}, bf16[256,512]{1,0:T(8,128)(2,1)}, bf16[256,512]{1,0:T(8,128)(2,1)}, f32[512,102...) custom-call(s32[55]{0:T(128)} %fusion.21.table_ref, ...), custom_call_target="tpu_custom_call" | custom-call | flops 50600001536 | tf_op jit(solution)/shard_map/middle/pallas_call | solution.py:860
  212.2 1.9 collective-permute-start.18
  214.2 2.9 collective-permute-start.20
  217.2 131.4 %attend_back.1 = (f32[8,64,1024]{2,1,0:T(8,128)}, f32[2048,128]{1,0:T(8,128)}, bf16[2048,128]{1,0:T(8,128)(2,1)}, f32[2048,128]{1,0:T(8,128)}, bf16[2048,128]{1,...) custom-call(s32[55]{0:T(128)} %fusion.21.table_ref, bf16[2048,128]{1,0:T(8,128)(2,1)} %copy-done.8, ...), custom_call_target="tpu_custom_call" | custom-call | flops 149500002304 | tf_op jit(solution)/shard_map/attend_back/pallas_call | solution.py:633
  348.8 10.6 %query_back.1 = (f32[512,1024]{1,0:T(8,128)}, bf16[2,2,64,1536]{3,2,1,0:T(8,128)(2,1)}, bf16[2,2,64,1536]{3,2,1,0:T(8,128)(2,1)}, f32[512,32]{1,0:T(8,128)}) custom-call(s32[55]{0:T(128)} %fusion.21.table_ref, bf16[512,1024]{1,0:T(8,128)(2,1)} %get-tuple-element.143.first_ref.refs_1_, s32[8,1024]{1,0:T(8,128)} %get-tuple-element.144.index_ref.refs_6_, ...), custom_call_target="tpu_custom_call" | custom-call | tf_op jit(solution)/shard_map/query_back/pallas_call | solution.py:957
  361.9 1.8 fusion.2.refs_9_
  363.7 3.0 unpack.2
  368.0 1.1 convert_add_fusion
  369.8 5.1 %collective-permute-start.25 = (bf16[1024,128]{1,0:T(8,128)(2,1)}, bf16[1024,128]{1,0:T(8,128)(2,1)S(1)}, u32[]{:S(2)}, u32[]{:S(2)}) collective-permute-start(bf16[1024,128]{1,0:T(8,128)(2,1)} %slice.303), channel_id=1, source_target_pairs={{0,8},{2,10},{4,12},{6,14},{8,0},{10,2},{12,4},{14,6},{16,24},{18,... | collective-permute-start | bytes 786440 | tf_op jit(solution)/shard_map/ppermute | solution.py:1100
  374.9 1.3 add_convert_fusion
  376.3 12.4 %all-reduce.4.cloned.1.call-done = (bf16[1536,512]{1,0:T(8,128)(2,1)}, bf16[512,2048]{1,0:T(8,128)(2,1)}, bf16[2048,512]{1,0:T(8,128)(2,1)}) async-done(((bf16[1536,512]{1,0:T(8,128)(2,1)}, bf16[512,2048]{1,0:T(8,128)(2,1)}, bf16[2048,512]{1,0:T(8,128)(2,1)}), (bf16[1536,512]{1,0:T(8,128)(2,1)}, bf16[512,2048]{1,0:T(8,128)(2,1)}, bf16[2048,512]{1,0:T(8,128)(2,1)})) %all-reduce.4.cloned.1.call-update) | async-done | bytes 5767184 | tf_op jit(solution)/shard_map/psum | solution.py:1315
  389.4 1.6 collective-permute-start.27
  391.1 1.3 collective-permute-start.29
  392.4 2.5 collective-permute-start.30
  395.0 2.0 collective-permute-start.28
  397.0 7.1 %collective-permute-done.30 = bf16[512,128]{1,0:T(8,128)(2,1)S(1)} collective-permute-done((bf16[512,128]{1,0:T(8,128)(2,1)S(1)}, bf16[512,128]{1,0:T(8,128)(2,1)S(1)}, u32[]{:S(2)}, u32[]{:S(2)}) %collective-permute-start.30) | collective-permute-done | bytes 131104 | tf_op jit(solution)/shard_map/ppermute | solution.py:1100
  404.9 1.2 collective-permute-done.28
  406.7 8.1 %first_back.1 = (bf16[256,512]{1,0:T(8,128)(2,1)}, bf16[256,512]{1,0:T(8,128)(2,1)}, bf16[256,512]{1,0:T(8,128)(2,1)}, bf16[256,512]{1,0:T(8,128)(2,1)}, bf16[2,...) custom-call(s32[55]{0:T(128)} %fusion.21.table_ref, bf16[1024,512]{1,0:T(8,128)(2,1)} %get-tuple-element.158.refs_5_.refs_0_, ...), custom_call_target="tpu_custom_call" | custom-call | flops 8049999872 | tf_op jit(solution)/shard_map/first_back/pallas_call | solution.py:1062
  414.8 2.1 collective-permute-start.31
  417.0 2.9 collective-permute-start.33
  419.9 1.5 collective-permute-start.40
  421.4 1.6 dynamic-slice_convert_fusion.1
  423.4 1.6 dynamic-slice_convert_fusion
  425.0 2.3 collective-permute-done.35
  428.0 1.4 dynamic-slice_convert_fusion.2
  429.3 8.7 %collective-permute-done.36 = bf16[128,256]{1,0:T(8,128)(2,1)S(1)} collective-permute-done((bf16[128,256]{1,0:T(8,128)(2,1)S(1)}, bf16[128,256]{1,0:T(8,128)(2,1)S(1)}, u32[]{:S(2)}, u32[]{:S(2)}) %collective-permute-start.36) | collective-permute-done | bytes 65568 | tf_op jit(solution)/shard_map/ppermute | solution.py:1100
  438.2 2.1 collective-permute-start.41
  441.2 3.0 unpack.3
  444.2 2.9 collective-permute-start.38
  447.3 2.3 collective-permute-done.38
  449.7 10.2 %collective-permute-done.42 = bf16[64,1536]{1,0:T(8,128)(2,1)S(1)} collective-permute-done((bf16[64,1536]{1,0:T(8,128)(2,1)S(1)}, bf16[64,1536]{1,0:T(8,128)(2,1)S(1)}, u32[]{:S(2)}, u32[]{:S(2)}) %collective-permute-start.42) | collective-permute-done | bytes 196640 | tf_op jit(solution)/shard_map/ppermute | solution.py:1100
  459.9 1.9 collective-permute-start.43
  461.9 4.8 %collective-permute-done.43 = bf16[64,1536]{1,0:T(8,128)(2,1)S(1)} collective-permute-done((bf16[64,1536]{1,0:T(8,128)(2,1)S(1)}, bf16[64,1536]{1,0:T(8,128)(2,1)S(1)}, u32[]{:S(2)}, u32[]{:S(2)}) %collective-permute-start.43) | collective-permute-done | bytes 196640 | tf_op jit(solution)/shard_map/ppermute | solution.py:1100
  470.0 1.0 slice_reduce_fusion
  471.1 1.3 maximum_convert_fusion
  (190 shorter events, 20.0 us)
Async XLA Ops:
  7.2 381.4 %all-reduce.4.cloned.1.call-start = ((), (), s32[]{:S(2)}) async-start(), calls=%async_computation | async-start | bytes 11534336 | tf_op jit(solution)/shard_map/psum | solution.py:1315
  8.4 11.0 %copy-start.20 = (bf16[256,24]{0,1:T(8,128)(2,1)S(1)}, bf16[256,24]{0,1:T(8,128)(2,1)}, u32[]{:S(2)}) copy-start(bf16[256,24]{0,1:T(8,128)(2,1)} %param.21) | copy-start | bytes 36868
  8.4 11.1 %copy-start.23 = (bf16[256]{0:T(256)(128)(2,1)S(1)}, bf16[256]{0:T(256)(128)(2,1)}, u32[]{:S(2)}) copy-start(bf16[256]{0:T(256)(128)(2,1)} %param.19) | copy-start | bytes 1540
  8.4 11.2 %copy-start.24 = (bf16[256]{0:T(256)(128)(2,1)S(1)}, bf16[256]{0:T(256)(128)(2,1)}, u32[]{:S(2)}) copy-start(bf16[256]{0:T(256)(128)(2,1)} %param.20) | copy-start | bytes 1540
  8.5 11.3 %copy-start.25 = (bf16[256]{0:T(256)(128)(2,1)S(1)}, bf16[256]{0:T(256)(128)(2,1)}, u32[]{:S(2)}) copy-start(bf16[256]{0:T(256)(128)(2,1)} %param.26) | copy-start | bytes 1540
  8.5 11.4 %copy-start.26 = (bf16[256]{0:T(256)(128)(2,1)S(1)}, bf16[256]{0:T(256)(128)(2,1)}, u32[]{:S(2)}) copy-start(bf16[256]{0:T(256)(128)(2,1)} %param.27) | copy-start | bytes 1540
  8.5 11.5 %copy-start.27 = (bf16[256]{0:T(256)(128)(2,1)S(1)}, bf16[256]{0:T(256)(128)(2,1)}, u32[]{:S(2)}) copy-start(bf16[256]{0:T(256)(128)(2,1)} %param.31) | copy-start | bytes 1540
  8.5 11.6 %copy-start.22 = (bf16[1024]{0:T(1024)(128)(2,1)S(1)}, bf16[1024]{0:T(1024)(128)(2,1)}, u32[]{:S(2)}) copy-start(bf16[1024]{0:T(1024)(128)(2,1)} %param.29) | copy-start | bytes 6148
  11.6 11.3 %copy-start = (bf16[1024,512]{1,0:T(8,128)(2,1)S(1)}, bf16[1024,512]{1,0:T(8,128)(2,1)}, u32[]{:S(2)}) copy-start(bf16[1024,512]{1,0:T(8,128)(2,1)} %refs_11_.1) | copy-start | bytes 3145732
  11.6 21.3 %collective-permute-start.1 = (bf16[272,512]{1,0:T(8,128)(2,1)}, bf16[272,512]{1,0:T(8,128)(2,1)}, u32[]{:S(2)}, u32[]{:S(2)}) collective-permute-start(bf16[272,512]{1,0:T(8,128)(2,1)} %get-tuple-element.131.refs_1_), channel_id=1, source_target_pairs={{0,14},{14,0},{2,12},{12,2},{4,10},{10,4},{6,8},{8,6},{1,15},{15,1... | collective-permute-start | bytes 835592 | tf_op jit(solution)/shard_map/ppermute | solution.py:1186
  17.0 22.4 %collective-permute-start.2 = (bf16[272,512]{1,0:T(8,128)(2,1)}, bf16[272,512]{1,0:T(8,128)(2,1)}, u32[]{:S(2)}, u32[]{:S(2)}) collective-permute-start(bf16[272,512]{1,0:T(8,128)(2,1)} %get-tuple-element.132), channel_id=1, source_target_pairs={{0,16},{16,0},{14,30},{30,14},{2,18},{18,2},{12,28},{28,12},{4,20}... | collective-permute-start | bytes 835592 | tf_op jit(solution)/shard_map/ppermute | solution.py:1186
  17.1 28.2 %collective-permute-start.3 = (bf16[272,512]{1,0:T(8,128)(2,1)}, bf16[272,512]{1,0:T(8,128)(2,1)}, u32[]{:S(2)}, u32[]{:S(2)}) collective-permute-start(bf16[272,512]{1,0:T(8,128)(2,1)} %get-tuple-element.133), channel_id=1, source_target_pairs={{0,30},{14,16},{16,0},{30,14},{2,28},{12,18},{18,2},{28,12},{4,26}... | collective-permute-start | bytes 835592 | tf_op jit(solution)/shard_map/ppermute | solution.py:1186
  20.6 6.4 %collective-permute-start = (bf16[256,169]{1,0:T(8,128)(2,1)S(1)}, bf16[256,169]{1,0:T(8,128)(2,1)S(1)}, u32[]{:S(2)}, u32[]{:S(2)}) collective-permute-start(bf16[256,169]{1,0:T(8,128)(2,1)S(1)} %concatenate.51), channel_id=1, source_target_pairs={{0,1},{1,0},{2,3},{3,2},{4,5},{5,4},{6,7},{7,6},{8,9},{9,8},{10,11... | collective-permute-start | bytes 259592 | tf_op jit(solution)/shard_map/ppermute | solution.py:1090
  32.9 25.3 %copy-start.4 = (bf16[256,1536]{1,0:T(8,128)(2,1)S(1)}, bf16[256,1536]{1,0:T(8,128)(2,1)}, u32[]{:S(2)}) copy-start(bf16[256,1536]{1,0:T(8,128)(2,1)} %own_ref.3) | copy-start | bytes 2359300
  51.4 6.7 %collective-permute-start.4 = (bf16[512,128]{1,0:T(8,128)(2,1)}, bf16[512,128]{1,0:T(8,128)(2,1)S(1)}, u32[]{:S(2)}, u32[]{:S(2)}) collective-permute-start(bf16[512,128]{1,0:T(8,128)(2,1)} %get-tuple-element.145), channel_id=1, source_target_pairs={{0,16},{2,18},{4,20},{6,22},{8,24},{10,26},{12,28},{14,30},{16,0},... | collective-permute-start | bytes 393224 | tf_op jit(solution)/shard_map/ppermute | solution.py:1100
  58.1 5.0 %collective-permute-start.5 = (bf16[512,128]{1,0:T(8,128)(2,1)S(1)}, bf16[512,128]{1,0:T(8,128)(2,1)S(1)}, u32[]{:S(2)}, u32[]{:S(2)}) collective-permute-start(bf16[512,128]{1,0:T(8,128)(2,1)S(1)} %pad_maximum_fusion.7), channel_id=1, source_target_pairs={{0,8},{2,10},{4,12},{6,14},{8,0},{10,2},{12,4},{14,6},{16,24},{18,... | collective-permute-start | bytes 393224 | tf_op jit(solution)/shard_map/ppermute | solution.py:1100
  58.2 18.9 %collective-permute-start.12 = (bf16[256,1536]{1,0:T(8,128)(2,1)S(1)}, bf16[256,1536]{1,0:T(8,128)(2,1)}, u32[]{:S(2)}, u32[]{:S(2)}) collective-permute-start(bf16[256,1536]{1,0:T(8,128)(2,1)S(1)} %copy-done.4), channel_id=1, source_target_pairs={{0,1},{1,0},{2,3},{3,2},{4,5},{5,4},{6,7},{7,6},{8,9},{9,8},{10,11... | collective-permute-start | bytes 2359304 | tf_op jit(solution)/shard_map/ppermute | solution.py:1090
  59.8 5.3 %collective-permute-start.8 = (bf16[512,128]{1,0:T(8,128)(2,1)S(1)}, bf16[512,128]{1,0:T(8,128)(2,1)S(1)}, u32[]{:S(2)}, u32[]{:S(2)}) collective-permute-start(bf16[512,128]{1,0:T(8,128)(2,1)S(1)} %pad_maximum_fusion.8), channel_id=1, source_target_pairs={{0,4},{2,6},{4,0},{6,2},{8,12},{10,14},{12,8},{14,10},{16,20},{18,... | collective-permute-start | bytes 393224 | tf_op jit(solution)/shard_map/ppermute | solution.py:1100
  63.9 7.3 %collective-permute-start.6 = (bf16[1024,128]{1,0:T(8,128)(2,1)}, bf16[1024,128]{1,0:T(8,128)(2,1)}, u32[]{:S(2)}, u32[]{:S(2)}) collective-permute-start(bf16[1024,128]{1,0:T(8,128)(2,1)} %pad_maximum_fusion.5), channel_id=1, source_target_pairs={{0,4},{2,6},{4,0},{6,2},{8,12},{10,14},{12,8},{14,10},{16,20},{18,... | collective-permute-start | bytes 786440 | tf_op jit(solution)/shard_map/ppermute | solution.py:1100
  65.1 8.8 %collective-permute-start.9 = (bf16[1024,128]{1,0:T(8,128)(2,1)S(1)}, bf16[1024,128]{1,0:T(8,128)(2,1)}, u32[]{:S(2)}, u32[]{:S(2)}) collective-permute-start(bf16[1024,128]{1,0:T(8,128)(2,1)S(1)} %pad_maximum_fusion.6), channel_id=1, source_target_pairs={{0,8},{2,10},{4,12},{6,14},{8,0},{10,2},{12,4},{14,6},{16,24},{18,... | collective-permute-start | bytes 786440 | tf_op jit(solution)/shard_map/ppermute | solution.py:1100
  69.1 20.4 %collective-permute-start.11 = (bf16[512,128]{1,0:T(8,128)(2,1)}, bf16[512,128]{1,0:T(8,128)(2,1)}, u32[]{:S(2)}, u32[]{:S(2)}) collective-permute-start(bf16[512,128]{1,0:T(8,128)(2,1)} %get-tuple-element.146.refs_4_), channel_id=1, source_target_pairs={{0,16},{2,18},{4,20},{6,22},{8,24},{10,26},{12,28},{14,30},{16,0},... | collective-permute-start | bytes 393224 | tf_op jit(solution)/shard_map/ppermute | solution.py:1100
  72.1 17.4 %copy-start.8 = (bf16[2048,128]{1,0:T(8,128)(2,1)}, bf16[2048,128]{1,0:T(8,128)(2,1)S(1)}, u32[]{:S(2)}) copy-start(bf16[2048,128]{1,0:T(8,128)(2,1)S(1)} %pad_maximum_fusion.2.refs_0_) | copy-start | bytes 1572868
  72.1 17.4 %collective-permute-start.7 = (bf16[2048,128]{1,0:T(8,128)(2,1)S(1)}, bf16[2048,128]{1,0:T(8,128)(2,1)}, u32[]{:S(2)}, u32[]{:S(2)}) collective-permute-start(bf16[2048,128]{1,0:T(8,128)(2,1)S(1)} %pad_maximum_fusion.2.refs_0_), channel_id=1, source_target_pairs={{0,2},{2,0},{4,6},{6,4},{8,10},{10,8},{12,14},{14,12},{16,18},{18,... | collective-permute-start | bytes 1572872 | tf_op jit(solution)/shard_map/ppermute | solution.py:1100
  74.9 14.6 %copy-start.9 = (bf16[2048,128]{1,0:T(8,128)(2,1)}, bf16[2048,128]{1,0:T(8,128)(2,1)S(1)}, u32[]{:S(2)}) copy-start(bf16[2048,128]{1,0:T(8,128)(2,1)S(1)} %pad_maximum_fusion.3.refs_2_) | copy-start | bytes 1572868
  74.9 14.7 %collective-permute-start.10 = (bf16[2048,128]{1,0:T(8,128)(2,1)S(1)}, bf16[2048,128]{1,0:T(8,128)(2,1)}, u32[]{:S(2)}, u32[]{:S(2)}) collective-permute-start(bf16[2048,128]{1,0:T(8,128)(2,1)S(1)} %pad_maximum_fusion.3.refs_2_), channel_id=1, source_target_pairs={{0,2},{2,0},{4,6},{6,4},{8,10},{10,8},{12,14},{14,12},{16,18},{18,... | collective-permute-start | bytes 1572872 | tf_op jit(solution)/shard_map/ppermute | solution.py:1100
  77.1 85.0 %collective-permute-start.16 = (bf16[1792,512]{1,0:T(8,128)(2,1)S(1)}, bf16[1792,512]{1,0:T(8,128)(2,1)}, u32[]{:S(2)}, u32[]{:S(2)}) collective-permute-start(bf16[1792,512]{1,0:T(8,128)(2,1)S(1)} %pad_maximum_fusion), channel_id=1, source_target_pairs={{0,1},{1,0},{2,3},{3,2},{4,5},{5,4},{6,7},{7,6},{8,9},{9,8},{10,11... | collective-permute-start | bytes 5505032 | tf_op jit(solution)/shard_map/ppermute | solution.py:1090
  78.6 83.5 %collective-permute-start.17 = (bf16[256,2048]{1,0:T(8,128)(2,1)}, bf16[256,2048]{1,0:T(8,128)(2,1)S(1)}, u32[]{:S(2)}, u32[]{:S(2)}) collective-permute-start(bf16[256,2048]{1,0:T(8,128)(2,1)} %refs_13_.1), channel_id=1, source_target_pairs={{0,1},{1,0},{2,3},{3,2},{4,5},{5,4},{6,7},{7,6},{8,9},{9,8},{10,11... | collective-permute-start | bytes 3145736 | tf_op jit(solution)/shard_map/ppermute | solution.py:1090
  89.5 72.5 %collective-permute-start.13 = (bf16[256,512]{1,0:T(8,128)(2,1)}, bf16[256,512]{1,0:T(8,128)(2,1)S(1)}, u32[]{:S(2)}, u32[]{:S(2)}) collective-permute-start(bf16[256,512]{1,0:T(8,128)(2,1)} %get-tuple-element.155.refs_1_), channel_id=1, source_target_pairs={{0,14},{14,0},{2,12},{12,2},{4,10},{10,4},{6,8},{8,6},{1,15},{15,1... | collective-permute-start | bytes 786440 | tf_op jit(solution)/shard_map/ppermute | solution.py:1186
  92.0 70.0 %collective-permute-start.14 = (bf16[256,512]{1,0:T(8,128)(2,1)}, bf16[256,512]{1,0:T(8,128)(2,1)S(1)}, u32[]{:S(2)}, u32[]{:S(2)}) collective-permute-start(bf16[256,512]{1,0:T(8,128)(2,1)} %get-tuple-element.156), channel_id=1, source_target_pairs={{0,16},{16,0},{14,30},{30,14},{2,18},{18,2},{12,28},{28,12},{4,20}... | collective-permute-start | bytes 786440 | tf_op jit(solution)/shard_map/ppermute | solution.py:1186
  92.0 70.0 %collective-permute-start.15 = (bf16[256,512]{1,0:T(8,128)(2,1)}, bf16[256,512]{1,0:T(8,128)(2,1)S(1)}, u32[]{:S(2)}, u32[]{:S(2)}) collective-permute-start(bf16[256,512]{1,0:T(8,128)(2,1)} %get-tuple-element.157), channel_id=1, source_target_pairs={{0,30},{14,16},{16,0},{30,14},{2,28},{12,18},{18,2},{28,12},{4,26}... | collective-permute-start | bytes 786440 | tf_op jit(solution)/shard_map/ppermute | solution.py:1186
  212.2 136.4 %collective-permute-start.18 = (bf16[256,512]{1,0:T(8,128)(2,1)}, bf16[256,512]{1,0:T(8,128)(2,1)}, u32[]{:S(2)}, u32[]{:S(2)}) collective-permute-start(bf16[256,512]{1,0:T(8,128)(2,1)} %get-tuple-element.205.own_ref), channel_id=1, source_target_pairs={{14,0},{0,14},{12,2},{2,12},{10,4},{4,10},{8,6},{6,8},{15,1},{1,15... | collective-permute-start | bytes 786440 | tf_op jit(solution)/shard_map/ppermute | solution.py:1192
  214.1 134.5 %collective-permute-start.19 = (bf16[256,512]{1,0:T(8,128)(2,1)}, bf16[256,512]{1,0:T(8,128)(2,1)}, u32[]{:S(2)}, u32[]{:S(2)}) collective-permute-start(bf16[256,512]{1,0:T(8,128)(2,1)} %get-tuple-element.183), channel_id=1, source_target_pairs={{16,0},{0,16},{30,14},{14,30},{18,2},{2,18},{28,12},{12,28},{20,4}... | collective-permute-start | bytes 786440 | tf_op jit(solution)/shard_map/ppermute | solution.py:1192
  214.2 134.4 %collective-permute-start.20 = (bf16[256,512]{1,0:T(8,128)(2,1)}, bf16[256,512]{1,0:T(8,128)(2,1)}, u32[]{:S(2)}, u32[]{:S(2)}) collective-permute-start(bf16[256,512]{1,0:T(8,128)(2,1)} %get-tuple-element.184), channel_id=1, source_target_pairs={{30,0},{16,14},{0,16},{14,30},{28,2},{18,12},{2,18},{12,28},{26,4}... | collective-permute-start | bytes 786440 | tf_op jit(solution)/shard_map/ppermute | solution.py:1192
  348.6 18.0 %collective-permute-start.22 = (bf16[2048,128]{1,0:T(8,128)(2,1)}, bf16[2048,128]{1,0:T(8,128)(2,1)S(1)}, u32[]{:S(2)}, u32[]{:S(2)}) collective-permute-start(bf16[2048,128]{1,0:T(8,128)(2,1)} %get-tuple-element.216), channel_id=1, source_target_pairs={{0,2},{2,0},{4,6},{6,4},{8,10},{10,8},{12,14},{14,12},{16,18},{18,... | collective-permute-start | bytes 1572872 | tf_op jit(solution)/shard_map/ppermute | solution.py:1100
  348.8 11.1 %copy-start.16 = (f32[512,128]{1,0:T(8,128)S(1)}, f32[512,128]{1,0:T(8,128)}, u32[]{:S(2)}) copy-start(f32[512,128]{1,0:T(8,128)} %get-tuple-element.199) | copy-start | bytes 786436
  348.8 11.4 %copy-start.15 = (f32[512,128]{1,0:T(8,128)S(1)}, f32[512,128]{1,0:T(8,128)}, u32[]{:S(2)}) copy-start(f32[512,128]{1,0:T(8,128)} %get-tuple-element.200) | copy-start | bytes 786436
  348.8 11.7 %copy-start.21 = (f32[1,512]{1,0:T(1,128)S(1)}, f32[1,512]{1,0:T(1,128)}, u32[]{:S(2)}) copy-start(f32[1,512]{1,0:T(1,128)} %get-tuple-element.201) | copy-start | bytes 6148
  348.8 11.9 %copy-start.1 = (f32[2048,128]{1,0:T(8,128)S(1)}, f32[2048,128]{1,0:T(8,128)}, u32[]{:S(2)}) copy-start(f32[2048,128]{1,0:T(8,128)} %get-tuple-element.202) | copy-start | bytes 3145732
  359.4 15.5 %collective-permute-start.21 = (bf16[2,2,64,1536]{3,2,1,0:T(8,128)(2,1)}, bf16[2,2,64,1536]{3,2,1,0:T(8,128)(2,1)}, u32[]{:S(2)}, u32[]{:S(2)}) collective-permute-start(bf16[2,2,64,1536]{3,2,1,0:T(8,128)(2,1)} %get-tuple-element.188), channel_id=1, source_target_pairs={{0,2},{2,0},{4,6},{6,4},{8,10},{10,8},{12,14},{14,12},{16,18},{18,... | collective-permute-start | bytes 2359304 | tf_op jit(solution)/shard_map/ppermute | solution.py:1100
  361.3 6.2 %collective-permute-start.24 = (bf16[2048,128]{1,0:T(8,128)(2,1)}, bf16[2048,128]{1,0:T(8,128)(2,1)}, u32[]{:S(2)}, u32[]{:S(2)}) collective-permute-start(bf16[2048,128]{1,0:T(8,128)(2,1)} %get-tuple-element.218), channel_id=1, source_target_pairs={{0,2},{2,0},{4,6},{6,4},{8,10},{10,8},{12,14},{14,12},{16,18},{18,... | collective-permute-start | bytes 1572872 | tf_op jit(solution)/shard_map/ppermute | solution.py:1100
  367.5 21.1 %collective-permute-start.23 = (bf16[1024,128]{1,0:T(8,128)(2,1)}, bf16[1024,128]{1,0:T(8,128)(2,1)S(1)}, u32[]{:S(2)}, u32[]{:S(2)}) collective-permute-start(bf16[1024,128]{1,0:T(8,128)(2,1)} %slice.304), channel_id=1, source_target_pairs={{0,4},{2,6},{4,0},{6,2},{8,12},{10,14},{12,8},{14,10},{16,20},{18,... | collective-permute-start | bytes 786440 | tf_op jit(solution)/shard_map/ppermute | solution.py:1100
  369.8 18.8 %collective-permute-start.25 = (bf16[1024,128]{1,0:T(8,128)(2,1)}, bf16[1024,128]{1,0:T(8,128)(2,1)S(1)}, u32[]{:S(2)}, u32[]{:S(2)}) collective-permute-start(bf16[1024,128]{1,0:T(8,128)(2,1)} %slice.303), channel_id=1, source_target_pairs={{0,8},{2,10},{4,12},{6,14},{8,0},{10,2},{12,4},{14,6},{16,24},{18,... | collective-permute-start | bytes 786440 | tf_op jit(solution)/shard_map/ppermute | solution.py:1100
  376.2 16.1 %copy-start.32 = (bf16[512,128]{1,0:T(8,128)(2,1)S(1)}, bf16[512,128]{1,0:T(8,128)(2,1)}, u32[]{:S(2)}) copy-start(bf16[512,128]{1,0:T(8,128)(2,1)} %get-tuple-element.228) | copy-start | bytes 393220
  388.7 15.4 %copy-start.14 = (f32[512,128]{1,0:T(8,128)S(1)}, f32[512,128]{1,0:T(8,128)}, u32[]{:S(2)}) copy-start(f32[512,128]{1,0:T(8,128)} %get-tuple-element.227) | copy-start | bytes 786436
  388.8 6.1 %collective-permute-start.26 = (bf16[512,128]{1,0:T(8,128)(2,1)S(1)}, bf16[512,128]{1,0:T(8,128)(2,1)S(1)}, u32[]{:S(2)}, u32[]{:S(2)}) collective-permute-start(bf16[512,128]{1,0:T(8,128)(2,1)S(1)} %slice.306), channel_id=1, source_target_pairs={{0,8},{2,10},{4,12},{6,14},{8,0},{10,2},{12,4},{14,6},{16,24},{18,... | collective-permute-start | bytes 393224 | tf_op jit(solution)/shard_map/ppermute | solution.py:1100
  389.4 5.4 %collective-permute-start.27 = (bf16[512,128]{1,0:T(8,128)(2,1)S(1)}, bf16[512,128]{1,0:T(8,128)(2,1)S(1)}, u32[]{:S(2)}, u32[]{:S(2)}) collective-permute-start(bf16[512,128]{1,0:T(8,128)(2,1)S(1)} %slice.305), channel_id=1, source_target_pairs={{0,4},{2,6},{4,0},{6,2},{8,12},{10,14},{12,8},{14,10},{16,20},{18,... | collective-permute-start | bytes 393224 | tf_op jit(solution)/shard_map/ppermute | solution.py:1100
  391.1 13.7 %collective-permute-start.29 = (bf16[2,64,1536]{2,1,0:T(8,128)(2,1)S(1)}, bf16[2,64,1536]{2,1,0:T(8,128)(2,1)S(1)}, u32[]{:S(2)}, u32[]{:S(2)}) collective-permute-start(bf16[2,64,1536]{2,1,0:T(8,128)(2,1)S(1)} %slice_bitcast_fusion), channel_id=1, source_target_pairs={{0,1},{1,0},{2,3},{3,2},{4,5},{5,4},{6,7},{7,6},{8,9},{9,8},{10,11... | collective-permute-start | bytes 1179656 | tf_op jit(solution)/shard_map/ppermute | solution.py:1090
  392.4 11.7 %collective-permute-start.30 = (bf16[512,128]{1,0:T(8,128)(2,1)S(1)}, bf16[512,128]{1,0:T(8,128)(2,1)S(1)}, u32[]{:S(2)}, u32[]{:S(2)}) collective-permute-start(bf16[512,128]{1,0:T(8,128)(2,1)S(1)} %copy-done.32), channel_id=1, source_target_pairs={{0,16},{2,18},{4,20},{6,22},{8,24},{10,26},{12,28},{14,30},{16,0},... | collective-permute-start | bytes 393224 | tf_op jit(solution)/shard_map/ppermute | solution.py:1100
  395.0 11.1 %collective-permute-start.28 = (bf16[512,128]{1,0:T(8,128)(2,1)S(1)}, bf16[512,128]{1,0:T(8,128)(2,1)S(1)}, u32[]{:S(2)}, u32[]{:S(2)}) collective-permute-start(bf16[512,128]{1,0:T(8,128)(2,1)S(1)} %pad_maximum_fusion.9), channel_id=1, source_target_pairs={{0,16},{2,18},{4,20},{6,22},{8,24},{10,26},{12,28},{14,30},{16,0},... | collective-permute-start | bytes 393224 | tf_op jit(solution)/shard_map/ppermute | solution.py:1100
  406.7 14.6 %copy-start.7 = (bf16[512,2048]{1,0:T(8,128)(2,1)S(1)}, bf16[512,2048]{1,0:T(8,128)(2,1)}, u32[]{:S(2)}) copy-start(bf16[512,2048]{1,0:T(8,128)(2,1)} %get-tuple-element.243) | copy-start | bytes 6291460
  414.8 25.4 %collective-permute-start.31 = (bf16[256,512]{1,0:T(8,128)(2,1)}, bf16[256,512]{1,0:T(8,128)(2,1)S(1)}, u32[]{:S(2)}, u32[]{:S(2)}) collective-permute-start(bf16[256,512]{1,0:T(8,128)(2,1)} %get-tuple-element.231.own_ref), channel_id=1, source_target_pairs={{14,0},{0,14},{12,2},{2,12},{10,4},{4,10},{8,6},{6,8},{15,1},{1,15... | collective-permute-start | bytes 786440 | tf_op jit(solution)/shard_map/ppermute | solution.py:1192
  416.9 23.4 %collective-permute-start.32 = (bf16[256,512]{1,0:T(8,128)(2,1)}, bf16[256,512]{1,0:T(8,128)(2,1)S(1)}, u32[]{:S(2)}, u32[]{:S(2)}) collective-permute-start(bf16[256,512]{1,0:T(8,128)(2,1)} %get-tuple-element.232), channel_id=1, source_target_pairs={{16,0},{0,16},{30,14},{14,30},{18,2},{2,18},{28,12},{12,28},{20,4}... | collective-permute-start | bytes 786440 | tf_op jit(solution)/shard_map/ppermute | solution.py:1192
  417.0 23.3 %collective-permute-start.33 = (bf16[256,512]{1,0:T(8,128)(2,1)}, bf16[256,512]{1,0:T(8,128)(2,1)S(1)}, u32[]{:S(2)}, u32[]{:S(2)}) collective-permute-start(bf16[256,512]{1,0:T(8,128)(2,1)} %get-tuple-element.233), channel_id=1, source_target_pairs={{30,0},{16,14},{0,16},{14,30},{28,2},{18,12},{2,18},{12,28},{26,4}... | collective-permute-start | bytes 786440 | tf_op jit(solution)/shard_map/ppermute | solution.py:1192
  419.9 3.0 collective-permute-start.34
  419.9 18.2 %collective-permute-start.40 = (bf16[64,1536]{1,0:T(8,128)(2,1)S(1)}, bf16[64,1536]{1,0:T(8,128)(2,1)S(1)}, u32[]{:S(2)}, u32[]{:S(2)}) collective-permute-start(bf16[64,1536]{1,0:T(8,128)(2,1)S(1)} %slice_bitcast_fusion.1), channel_id=1, source_target_pairs={{0,4},{2,6},{4,0},{6,2},{8,12},{10,14},{12,8},{14,10},{16,20},{18,... | collective-permute-start | bytes 589832 | tf_op jit(solution)/shard_map/ppermute | solution.py:1100
  423.0 4.3 collective-permute-start.35
  427.3 10.7 %collective-permute-start.36 = (bf16[128,256]{1,0:T(8,128)(2,1)S(1)}, bf16[128,256]{1,0:T(8,128)(2,1)S(1)}, u32[]{:S(2)}, u32[]{:S(2)}) collective-permute-start(bf16[128,256]{1,0:T(8,128)(2,1)S(1)} %fusion.19), channel_id=1, source_target_pairs={{0,4},{2,6},{4,0},{6,2},{8,12},{10,14},{12,8},{14,10},{16,20},{18,... | collective-permute-start | bytes 196616 | tf_op jit(solution)/shard_map/ppermute | solution.py:1100
  438.1 6.1 %collective-permute-start.37 = (bf16[128,256]{1,0:T(8,128)(2,1)S(1)}, bf16[128,256]{1,0:T(8,128)(2,1)S(1)}, u32[]{:S(2)}, u32[]{:S(2)}) collective-permute-start(bf16[128,256]{1,0:T(8,128)(2,1)S(1)} %add_convert_fusion.7), channel_id=1, source_target_pairs={{0,8},{2,10},{4,12},{6,14},{8,0},{10,2},{12,4},{14,6},{16,24},{18,... | collective-permute-start | bytes 196616 | tf_op jit(solution)/shard_map/ppermute | solution.py:1100
  438.2 8.8 %collective-permute-start.41 = (bf16[64,1536]{1,0:T(8,128)(2,1)S(1)}, bf16[64,1536]{1,0:T(8,128)(2,1)S(1)}, u32[]{:S(2)}, u32[]{:S(2)}) collective-permute-start(bf16[64,1536]{1,0:T(8,128)(2,1)S(1)} %fusion.1), channel_id=1, source_target_pairs={{0,8},{2,10},{4,12},{6,14},{8,0},{10,2},{12,4},{14,6},{16,24},{18,... | collective-permute-start | bytes 589832 | tf_op jit(solution)/shard_map/ppermute | solution.py:1100
  444.2 5.4 %collective-permute-start.38 = (bf16[128,256]{1,0:T(8,128)(2,1)S(1)}, bf16[128,256]{1,0:T(8,128)(2,1)S(1)}, u32[]{:S(2)}, u32[]{:S(2)}) collective-permute-start(bf16[128,256]{1,0:T(8,128)(2,1)S(1)} %add_convert_fusion.6), channel_id=1, source_target_pairs={{0,16},{2,18},{4,20},{6,22},{8,24},{10,26},{12,28},{14,30},{16,0},... | collective-permute-start | bytes 196616 | tf_op jit(solution)/shard_map/ppermute | solution.py:1100
  447.1 12.8 %collective-permute-start.42 = (bf16[64,1536]{1,0:T(8,128)(2,1)S(1)}, bf16[64,1536]{1,0:T(8,128)(2,1)S(1)}, u32[]{:S(2)}, u32[]{:S(2)}) collective-permute-start(bf16[64,1536]{1,0:T(8,128)(2,1)S(1)} %add_convert_fusion.2), channel_id=1, source_target_pairs={{0,16},{2,18},{4,20},{6,22},{8,24},{10,26},{12,28},{14,30},{16,0},... | collective-permute-start | bytes 589832 | tf_op jit(solution)/shard_map/ppermute | solution.py:1100
  449.6 12.3 %collective-permute-start.39 = (bf16[128,256]{1,0:T(8,128)(2,1)S(1)}, bf16[128,256]{1,0:T(8,128)(2,1)S(1)}, u32[]{:S(2)}, u32[]{:S(2)}) collective-permute-start(bf16[128,256]{1,0:T(8,128)(2,1)S(1)} %add_convert_fusion.5), channel_id=1, source_target_pairs={{0,2},{2,0},{4,6},{6,4},{8,10},{10,8},{12,14},{14,12},{16,18},{18,... | collective-permute-start | bytes 196616 | tf_op jit(solution)/shard_map/ppermute | solution.py:1100
  459.9 6.8 %collective-permute-start.43 = (bf16[64,1536]{1,0:T(8,128)(2,1)S(1)}, bf16[64,1536]{1,0:T(8,128)(2,1)S(1)}, u32[]{:S(2)}, u32[]{:S(2)}) collective-permute-start(bf16[64,1536]{1,0:T(8,128)(2,1)S(1)} %add_convert_fusion.1), channel_id=1, source_target_pairs={{0,4},{2,6},{4,0},{6,2},{8,12},{10,14},{12,8},{14,10},{16,20},{18,... | collective-permute-start | bytes 589832 | tf_op jit(solution)/shard_map/ppermute | solution.py:1100
  466.8 4.2 collective-permute-start.44
  (15 other events, 63.9 us)
Sparse Core Ops, SparseCore 0:
  217.3 171.3 all-reduce.3
